TPU v7x, 128 devices: a whole 4x4x4 slice. The times are simulated.
128 devices in a mesh: seq: 16 (over z, x), head: 8 (over y, core).
Axes of the slice: x: 4, y: 4, z: 4, core: 2. Of those that a mesh axis runs over, the one named last changes fastest.
Arguments:
- hidden: bfloat16 [8192, 8192], P('seq', 'head'), may hold values from -6 to 6
- w_query: bfloat16 [8192, 4096], P(None, 'head'), may hold values from -0.0625 to 0.0625
- w_key: bfloat16 [8192, 1024], P(None, 'head'), may hold values from -0.0625 to 0.0625
- w_value: bfloat16 [8192, 1024], P(None, 'head'), may hold values from -0.0625 to 0.0625
- w_out: bfloat16 [4096, 8192], P('head'), may hold values from -0.125 to 0.125
- prefix_keys: bfloat16 [65536, 1024], P('seq', 'head'), may hold values from -300 to 300
- prefix_values: bfloat16 [65536, 1024], P('seq', 'head'), may hold values from -6 to 6
- seg_lengths: int32 [256], replicated, may hold values from 1 to 256, as said below
- ancestors: int32 [64, 4], replicated, may hold values from -1 to 255, as said below
Outputs:
- attn_out: bfloat16 [8192, 8192], P('seq', 'head')
Inputs may be any that keep to these rules, and one draw needn't show every extreme that they name: `seg_lengths`: entry 0 is 256. `ancestors`: entry l of a row is -1 or a segment whose index is l modulo 4; entry 0 is never -1; the non-negative entries come first, and each descends from the one before.
All inputs are finite; a program needn't handle non-finite values.
Results may differ from a plain program's by a relative error of at most 0.02.
Values may be sent and summed in bfloat16 or wider, within the bound.
No kernel may reach another device: no remote copies, remote signals or barrier semaphores. Data moves between devices by JAX's collectives and lax.ppermute only.
A program may use at most 192 MiB of HBM per device.

v0:
```python
import math

import jax
import jax.numpy as jnp
from jax import lax
from jax.sharding import PartitionSpec as P

QH = 32
KVH = 8
HD = 128
ROLL = 128
SEG_LEN = 256
DEPTH = 4


def absorb(carry_state, query_block, seg_keys, seg_values, live_slots, inv_root):
    row_max, row_sum, weighted = carry_state
    scores = (
        jnp.einsum("rkgd,nkd->kgrn", query_block, seg_keys, preferred_element_type=jnp.float32)
        * inv_root
    )
    scores = jnp.where(live_slots[None, None, None, :], scores, -jnp.inf)
    new_max = jnp.maximum(row_max, jnp.max(scores, axis=-1))
    rescale = jnp.exp(row_max - new_max)
    numer = jnp.exp(scores - new_max[..., None])
    row_sum = row_sum * rescale + jnp.sum(numer, axis=-1)
    weighted = weighted * rescale[..., None] + jnp.einsum(
        "kgrn,nkd->kgrd", numer.astype(jnp.bfloat16), seg_values, preferred_element_type=jnp.float32
    )
    return (new_max, row_sum, weighted)


def per_device(
    hidden, w_query, w_key, w_value, w_out, prefix_keys, prefix_values, seg_lengths, ancestors
):
    per_group = QH // KVH
    inv_root = 1.0 / math.sqrt(HD)
    gathered = lax.all_gather(hidden, "head", axis=1, tiled=True)
    row_count = gathered.shape[0]
    queries = jnp.dot(gathered, w_query, preferred_element_type=jnp.float32).astype(jnp.bfloat16)
    leaf_keys = jnp.dot(gathered, w_key, preferred_element_type=jnp.float32).astype(jnp.bfloat16)
    leaf_values = jnp.dot(gathered, w_value, preferred_element_type=jnp.float32).astype(
        jnp.bfloat16
    )
    kv_local = leaf_keys.shape[1] // HD
    roll_count = row_count // ROLL
    my_index = lax.axis_index("seq")
    my_ancestors = lax.dynamic_slice_in_dim(ancestors, my_index * roll_count, roll_count, 0)
    query_rolls = queries.reshape(roll_count, ROLL, kv_local, per_group, HD)
    key_rolls = leaf_keys.reshape(roll_count, ROLL, kv_local, HD)
    value_rolls = leaf_values.reshape(roll_count, ROLL, kv_local, HD)
    slot_ids = jnp.arange(SEG_LEN, dtype=jnp.int32)
    causal = jnp.arange(ROLL)[:, None] >= jnp.arange(ROLL)[None, :]
    own_scores = (
        jnp.einsum("brkgd,bnkd->bkgrn", query_rolls, key_rolls, preferred_element_type=jnp.float32)
        * inv_root
    )
    own_scores = jnp.where(causal[None, None, None], own_scores, -jnp.inf)
    own_max = jnp.max(own_scores, axis=-1)
    own_numer = jnp.exp(own_scores - own_max[..., None])
    own_sum = jnp.sum(own_numer, axis=-1)
    own_weighted = jnp.einsum(
        "bkgrn,bnkd->bkgrd",
        own_numer.astype(jnp.bfloat16),
        value_rolls,
        preferred_element_type=jnp.float32,
    )
    piece_keys = lax.all_gather(prefix_keys, "seq", axis=0, tiled=True)
    piece_values = lax.all_gather(prefix_values, "seq", axis=0, tiled=True)
    seg_count = piece_keys.shape[0] // SEG_LEN
    piece_keys = piece_keys.reshape(seg_count, SEG_LEN, kv_local, HD)
    piece_values = piece_values.reshape(seg_count, SEG_LEN, kv_local, HD)

    def visit(roll_step, carry_in):
        query_block = lax.dynamic_index_in_dim(query_rolls, roll_step, 0, keepdims=False)
        for level in range(DEPTH):
            segment = my_ancestors[roll_step, level]
            present = (segment >= 0) & (segment >= 0) & (segment < seg_count)
            safe = jnp.clip(segment, 0, seg_count - 1)
            seg_keys = lax.dynamic_index_in_dim(piece_keys, safe, 0, keepdims=False)
            seg_values = lax.dynamic_index_in_dim(piece_values, safe, 0, keepdims=False)
            live_slots = slot_ids < seg_lengths[jnp.maximum(segment, 0)]

            def update(kept):
                single = jax.tree.map(
                    lambda whole: lax.dynamic_index_in_dim(whole, roll_step, 0, keepdims=False),
                    kept,
                )
                single = absorb(single, query_block, seg_keys, seg_values, live_slots, inv_root)
                return jax.tree.map(
                    lambda whole, new: lax.dynamic_update_index_in_dim(whole, new, roll_step, 0),
                    kept,
                    single,
                )

            carry_in = lax.cond(present, update, lambda kept: kept, carry_in)
        return carry_in

    row_max, row_sum, weighted = lax.fori_loop(
        0, roll_count, visit, (own_max, own_sum, own_weighted)
    )
    attended = (weighted / row_sum[..., None]).astype(jnp.bfloat16)
    attended = jnp.transpose(attended, (0, 3, 1, 2, 4)).reshape(
        row_count, kv_local * per_group * HD
    )
    partial_out = jnp.dot(attended, w_out, preferred_element_type=jnp.float32)
    return lax.psum_scatter(
        partial_out.astype(jnp.bfloat16), "head", scatter_dimension=1, tiled=True
    )


def solution(mesh):
    in_specs = (
        P("seq", "head"),
        P(None, "head"),
        P(None, "head"),
        P(None, "head"),
        P("head", None),
        P("seq", "head"),
        P("seq", "head"),
        P(),
        P(),
    )
    out_specs = P("seq", "head")
    return jax.shard_map(
        per_device, mesh=mesh, in_specs=in_specs, out_specs=out_specs, check_vma=False
    )
```

profile of v0, /device:TPU:1, one launch (start us, length us, event | category | flops | bytes accessed | tf_op | source)
XLA Modules:
  0.0 424.4 jit_solution(15618082417429108992)
XLA Ops:
  6.5 0.7 all-gather.4.cloned.1.call-update
  7.3 0.7 all-gather.6.cloned.1.call-update
  8.1 0.7 all-gather.8.cloned.1.call-update
  8.8 0.8 constant_dynamic-slice_fusion.13
  9.7 52.7 %all-gather.4.cloned.1.call-done = bf16[512,8192]{1,0:T(8,128)(2,1)} async-done(((bf16[512,1024]{1,0:T(8,128)(2,1)}), bf16[512,8192]{1,0:T(8,128)(2,1)}) %all-gather.4.cloned.1.call-update) | async-done | bytes 8388624 | tf_op jit(solution)/shard_map/all_gather | solution.py:38
  62.4 10.2 %convolution_convert_fusion.1 = bf16[512,512]{1,0:T(8,128)(2,1)S(1)} fusion(bf16[512,8192]{1,0:T(8,128)(2,1)} %all-gather.4.cloned.1.call-done, bf16[8192,512]{1,0:T(8,128)(2,1)} %param.20), kind=kOutput, calls=%fused_computation.125 | convolution fusion | flops 4295229440 | bytes 17301504 | tf_op jit(solution)/shard_map/dot_general | solution.py:40
  72.7 0.8 copy-done.2
  73.6 1.2 reshape.411
  74.8 6.3 %convolution_convert_fusion.3 = bf16[512,128]{1,0:T(8,128)(2,1)S(1)} fusion(bf16[512,8192]{1,0:T(8,128)(2,1)} %all-gather.4.cloned.1.call-done, bf16[8192,128]{1,0:T(8,128)(2,1)S(1)} %copy-done), kind=kOutput, calls=%fused_computation.128 | convolution fusion | flops 1073807360 | bytes 10616832 | tf_op jit(solution)/shard_map/dot_general | solution.py:41
  81.7 5.9 %convolution_convert_fusion.2 = bf16[512,128]{1,0:T(8,128)(2,1)S(1)} fusion(bf16[512,8192]{1,0:T(8,128)(2,1)} %all-gather.4.cloned.1.call-done, bf16[8192,128]{1,0:T(8,128)(2,1)S(1)} %copy-done.4), kind=kOutput, calls=%fused_computation.127 | convolution fusion | flops 1073807360 | bytes 10616832 | tf_op jit(solution)/shard_map/dot_general | solution.py:42
  87.9 87.9 %all-gather.6.cloned.1.call-done = bf16[65536,128]{1,0:T(8,128)(2,1)} async-done(((bf16[4096,128]{1,0:T(8,128)(2,1)}), bf16[65536,128]{1,0:T(8,128)(2,1)}) %all-gather.6.cloned.1.call-update) | async-done | bytes 16777232 | tf_op jit(solution)/shard_map/all_gather | solution.py:68
  175.8 113.2 %all-gather.8.cloned.1.call-done = bf16[65536,128]{1,0:T(8,128)(2,1)} async-done(((bf16[4096,128]{1,0:T(8,128)(2,1)}), bf16[65536,128]{1,0:T(8,128)(2,1)}) %all-gather.8.cloned.1.call-update) | async-done | bytes 16777232 | tf_op jit(solution)/shard_map/all_gather | solution.py:69
  289.0 58.1 %while.19 = (s32[]{:T(128)}, f32[4,1,4,128]{3,2,1,0:T(4,128)S(1)}, f32[4,1,4,128]{3,2,1,0:T(4,128)S(1)}, f32[4,1,4,128,128]{4,3,2,1,0:T(8,128)S(1)}, s32[4,4]{1,...) while((s32[]{:T(128)}, f32[4,1,4,128]{3,2,1,0:T(4,128)S(1)}, ...), condition=%wide.region_19.20_spmd.clone.clone, body=%wide.region_2.19_spmd.clone.clone.sunk | while | flops 272639008 | bytes 12973141 | solution.py:99
  289.0 0.7 constant_dynamic-slice_fusion.16
  297.0 0.7 fusion.96
  298.3 1.0 dynamic-slice_bitcast_fusion.7
  299.4 0.7 conditional.16
  300.2 0.6 iota_compare_fusion.8
  300.8 0.7 conditional.17
  301.6 0.6 iota_compare_fusion.9
  302.3 0.7 constant_dynamic-slice_fusion.16
  310.3 0.7 fusion.96
  311.6 1.0 dynamic-slice_bitcast_fusion.7
  312.7 0.7 conditional.16
  313.4 0.6 iota_compare_fusion.8
  314.1 0.6 iota_compare_fusion.9
  314.8 0.7 constant_dynamic-slice_fusion.16
  322.8 0.7 fusion.96
  324.1 1.0 dynamic-slice_bitcast_fusion.7
  325.2 0.7 conditional.16
  326.0 0.6 iota_compare_fusion.8
  326.6 0.7 conditional.17
  327.4 0.6 iota_compare_fusion.9
  328.0 0.7 conditional.18
  328.8 4.3 %conditional.19 = ((f32[4,1,4,128]{3,2,1,0:T(4,128)S(1)}, f32[4,1,4,128]{3,2,1,0:T(4,128)S(1)}, f32[4,1,4,128,128]{4,3,2,1,0:T(8,128)S(1)})) conditional(s32[]{:T(128)} %convert_element_type.121, (f32[4,1,4,128]{3,2,1,0:T(4,128)S(1)}, f32[4,1,4,128]{3,2,1,0:T(4,128)S(1)}, f32[4,1,4,128,128]{4,3,2,1,0:T(8,128)S(1)}) %get-tuple-element.741, ...), branch_computations={%region_15.15_spmd, %region_16.18_spmd} | conditional | flops 68159744 | bytes 2915970 | solution.py:96
  330.1 0.6 broadcast_compare_fusion
  330.7 1.1 fusion.83
  332.0 1.1 fusion.54
  333.1 0.7 constant_dynamic-slice_fusion.16
  341.2 0.7 fusion.96
  342.4 1.0 dynamic-slice_bitcast_fusion.7
  343.5 0.7 conditional.16
  344.3 0.6 iota_compare_fusion.8
  344.9 0.7 conditional.17
  345.7 0.6 iota_compare_fusion.9
  346.3 0.7 conditional.18
  347.9 10.3 %convolution_convert_fusion = bf16[512,8192]{1,0:T(8,128)(2,1)} fusion(bf16[512,8192]{1,0:T(8,128)(2,1)} %param.23, bf16[64,8,4,128]{3,2,1,0:T(4,128)(2,1)S(1)} %bitcast.302), kind=kOutput, calls=%fused_computation.121 | convolution fusion | flops 4299161600 | bytes 17301504 | tf_op jit(solution)/shard_map/dot_general | solution.py:106
  358.2 59.7 %reduce-scatter.2.cloned.1.call-done = bf16[512,1024]{1,0:T(8,128)(2,1)} async-done(((bf16[512,8192]{1,0:T(8,128)(2,1)}), bf16[512,1024]{1,0:T(8,128)(2,1)}) %reduce-scatter.2.cloned.1.call-update) | async-done | bytes 1048592 | tf_op jit(solution)/shard_map/reduce_scatter | solution.py:107
  (103 shorter events, 11.7 us)
Async XLA Ops:
  6.5 68.3 %copy-start = (bf16[8192,128]{1,0:T(8,128)(2,1)S(1)}, bf16[8192,128]{1,0:T(8,128)(2,1)}, u32[]{:S(2)}) copy-start(bf16[8192,128]{1,0:T(8,128)(2,1)} %param.21) | copy-start | bytes 6291460
  6.5 55.9 %all-gather.4.cloned.1.call-start = ((), (), s32[]{:S(2)}) async-start(), calls=%async_computation.1 | async-start | bytes 9437184 | tf_op jit(solution)/shard_map/all_gather | solution.py:38
  7.3 168.5 %all-gather.6.cloned.1.call-start = ((), (), s32[]{:S(2)}) async-start(), calls=%async_computation.2 | async-start | bytes 17825792 | tf_op jit(solution)/shard_map/all_gather | solution.py:68
  8.0 281.0 %all-gather.8.cloned.1.call-start = ((), (), s32[]{:S(2)}) async-start(), calls=%async_computation.3 | async-start | bytes 17825792 | tf_op jit(solution)/shard_map/all_gather | solution.py:69
  8.7 409.2 %reduce-scatter.2.cloned.1.call-start = ((), (), s32[]{:S(2)}) async-start(), calls=%async_computation.4 | async-start | bytes 9437184 | tf_op jit(solution)/shard_map/reduce_scatter | solution.py:107
  72.7 0.8 copy-start.2
  74.8 6.8 %copy-start.4 = (bf16[8192,128]{1,0:T(8,128)(2,1)S(1)}, bf16[8192,128]{1,0:T(8,128)(2,1)}, u32[]{:S(2)}) copy-start(bf16[8192,128]{1,0:T(8,128)(2,1)} %param.22) | copy-start | bytes 6291460
  81.1 207.9 %copy-start.3 = (s32[256]{0:T(256)S(1)}, s32[256]{0:T(256)}, u32[]{:S(2)}) copy-start(s32[256]{0:T(256)} %param.26) | copy-start | bytes 3076
  347.9 70.0 %copy-start.1 = (bf16[8192,128]{1,0:T(8,128)(2,1)S(1)}, bf16[8192,128]{1,0:T(8,128)(2,1)}, u32[]{:S(2)}) copy-start(bf16[8192,128]{1,0:T(8,128)(2,1)} %param.21) | copy-start | bytes 6291460
Sparse Core Ops, SparseCore 0:
  9.1 53.3 all-gather.3
  64.6 111.1 all-gather.5
  177.9 111.0 all-gather.7
  358.3 59.5 reduce-scatter.1
where the time goes:
time: 424 us
  waiting for transfers between devices  316 us (75%)
  matrix products  40.4 us (10%)
  loops' own time  31 us (7%)
  local copies, waits for them, and re-layouts  14.1 us (3%)
  between operations  13.2 us (3%)
  other arithmetic  9.93 us (2%)
    all_gather x1, waiting for transfers between devices, per_device(): piece_values = lax.all_gather(prefix_values, 'seq', axis=0, tiled=True)  113 us
    all_gather x1, waiting for transfers between devices, per_device(): piece_keys = lax.all_gather(prefix_keys, 'seq', axis=0, tiled=True)  87.9 us
    reduce_scatter x1, waiting for transfers between devices, per_device(): lax.psum_scatter(partial_out.astype(jnp.bfloat16), 'head', scatter_dimens...  59.7 us
    all_gather x1, waiting for transfers between devices, per_device(): gathered = lax.all_gather(hidden, 'head', axis=1, tiled=True)  52.7 us
    another operation x1, loops' own time, per_device(): lax.fori_loop(0, roll_count, visit, (own_max, own_sum, own_weighted))  29.8 us
    dot_general x1, matrix products, per_device(): partial_out = jnp.dot(attended, w_out, preferred_element_type=jnp.float32)  10.3 us
    dot_general x1, matrix products, per_device(): jnp.dot(gathered, w_query, preferred_element_type=jnp.float32)  10.2 us
  transfers between devices with their start and end apart: 4, of which 4 were waited for; matrix products, arithmetic and copies ran while one was open for 6% of the time, Pallas kernels for 0%

commit v1 on v0

v1 whole, which is shorter than its diff:
```python
import math

import jax
import jax.numpy as jnp
import numpy as np
from jax import lax
from jax.experimental import pallas as pl
from jax.experimental.pallas import tpu as pltpu
from jax.sharding import PartitionSpec as P

QH = 32
KVH = 8
HD = 128
ROLL = 128
SEG_LEN = 256
DEPTH = 4
GROUP = QH // KVH
GRAN = 16

RING = 4


def y_shift(step):
    return [(y * 2 + c, ((y + step) % RING) * 2 + c) for y in range(RING) for c in range(2)]


SIBLING = [(h, h ^ 1) for h in range(2 * RING)]
UP = y_shift(1)
DOWN = y_shift(-1)


def send(x, pairs):
    return lax.ppermute(x, "head", pairs)


def params(mib):
    return pltpu.CompilerParams(vmem_limit_bytes=mib * 1024 * 1024)


def cost(flops, nbytes):
    return pl.CostEstimate(flops=int(flops), bytes_accessed=int(nbytes), transcendentals=0)


def index_table():
    rows = []
    for h in range(2 * RING):
        y, c = divmod(h, 2)
        row = []
        for other in (y, (y - 1) % RING, (y + 1) % RING, (y + 2) % RING):
            row += [2 * other + c, 2 * other + 1 - c]
        order = [(y + 2) % RING, (y + 1) % RING, (y - 1) % RING, y]
        row += [2 * t + c for t in order] + order
        row += [2 * t + 1 - c for t in range(RING)]
        rows.append(row)
    return np.asarray(rows, np.int32)


def spread_kernel(k_ref, v_ref, out_ref):
    out_ref[:, :, :GRAN, :] = pltpu.einshape("abcd->bacd", k_ref[...])
    out_ref[:, :, GRAN:, :] = pltpu.einshape("abcd->bacd", v_ref[...])


def spread(keys, values):
    segs = keys.shape[0] // SEG_LEN
    parts = SEG_LEN // GRAN
    step = 4
    view = (segs, parts, GRAN, HD)
    block = pl.BlockSpec((segs, step, GRAN, HD), lambda i: (0, i, 0, 0))
    return pl.pallas_call(
        spread_kernel,
        grid=(parts // step,),
        in_specs=[block, block],
        out_specs=pl.BlockSpec((step, segs, 2 * GRAN, HD), lambda i: (i, 0, 0, 0)),
        out_shape=jax.ShapeDtypeStruct((parts, segs, 2 * GRAN, HD), jnp.bfloat16),
        compiler_params=params(32),
        cost_estimate=cost(0, 4 * keys.size * 2),
    )(keys.reshape(view), values.reshape(view))


def pick_kernel(chain_ref, table_ref, out_ref):
    def body(n, carry):
        out_ref[n] = table_ref[jnp.maximum(chain_ref[n], 0)]
        return carry

    lax.fori_loop(0, out_ref.shape[0], body, 0, unroll=8)


def pick(chain, table):
    count = chain.shape[0]
    return pl.pallas_call(
        pick_kernel,
        grid_spec=pltpu.PrefetchScalarGridSpec(
            num_scalar_prefetch=1,
            grid=(1,),
            in_specs=[pl.BlockSpec(table.shape, lambda i, s: (0, 0, 0))],
            out_specs=pl.BlockSpec((count,) + table.shape[1:], lambda i, s: (0, 0, 0)),
        ),
        out_shape=jax.ShapeDtypeStruct((count,) + table.shape[1:], jnp.bfloat16),
        compiler_params=params(32),
        cost_estimate=cost(0, 2 * table.size * 2),
    )(chain, table)


def exchange(x):
    return lax.all_to_all(x, "seq", 0, 0, tiled=True)


def project_kernel(idx_ref, *refs):
    own, sib, *halves, wq, wk, wv, q_out, k_out, v_out, acc = refs
    step = pl.program_id(0)
    half = own.shape[0] // 2
    nq = wq.shape[1]
    nk = wk.shape[1]

    def add(rows, x, first):
        for w, lo, n in ((wq, 0, nq), (wk, nq, nk), (wv, nq + nk, nk)):
            d = jnp.dot(x, w[...], preferred_element_type=jnp.float32)
            if first:
                acc[rows, lo : lo + n] = d
            else:
                acc[rows, lo : lo + n] += d

    for s in range(8):

        @pl.when(step == s)
        def _():
            if s < 2:
                add(slice(None), (own, sib)[s][...], s == 0)
            else:
                top, bottom = halves[2 * (s - 2)], halves[2 * (s - 2) + 1]
                add(slice(0, half), top[...], False)
                add(slice(half, None), bottom[...], False)
            if s == 7:
                q_out[...] = acc[:, :nq].astype(jnp.bfloat16)
                k_out[...] = acc[:, nq : nq + nk].astype(jnp.bfloat16)
                v_out[...] = acc[:, nq + nk :].astype(jnp.bfloat16)


def project(idx, own, sib, halves, w_query, w_key, w_value):
    rows, depth = own.shape
    nq, nk = w_query.shape[1], w_key.shape[1]
    whole = lambda a: pl.BlockSpec(a.shape, lambda i, s: (0, 0))
    weight = lambda n: pl.BlockSpec((depth, n), lambda i, s: (s[i], 0))
    result = lambda n: pl.BlockSpec((rows, n), lambda i, s: (0, 0))
    return pl.pallas_call(
        project_kernel,
        grid_spec=pltpu.PrefetchScalarGridSpec(
            num_scalar_prefetch=1,
            grid=(8,),
            in_specs=[whole(a) for a in (own, sib, *halves)] + [weight(nq), weight(nk), weight(nk)],
            out_specs=[result(nq), result(nk), result(nk)],
            scratch_shapes=[pltpu.VMEM((rows, nq + 2 * nk), jnp.float32)],
        ),
        out_shape=[jax.ShapeDtypeStruct((rows, n), jnp.bfloat16) for n in (nq, nk, nk)],
        compiler_params=params(48),
        cost_estimate=cost(16 * rows * depth * (nq + 2 * nk), 16 * depth * (nq + 2 * nk + rows)),
    )(idx, own, sib, *halves, w_query, w_key, w_value)


def attend_kernel(chain_ref, len_ref, q_ref, k_ref, v_ref, far_ref, out_ref):
    base = (lax.axis_index("seq") * pl.num_programs(0) + pl.program_id(0)) * DEPTH
    inv_root = 1.0 / math.sqrt(HD)
    slot = lax.broadcasted_iota(jnp.int32, (1, SEG_LEN), 1)
    lives = []
    keys = []
    values = []
    for level in range(DEPTH):
        seg = chain_ref[base + level]
        live = jnp.where(seg >= 0, len_ref[jnp.maximum(seg, 0)], 0)
        lives.append(slot < live)
        keys.append(far_ref[:, level, :GRAN, :].reshape(SEG_LEN, HD))
        values.append(far_ref[:, level, GRAN:, :].reshape(SEG_LEN, HD))
    live = jnp.concatenate(lives, axis=1)
    keys = jnp.concatenate(keys, axis=0)
    values = jnp.concatenate(values, axis=0)
    own_keys = k_ref[...]
    own_values = v_ref[...]
    causal = lax.broadcasted_iota(jnp.int32, (ROLL, ROLL), 0) >= lax.broadcasted_iota(
        jnp.int32, (ROLL, ROLL), 1
    )
    nt = (((1,), (1,)), ((), ()))
    for g in range(GROUP):
        q = q_ref[:, g * HD : (g + 1) * HD]
        far = lax.dot_general(q, keys, nt, preferred_element_type=jnp.float32) * inv_root
        own = lax.dot_general(q, own_keys, nt, preferred_element_type=jnp.float32) * inv_root
        far = jnp.where(live, far, -jnp.inf)
        own = jnp.where(causal, own, -jnp.inf)
        m = jnp.maximum(
            jnp.max(far, axis=1, keepdims=True), jnp.max(own, axis=1, keepdims=True)
        )
        far = jnp.exp(far - m)
        own = jnp.exp(own - m)
        total = jnp.sum(far, axis=1, keepdims=True) + jnp.sum(own, axis=1, keepdims=True)
        mix = jnp.dot(far.astype(jnp.bfloat16), values, preferred_element_type=jnp.float32)
        mix += jnp.dot(own.astype(jnp.bfloat16), own_values, preferred_element_type=jnp.float32)
        out_ref[:, g * HD : (g + 1) * HD] = (mix / total).astype(jnp.bfloat16)


def attend(chain, lengths, q, k, v, far):
    rolls = q.shape[0] // ROLL
    row = lambda n: pl.BlockSpec((ROLL, n), lambda i, a, b: (i, 0))
    far_block = (far.shape[0], DEPTH, 2 * GRAN, HD)
    return pl.pallas_call(
        attend_kernel,
        grid_spec=pltpu.PrefetchScalarGridSpec(
            num_scalar_prefetch=2,
            grid=(rolls,),
            in_specs=[
                row(GROUP * HD),
                row(HD),
                row(HD),
                pl.BlockSpec(far_block, lambda i, a, b: (0, i, 0, 0)),
            ],
            out_specs=row(GROUP * HD),
        ),
        out_shape=jax.ShapeDtypeStruct(q.shape, jnp.bfloat16),
        compiler_params=params(48),
        cost_estimate=cost(4 * q.size * (DEPTH * SEG_LEN + ROLL), 2 * (2 * q.size + far.size)),
    )(chain, lengths, q, k, v, far)


def columns_kernel(idx_ref, w_ref, out_ref):
    out_ref[...] = w_ref[...]


def sibling_columns(idx, w_out):
    rows, cols = w_out.shape
    width = cols // (2 * RING)
    return pl.pallas_call(
        columns_kernel,
        grid_spec=pltpu.PrefetchScalarGridSpec(
            num_scalar_prefetch=1,
            grid=(RING,),
            in_specs=[pl.BlockSpec((rows, width), lambda j, s: (0, s[16 + j]))],
            out_specs=pl.BlockSpec((rows, width), lambda j, s: (0, j)),
        ),
        out_shape=jax.ShapeDtypeStruct((rows, RING * width), jnp.bfloat16),
        compiler_params=params(32),
        cost_estimate=cost(0, 2 * rows * cols),
    )(idx, w_out)


def chunk_kernel(idx_ref, a_ref, b_ref, wa_ref, wb_ref, *refs):
    *terms, out_ref = refs
    acc = jnp.dot(a_ref[...], wa_ref[...], preferred_element_type=jnp.float32)
    acc += jnp.dot(b_ref[...], wb_ref[...], preferred_element_type=jnp.float32)
    for t in terms:
        acc += t[...].astype(jnp.float32)
    out_ref[...] = acc.astype(out_ref.dtype)


def chunk(idx, which, part, parts, own, sib, w_own, w_sib, *terms):
    rows = own.shape[0] // parts
    depth = own.shape[1]
    width = w_own.shape[1] // (2 * RING)
    cut = 2
    tile = width // cut
    left = pl.BlockSpec((rows, depth), lambda j, s: (part, 0))
    term = pl.BlockSpec((rows, tile), lambda j, s: (0, j))
    return pl.pallas_call(
        chunk_kernel,
        grid_spec=pltpu.PrefetchScalarGridSpec(
            num_scalar_prefetch=1,
            grid=(cut,),
            in_specs=[
                left,
                left,
                pl.BlockSpec((depth, tile), lambda j, s: (0, s[8 + which] * cut + j)),
                pl.BlockSpec((depth, tile), lambda j, s: (0, s[12 + which] * cut + j)),
            ]
            + [term for _ in terms],
            out_specs=term,
        ),
        out_shape=jax.ShapeDtypeStruct((rows, width), jnp.bfloat16),
        compiler_params=params(32),
        cost_estimate=cost(4 * rows * depth * width, 4 * depth * width + 2 * rows * width),
    )(idx, own, sib, w_own, w_sib, *terms)


def per_device(
    hidden, w_query, w_key, w_value, w_out, prefix_keys, prefix_values, seg_lengths, ancestors
):
    head = lax.axis_index("head")
    idx = lax.dynamic_index_in_dim(jnp.asarray(index_table()), head, 0, keepdims=False)
    chain = ancestors.reshape(-1)
    half = hidden.shape[0] // 2

    top, bottom = hidden[:half], hidden[half:]
    low_top = send(top, UP)
    up_bottom = send(bottom, DOWN)
    low_bottom = send(bottom, UP)
    up_top = send(top, DOWN)
    sib = send(hidden, SIBLING)
    far_top = send(low_top, UP)
    far_bottom = send(up_bottom, DOWN)
    got = [low_top, low_bottom, up_top, up_bottom, far_top, far_bottom]
    twin = [send(x, SIBLING) for x in got]
    halves = []
    for n in range(3):
        halves += got[2 * n : 2 * n + 2] + twin[2 * n : 2 * n + 2]

    segs = spread(prefix_keys, prefix_values)
    table = exchange(segs).reshape(-1, 2 * GRAN, HD)
    wanted = pick(chain, table)
    far = exchange(wanted.reshape(segs.shape))

    w_sib = send(sibling_columns(idx, w_out), SIBLING)

    q, k, v = project(idx, hidden, sib, halves, w_query, w_key, w_value)
    own = attend(chain, seg_lengths, q, k, v, far)
    other = send(own, SIBLING)

    def piece(which, part, *terms):
        return chunk(idx, which, part, 2, own, other, w_out, w_sib, *terms)

    via_up = send(piece(0, 0), UP)
    via_down = send(piece(0, 1), DOWN)
    low_b = send(piece(1, 1), UP)
    up_t = send(piece(2, 0), DOWN)
    low_t = send(piece(1, 0, via_up), UP)
    up_b = send(piece(2, 1, via_down), DOWN)
    out_top = piece(3, 0, low_t, up_t)
    out_bottom = piece(3, 1, low_b, up_b)
    return jnp.concatenate([out_top, out_bottom], axis=0)


def solution(mesh):
    in_specs = (
        P("seq", "head"),
        P(None, "head"),
        P(None, "head"),
        P(None, "head"),
        P("head", None),
        P("seq", "head"),
        P("seq", "head"),
        P(),
        P(),
    )
    out_specs = P("seq", "head")
    return jax.shard_map(
        per_device, mesh=mesh, in_specs=in_specs, out_specs=out_specs, check_vma=False
    )
```

time: 424 us -> 154 us (0.36)
  waiting for transfers between devices: 316 us -> 50.8 us
  Pallas kernels: 0 us -> 48.9 us
  matrix products: 40.4 us -> 0 us
  starting transfers between devices: 0.12 us -> 36.5 us
  loops' own time: 31 us -> 0 us
  between operations: 13.2 us -> 0.23 us
  other arithmetic: 9.93 us -> 1.04 us
    all_gather x3 -> x0, waiting for transfers between devices: 254 us -> none  [the longest x1 113 us: per_device(): piece_values = lax.all_gather(prefix_values, 'seq', axis=0, tiled=True)]
    reduce_scatter x1 -> x0, waiting for transfers between devices: 59.7 us -> none  [per_device(): lax.psum_scatter(partial_out.astype(jnp.bfloat16), 'head', scatter_dimens...]
    pallas_call x0 -> x13, Pallas kernels: none -> 48.9 us  [the longest x8 20.7 us: chunk(): pl.pallas_call(chunk_kernel, grid_spec=pltpu.PrefetchScalarGridSpec(num_s...]
    ppermute x0 -> x21, waiting for transfers between devices: none -> 48.8 us  [send(): return lax.ppermute(x, 'head', pairs)]
    dot_general x26 -> x0, matrix products: 40.4 us -> none  [the longest x1 10.3 us: per_device(): partial_out = jnp.dot(attended, w_out, preferred_element_type=jnp.float32)]
    another operation x17 -> x0, loops' own time: 31 us -> none  [the longest x1 29.8 us: per_device(): lax.fori_loop(0, roll_count, visit, (own_max, own_sum, own_weighted))]
    ppermute x0 -> x21, starting transfers between devices: none -> 23.1 us  [send(): return lax.ppermute(x, 'head', pairs)]
    all_to_all x0 -> x2, starting transfers between devices: none -> 13.3 us  [exchange(): return lax.all_to_all(x, 'seq', 0, 0, tiled=True)]
  transfers between devices with their start and end apart: 4 -> 23, of which waited for: 4 -> 10; matrix products, arithmetic and copies ran while one was open for 6% -> 1% of each run, Pallas kernels for 0% -> 28%
where the time goes in v1:
time: 154 us; the launch traced here: 152 us
  waiting for transfers between devices  50.8 us (33%)
  Pallas kernels  48.9 us (32%)
  starting transfers between devices  36.5 us (24%)
  local copies, waits for them, and re-layouts  15 us (10%)
    ppermute x21, waiting for transfers between devices, send(): return lax.ppermute(x, 'head', pairs)  48.8 us
    ppermute x21, starting transfers between devices, send(): return lax.ppermute(x, 'head', pairs)  23.1 us
    pallas_call x8, Pallas kernels, chunk(): pl.pallas_call(chunk_kernel, grid_spec=pltpu.PrefetchScalarGridSpec(num_s...  20.7 us
    pallas_call x1, Pallas kernels, project(): pl.pallas_call(project_kernel, grid_spec=pltpu.PrefetchScalarGridSpec(num...  14.5 us
    unnamed x27, local copies, waits for them, and re-layouts  13.3 us
    all_to_all x2, starting transfers between devices, exchange(): return lax.all_to_all(x, 'seq', 0, 0, tiled=True)  13.3 us
    pallas_call x1, Pallas kernels, attend(): pl.pallas_call(attend_kernel, grid_spec=pltpu.PrefetchScalarGridSpec(num_...  7.56 us
    pallas_call x1, Pallas kernels, sibling_columns(): pl.pallas_call(columns_kernel, grid_spec=pltpu.PrefetchScalarGridSpec(num...  3.33 us
  transfers between devices with their start and end apart: 23, of which 10 were waited for; matrix products, arithmetic and copies ran while one was open for 1% of the time, Pallas kernels for 28%

profile of v1, /device:TPU:1, one launch (start us, length us, event | category | flops | bytes accessed | tf_op | source)
XLA Modules:
  0.0 152.5 jit_solution(17934565681760433885)
XLA Ops:
  0.0 1.2 copy-done.3
  1.2 1.2 copy-done.4
  2.8 1.4 copy-done.2
  4.2 8.4 %all-to-all-start = ((bf16[16,16,32,128]{3,2,1,0:T(8,128)(2,1)}), bf16[16,16,32,128]{3,2,1,0:T(8,128)(2,1)S(1)}, u32[]{:S(2)}, u32[]{:S(2)}) async-start(bf16[16,16,32,128]{3,2,1,0:T(8,128)(2,1)} %copy-done.2), calls=%async_computation | async-start | bytes 4194304 | tf_op jit(solution)/shard_map/all_to_all | solution.py:105
  12.6 0.7 dynamic-slice_bitcast_fusion.idx_ref
  13.3 3.4 %copy-done = bf16[512,8192]{1,0:T(8,128)(2,1)S(1)} copy-done((bf16[512,8192]{1,0:T(8,128)(2,1)S(1)}, bf16[512,8192]{1,0:T(8,128)(2,1)}, u32[]{:S(2)}) %copy-start) | copy-done | bytes 8388632
  16.7 3.3 %shard_map.104 = bf16[512,4096]{1,0:T(8,128)(2,1)} custom-call(s32[20]{0:T(128)S(1)} %dynamic-slice_bitcast_fusion.idx_ref, bf16[512,8192]{1,0:T(8,128)(2,1)S(1)} %copy-done), custom_call_target="tpu_custom_call" | custom-call | bytes 8388608 | tf_op jit(solution)/shard_map/pallas_call | solution.py:229
  20.1 1.0 collective-permute-start.14
  21.0 0.9 fusion
  21.9 2.7 %collective-permute-start.6 = (bf16[256,1024]{1,0:T(8,128)(2,1)S(1)}, bf16[256,1024]{1,0:T(8,128)(2,1)S(1)}, u32[]{:S(2)}, u32[]{:S(2)}) collective-permute-start(bf16[256,1024]{1,0:T(8,128)(2,1)S(1)} %get-tuple-element.11), channel_id=1, source_target_pairs={{0,6},{1,7},{2,0},{3,1},{4,2},{5,3},{6,4},{7,5},{8,14},{9,15},{10,... | collective-permute-start | bytes 1572872 | tf_op jit(solution)/shard_map/ppermute | solution.py:33
  24.6 2.7 %collective-permute-start.5 = (bf16[256,1024]{1,0:T(8,128)(2,1)}, bf16[256,1024]{1,0:T(8,128)(2,1)}, u32[]{:S(2)}, u32[]{:S(2)}) collective-permute-start(bf16[256,1024]{1,0:T(8,128)(2,1)} %get-tuple-element.12), channel_id=1, source_target_pairs={{0,6},{1,7},{2,0},{3,1},{4,2},{5,3},{6,4},{7,5},{8,14},{9,15},{10,... | collective-permute-start | bytes 1572872 | tf_op jit(solution)/shard_map/ppermute | solution.py:33
  27.3 8.7 %collective-permute-done.6.refs_7_ = bf16[256,1024]{1,0:T(8,128)(2,1)S(1)} collective-permute-done((bf16[256,1024]{1,0:T(8,128)(2,1)S(1)}, bf16[256,1024]{1,0:T(8,128)(2,1)S(1)}, u32[]{:S(2)}, u32[]{:S(2)}) %collective-permute-start.6) | collective-permute-done | bytes 524320 | tf_op jit(solution)/shard_map/ppermute | solution.py:33
  36.0 3.4 %collective-permute-start.10 = (bf16[256,1024]{1,0:T(8,128)(2,1)S(1)}, bf16[256,1024]{1,0:T(8,128)(2,1)}, u32[]{:S(2)}, u32[]{:S(2)}) collective-permute-start(bf16[256,1024]{1,0:T(8,128)(2,1)S(1)} %collective-permute-done.6.refs_7_), channel_id=1, source_target_pairs={{0,6},{1,7},{2,0},{3,1},{4,2},{5,3},{6,4},{7,5},{8,14},{9,15},{10,... | collective-permute-start | bytes 1572872 | tf_op jit(solution)/shard_map/ppermute | solution.py:33
  39.4 1.5 collective-permute-start.8
  41.1 2.1 %all-to-all-done = bf16[16,16,32,128]{3,2,1,0:T(8,128)(2,1)S(1)} async-done(((bf16[16,16,32,128]{3,2,1,0:T(8,128)(2,1)}), bf16[16,16,32,128]{3,2,1,0:T(8,128)(2,1)S(1)}, u32[]{:S(2)}, u32[]{:S(2)}) %all-to-all-start) | async-done | bytes 2097184 | tf_op jit(solution)/shard_map/all_to_all | solution.py:105
  43.1 2.4 %shard_map.102 = bf16[256,32,128]{2,1,0:T(8,128)(2,1)} custom-call(s32[256]{0:T(256)S(1)} %reshape.15.chain_ref, bf16[256,32,128]{2,1,0:T(8,128)(2,1)S(1)} %bitcast.6), custom_call_target="tpu_custom_call" | custom-call | bytes 4194304 | tf_op jit(solution)/shard_map/pallas_call | solution.py:90
  45.6 4.9 %all-to-all-start.1 = ((bf16[16,16,32,128]{3,2,1,0:T(8,128)(2,1)}), bf16[16,16,32,128]{3,2,1,0:T(8,128)(2,1)S(1)}, u32[]{:S(2)}, u32[]{:S(2)}) async-start(bf16[16,16,32,128]{3,2,1,0:T(8,128)(2,1)} %bitcast.4), calls=%async_computation.1 | async-start | bytes 4194304 | tf_op jit(solution)/shard_map/all_to_all | solution.py:105
  50.5 1.0 collective-permute-start
  51.6 6.8 %collective-permute-done.10.refs_11_ = bf16[256,1024]{1,0:T(8,128)(2,1)} collective-permute-done((bf16[256,1024]{1,0:T(8,128)(2,1)S(1)}, bf16[256,1024]{1,0:T(8,128)(2,1)}, u32[]{:S(2)}, u32[]{:S(2)}) %collective-permute-start.10) | collective-permute-done | bytes 524320 | tf_op jit(solution)/shard_map/ppermute | solution.py:33
  58.4 0.8 collective-permute-start.7
  59.2 0.9 collective-permute-start.9
  60.4 0.6 collective-permute-done.7.refs_8_
  61.3 13.9 %collective-permute-done.9.refs_10_ = bf16[256,1024]{1,0:T(8,128)(2,1)S(1)} collective-permute-done((bf16[256,1024]{1,0:T(8,128)(2,1)}, bf16[256,1024]{1,0:T(8,128)(2,1)S(1)}, u32[]{:S(2)}, u32[]{:S(2)}) %collective-permute-start.9) | collective-permute-done | bytes 524320 | tf_op jit(solution)/shard_map/ppermute | solution.py:33
  75.3 0.6 collective-permute-start.11
  75.9 1.5 collective-permute-done.11.refs_12_
  77.4 0.8 copy-done.12
  78.2 14.5 %shard_map.100 = (bf16[512,512]{1,0:T(8,128)(2,1)S(1)}, bf16[512,128]{1,0:T(8,128)(2,1)S(1)}, bf16[512,128]{1,0:T(8,128)(2,1)S(1)}) custom-call(s32[20]{0:T(128)S(1)} %dynamic-slice_bitcast_fusion.idx_ref, bf16[512,1024]{1,0:T(8,128)(2,1)} %refs_0_.1, bf16[512,1024]{1,0:T(8,128)(2,1)} %copy-done.10, bf16[256,1024]{1,0:T(8,128)(2,1)} %collective-permute-done.1.refs_2_, ...), custom_call_target="tpu_custom_call" | custom-call | flops 6442450944 | bytes 20971520 | tf_op jit(solution)/shard_map/pallas_call | solution.py:145
  92.7 0.8 copy-done.6
  93.5 1.0 copy-done.7
  94.5 7.6 %shard_map.103.a_ref = bf16[512,512]{1,0:T(8,128)(2,1)S(1)} custom-call(s32[256]{0:T(256)S(1)} %reshape.15.chain_ref, s32[256]{0:T(256)S(1)} %copy-done.5, bf16[512,512]{1,0:T(8,128)(2,1)S(1)} %copy-done.7, bf16[512,128]{1,0:T(8,128)(2,1)S(1)} %get-tuple-element.9.k_ref, bf16[512,128]{1,0:T(8,128)(2,1)S(1)} %get-tuple-element.10.v_ref, ...), custom_call_target="tpu_custom_call" | custom-call | flops 1207959552 | bytes 3145728 | tf_op jit(solution)/shard_map/pallas_call | solution.py:203
  102.1 0.4 collective-permute-start.13
  102.5 1.6 %collective-permute-done.13.b_ref = bf16[512,512]{1,0:T(8,128)(2,1)S(1)} collective-permute-done((bf16[512,512]{1,0:T(8,128)(2,1)S(1)}, bf16[512,512]{1,0:T(8,128)(2,1)S(1)}, u32[]{:S(2)}, u32[]{:S(2)}) %collective-permute-start.13) | collective-permute-done | bytes 524320 | tf_op jit(solution)/shard_map/ppermute | solution.py:33
  104.1 3.4 %copy-done.1 = bf16[512,8192]{1,0:T(8,128)(2,1)S(1)} copy-done((bf16[512,8192]{1,0:T(8,128)(2,1)S(1)}, bf16[512,8192]{1,0:T(8,128)(2,1)}, u32[]{:S(2)}) %copy-start.1) | copy-done | bytes 8388632
  107.5 2.6 %shard_map.105 = bf16[256,1024]{1,0:T(8,128)(2,1)S(1)} custom-call(s32[20]{0:T(128)S(1)} %dynamic-slice_bitcast_fusion.idx_ref, bf16[512,512]{1,0:T(8,128)(2,1)S(1)} %shard_map.103.a_ref, bf16[512,512]{1,0:T(8,128)(2,1)S(1)} %collective-permute-done.13.b_ref, bf16[512,8192]{1,0:T(8,128)(2,1)S(1)} %copy-done.1, bf16[512,4096]{1,0:T(8,128)(2,1)} %collective-permute-done.14.wb_ref), custom_call_target="tpu_custom_call" | custom-call | flops 536870912 | bytes 2621440 | tf_op jit(solution)/shard_map/pallas_call | solution.py:260
  110.1 2.6 %shard_map.110 = bf16[256,1024]{1,0:T(8,128)(2,1)S(1)} custom-call(s32[20]{0:T(128)S(1)} %dynamic-slice_bitcast_fusion.idx_ref, bf16[512,512]{1,0:T(8,128)(2,1)S(1)} %shard_map.103.a_ref, bf16[512,512]{1,0:T(8,128)(2,1)S(1)} %collective-permute-done.13.b_ref, bf16[512,8192]{1,0:T(8,128)(2,1)S(1)} %copy-done.1, bf16[512,4096]{1,0:T(8,128)(2,1)} %collective-permute-done.14.wb_ref), custom_call_target="tpu_custom_call" | custom-call | flops 536870912 | bytes 2621440 | tf_op jit(solution)/shard_map/pallas_call | solution.py:260
  112.7 2.7 %collective-permute-start.19 = (bf16[256,1024]{1,0:T(8,128)(2,1)S(1)}, bf16[256,1024]{1,0:T(8,128)(2,1)S(1)}, u32[]{:S(2)}, u32[]{:S(2)}) collective-permute-start(bf16[256,1024]{1,0:T(8,128)(2,1)S(1)} %shard_map.110), channel_id=1, source_target_pairs={{0,6},{1,7},{2,0},{3,1},{4,2},{5,3},{6,4},{7,5},{8,14},{9,15},{10,... | collective-permute-start | bytes 1572872 | tf_op jit(solution)/shard_map/ppermute | solution.py:33
  115.5 2.6 %shard_map.107 = bf16[256,1024]{1,0:T(8,128)(2,1)S(1)} custom-call(s32[20]{0:T(128)S(1)} %dynamic-slice_bitcast_fusion.idx_ref, bf16[512,512]{1,0:T(8,128)(2,1)S(1)} %shard_map.103.a_ref, bf16[512,512]{1,0:T(8,128)(2,1)S(1)} %collective-permute-done.13.b_ref, bf16[512,8192]{1,0:T(8,128)(2,1)S(1)} %copy-done.1, bf16[512,4096]{1,0:T(8,128)(2,1)} %collective-permute-done.14.wb_ref), custom_call_target="tpu_custom_call" | custom-call | flops 536870912 | bytes 2621440 | tf_op jit(solution)/shard_map/pallas_call | solution.py:260
  118.4 2.6 %shard_map.109 = bf16[256,1024]{1,0:T(8,128)(2,1)S(1)} custom-call(s32[20]{0:T(128)S(1)} %dynamic-slice_bitcast_fusion.idx_ref, bf16[512,512]{1,0:T(8,128)(2,1)S(1)} %shard_map.103.a_ref, bf16[512,512]{1,0:T(8,128)(2,1)S(1)} %collective-permute-done.13.b_ref, bf16[512,8192]{1,0:T(8,128)(2,1)S(1)} %copy-done.1, bf16[512,4096]{1,0:T(8,128)(2,1)} %collective-permute-done.14.wb_ref), custom_call_target="tpu_custom_call" | custom-call | flops 536870912 | bytes 2621440 | tf_op jit(solution)/shard_map/pallas_call | solution.py:260
  120.9 1.5 collective-permute-start.18
  122.4 2.1 %collective-permute-done.15.refs_0_ = bf16[256,1024]{1,0:T(8,128)(2,1)S(1)} collective-permute-done((bf16[256,1024]{1,0:T(8,128)(2,1)S(1)}, bf16[256,1024]{1,0:T(8,128)(2,1)S(1)}, u32[]{:S(2)}, u32[]{:S(2)}) %collective-permute-start.15) | collective-permute-done | bytes 524320 | tf_op jit(solution)/shard_map/ppermute | solution.py:33
  124.5 2.6 %shard_map.106 = bf16[256,1024]{1,0:T(8,128)(2,1)S(1)} custom-call(s32[20]{0:T(128)S(1)} %dynamic-slice_bitcast_fusion.idx_ref, bf16[512,512]{1,0:T(8,128)(2,1)S(1)} %shard_map.103.a_ref, bf16[512,512]{1,0:T(8,128)(2,1)S(1)} %collective-permute-done.13.b_ref, bf16[512,8192]{1,0:T(8,128)(2,1)S(1)} %copy-done.1, ...), custom_call_target="tpu_custom_call" | custom-call | flops 536870912 | bytes 2621440 | tf_op jit(solution)/shard_map/pallas_call | solution.py:260
  127.2 2.6 %shard_map.111 = bf16[256,1024]{1,0:T(8,128)(2,1)S(1)} custom-call(s32[20]{0:T(128)S(1)} %dynamic-slice_bitcast_fusion.idx_ref, bf16[512,512]{1,0:T(8,128)(2,1)S(1)} %shard_map.103.a_ref, bf16[512,512]{1,0:T(8,128)(2,1)S(1)} %collective-permute-done.13.b_ref, bf16[512,8192]{1,0:T(8,128)(2,1)S(1)} %copy-done.1, ...), custom_call_target="tpu_custom_call" | custom-call | flops 536870912 | bytes 2621440 | tf_op jit(solution)/shard_map/pallas_call | solution.py:260
  129.8 2.7 %collective-permute-start.20 = (bf16[256,1024]{1,0:T(8,128)(2,1)S(1)}, bf16[256,1024]{1,0:T(8,128)(2,1)S(1)}, u32[]{:S(2)}, u32[]{:S(2)}) collective-permute-start(bf16[256,1024]{1,0:T(8,128)(2,1)S(1)} %shard_map.111), channel_id=1, source_target_pairs={{0,6},{1,7},{2,0},{3,1},{4,2},{5,3},{6,4},{7,5},{8,14},{9,15},{10,... | collective-permute-start | bytes 1572872 | tf_op jit(solution)/shard_map/ppermute | solution.py:33
  132.5 4.8 %collective-permute-done.17.refs_1_ = bf16[256,1024]{1,0:T(8,128)(2,1)S(1)} collective-permute-done((bf16[256,1024]{1,0:T(8,128)(2,1)S(1)}, bf16[256,1024]{1,0:T(8,128)(2,1)S(1)}, u32[]{:S(2)}, u32[]{:S(2)}) %collective-permute-start.17) | collective-permute-done | bytes 524320 | tf_op jit(solution)/shard_map/ppermute | solution.py:33
  137.3 8.8 %collective-permute-done.16.refs_0_ = bf16[256,1024]{1,0:T(8,128)(2,1)S(1)} collective-permute-done((bf16[256,1024]{1,0:T(8,128)(2,1)S(1)}, bf16[256,1024]{1,0:T(8,128)(2,1)S(1)}, u32[]{:S(2)}, u32[]{:S(2)}) %collective-permute-start.16) | collective-permute-done | bytes 524320 | tf_op jit(solution)/shard_map/ppermute | solution.py:33
  146.2 2.6 %shard_map.108 = bf16[256,1024]{1,0:T(8,128)(2,1)S(1)} custom-call(s32[20]{0:T(128)S(1)} %dynamic-slice_bitcast_fusion.idx_ref, bf16[512,512]{1,0:T(8,128)(2,1)S(1)} %shard_map.103.a_ref, bf16[512,512]{1,0:T(8,128)(2,1)S(1)} %collective-permute-done.13.b_ref, bf16[512,8192]{1,0:T(8,128)(2,1)S(1)} %copy-done.1, ...), custom_call_target="tpu_custom_call" | custom-call | flops 536870912 | bytes 2621440 | tf_op jit(solution)/shard_map/pallas_call | solution.py:260
  148.8 2.6 %shard_map.112 = bf16[256,1024]{1,0:T(8,128)(2,1)S(1)} custom-call(s32[20]{0:T(128)S(1)} %dynamic-slice_bitcast_fusion.idx_ref, bf16[512,512]{1,0:T(8,128)(2,1)S(1)} %shard_map.103.a_ref, bf16[512,512]{1,0:T(8,128)(2,1)S(1)} %collective-permute-done.13.b_ref, bf16[512,8192]{1,0:T(8,128)(2,1)S(1)} %copy-done.1, ...), custom_call_target="tpu_custom_call" | custom-call | flops 536870912 | bytes 2621440 | tf_op jit(solution)/shard_map/pallas_call | solution.py:260
  151.4 1.0 pad_maximum_fusion
  (42 shorter events, 1.9 us)
Async XLA Ops:
  0.0 1.2 copy-start.3
  1.2 1.2 copy-start.4
  2.8 1.4 copy-start.2
  4.2 38.9 %all-to-all-start = ((bf16[16,16,32,128]{3,2,1,0:T(8,128)(2,1)}), bf16[16,16,32,128]{3,2,1,0:T(8,128)(2,1)S(1)}, u32[]{:S(2)}, u32[]{:S(2)}) async-start(bf16[16,16,32,128]{3,2,1,0:T(8,128)(2,1)} %copy-done.2), calls=%async_computation | async-start | bytes 4194304 | tf_op jit(solution)/shard_map/all_to_all | solution.py:105
  13.3 3.4 %copy-start = (bf16[512,8192]{1,0:T(8,128)(2,1)S(1)}, bf16[512,8192]{1,0:T(8,128)(2,1)}, u32[]{:S(2)}) copy-start(bf16[512,8192]{1,0:T(8,128)(2,1)} %wa_ref.15) | copy-start | bytes 25165828
  16.7 4.3 %copy-start.8 = (bf16[512,1024]{1,0:T(8,128)(2,1)S(1)}, bf16[512,1024]{1,0:T(8,128)(2,1)}, u32[]{:S(2)}) copy-start(bf16[512,1024]{1,0:T(8,128)(2,1)} %refs_0_.1) | copy-start | bytes 3145732
  20.1 20.8 %copy-start.9 = (s32[64,4]{0,1:T(4,128)S(1)}, s32[64,4]{0,1:T(4,128)}, u32[]{:S(2)}) copy-start(s32[64,4]{0,1:T(4,128)} %param.18) | copy-start | bytes 3076
  20.1 82.5 %collective-permute-start.14 = (bf16[512,4096]{1,0:T(8,128)(2,1)}, bf16[512,4096]{1,0:T(8,128)(2,1)}, u32[]{:S(2)}, u32[]{:S(2)}) collective-permute-start(bf16[512,4096]{1,0:T(8,128)(2,1)} %shard_map.104), channel_id=1, source_target_pairs={{0,1},{1,0},{2,3},{3,2},{4,5},{5,4},{6,7},{7,6},{8,9},{9,8},{10,11... | collective-permute-start | bytes 12582920 | tf_op jit(solution)/shard_map/ppermute | solution.py:33
  21.9 14.1 %collective-permute-start.6 = (bf16[256,1024]{1,0:T(8,128)(2,1)S(1)}, bf16[256,1024]{1,0:T(8,128)(2,1)S(1)}, u32[]{:S(2)}, u32[]{:S(2)}) collective-permute-start(bf16[256,1024]{1,0:T(8,128)(2,1)S(1)} %get-tuple-element.11), channel_id=1, source_target_pairs={{0,6},{1,7},{2,0},{3,1},{4,2},{5,3},{6,4},{7,5},{8,14},{9,15},{10,... | collective-permute-start | bytes 1572872 | tf_op jit(solution)/shard_map/ppermute | solution.py:33
  24.6 14.8 %collective-permute-start.2 = (bf16[256,1024]{1,0:T(8,128)(2,1)S(1)}, bf16[256,1024]{1,0:T(8,128)(2,1)S(1)}, u32[]{:S(2)}, u32[]{:S(2)}) collective-permute-start(bf16[256,1024]{1,0:T(8,128)(2,1)S(1)} %get-tuple-element.11), channel_id=1, source_target_pairs={{0,2},{1,3},{2,4},{3,5},{4,6},{5,7},{6,0},{7,1},{8,10},{9,11},{10,... | collective-permute-start | bytes 1572872 | tf_op jit(solution)/shard_map/ppermute | solution.py:33
  24.6 25.9 %collective-permute-start.5 = (bf16[256,1024]{1,0:T(8,128)(2,1)}, bf16[256,1024]{1,0:T(8,128)(2,1)}, u32[]{:S(2)}, u32[]{:S(2)}) collective-permute-start(bf16[256,1024]{1,0:T(8,128)(2,1)} %get-tuple-element.12), channel_id=1, source_target_pairs={{0,6},{1,7},{2,0},{3,1},{4,2},{5,3},{6,4},{7,5},{8,14},{9,15},{10,... | collective-permute-start | bytes 1572872 | tf_op jit(solution)/shard_map/ppermute | solution.py:33
  27.3 24.2 %collective-permute-start.1 = (bf16[256,1024]{1,0:T(8,128)(2,1)}, bf16[256,1024]{1,0:T(8,128)(2,1)}, u32[]{:S(2)}, u32[]{:S(2)}) collective-permute-start(bf16[256,1024]{1,0:T(8,128)(2,1)} %get-tuple-element.12), channel_id=1, source_target_pairs={{0,2},{1,3},{2,4},{3,5},{4,6},{5,7},{6,0},{7,1},{8,10},{9,11},{10,... | collective-permute-start | bytes 1572872 | tf_op jit(solution)/shard_map/ppermute | solution.py:33
  36.0 22.5 %collective-permute-start.10 = (bf16[256,1024]{1,0:T(8,128)(2,1)S(1)}, bf16[256,1024]{1,0:T(8,128)(2,1)}, u32[]{:S(2)}, u32[]{:S(2)}) collective-permute-start(bf16[256,1024]{1,0:T(8,128)(2,1)S(1)} %collective-permute-done.6.refs_7_), channel_id=1, source_target_pairs={{0,6},{1,7},{2,0},{3,1},{4,2},{5,3},{6,4},{7,5},{8,14},{9,15},{10,... | collective-permute-start | bytes 1572872 | tf_op jit(solution)/shard_map/ppermute | solution.py:33
  39.4 19.8 %collective-permute-start.8 = (bf16[256,1024]{1,0:T(8,128)(2,1)S(1)}, bf16[256,1024]{1,0:T(8,128)(2,1)}, u32[]{:S(2)}, u32[]{:S(2)}) collective-permute-start(bf16[256,1024]{1,0:T(8,128)(2,1)S(1)} %collective-permute-done.6.refs_7_), channel_id=1, source_target_pairs={{0,1},{1,0},{2,3},{3,2},{4,5},{5,4},{6,7},{7,6},{8,9},{9,8},{10,11... | collective-permute-start | bytes 1572872 | tf_op jit(solution)/shard_map/ppermute | solution.py:33
  45.6 47.9 %all-to-all-start.1 = ((bf16[16,16,32,128]{3,2,1,0:T(8,128)(2,1)}), bf16[16,16,32,128]{3,2,1,0:T(8,128)(2,1)S(1)}, u32[]{:S(2)}, u32[]{:S(2)}) async-start(bf16[16,16,32,128]{3,2,1,0:T(8,128)(2,1)} %bitcast.4), calls=%async_computation.1 | async-start | bytes 4194304 | tf_op jit(solution)/shard_map/all_to_all | solution.py:105
  50.5 43.0 %copy-start.5 = (s32[256]{0:T(256)S(1)}, s32[256]{0:T(256)}, u32[]{:S(2)}) copy-start(s32[256]{0:T(256)} %len_ref.1) | copy-start | bytes 3076
  50.5 25.3 %collective-permute-start = (bf16[512,1024]{1,0:T(8,128)(2,1)}, bf16[512,1024]{1,0:T(8,128)(2,1)S(1)}, u32[]{:S(2)}, u32[]{:S(2)}) collective-permute-start(bf16[512,1024]{1,0:T(8,128)(2,1)} %refs_0_.1), channel_id=1, source_target_pairs={{0,1},{1,0},{2,3},{3,2},{4,5},{5,4},{6,7},{7,6},{8,9},{9,8},{10,11... | collective-permute-start | bytes 3145736 | tf_op jit(solution)/shard_map/ppermute | solution.py:33
  51.5 8.6 %collective-permute-start.4 = (bf16[256,1024]{1,0:T(8,128)(2,1)S(1)}, bf16[256,1024]{1,0:T(8,128)(2,1)S(1)}, u32[]{:S(2)}, u32[]{:S(2)}) collective-permute-start(bf16[256,1024]{1,0:T(8,128)(2,1)S(1)} %collective-permute-done.2.refs_3_), channel_id=1, source_target_pairs={{0,1},{1,0},{2,3},{3,2},{4,5},{5,4},{6,7},{7,6},{8,9},{9,8},{10,11... | collective-permute-start | bytes 1572872 | tf_op jit(solution)/shard_map/ppermute | solution.py:33
  58.4 2.5 %collective-permute-start.7 = (bf16[256,1024]{1,0:T(8,128)(2,1)}, bf16[256,1024]{1,0:T(8,128)(2,1)S(1)}, u32[]{:S(2)}, u32[]{:S(2)}) collective-permute-start(bf16[256,1024]{1,0:T(8,128)(2,1)} %collective-permute-done.5.refs_6_), channel_id=1, source_target_pairs={{0,1},{1,0},{2,3},{3,2},{4,5},{5,4},{6,7},{7,6},{8,9},{9,8},{10,11... | collective-permute-start | bytes 1572872 | tf_op jit(solution)/shard_map/ppermute | solution.py:33
  59.2 16.0 %collective-permute-start.9 = (bf16[256,1024]{1,0:T(8,128)(2,1)}, bf16[256,1024]{1,0:T(8,128)(2,1)S(1)}, u32[]{:S(2)}, u32[]{:S(2)}) collective-permute-start(bf16[256,1024]{1,0:T(8,128)(2,1)} %collective-permute-done.1.refs_2_), channel_id=1, source_target_pairs={{0,2},{1,3},{2,4},{3,5},{4,6},{5,7},{6,0},{7,1},{8,10},{9,11},{10,... | collective-permute-start | bytes 1572872 | tf_op jit(solution)/shard_map/ppermute | solution.py:33
  60.1 15.7 %collective-permute-start.3 = (bf16[256,1024]{1,0:T(8,128)(2,1)}, bf16[256,1024]{1,0:T(8,128)(2,1)S(1)}, u32[]{:S(2)}, u32[]{:S(2)}) collective-permute-start(bf16[256,1024]{1,0:T(8,128)(2,1)} %collective-permute-done.1.refs_2_), channel_id=1, source_target_pairs={{0,1},{1,0},{2,3},{3,2},{4,5},{5,4},{6,7},{7,6},{8,9},{9,8},{10,11... | collective-permute-start | bytes 1572872 | tf_op jit(solution)/shard_map/ppermute | solution.py:33
  61.0 14.9 %collective-permute-start.12 = (bf16[256,1024]{1,0:T(8,128)(2,1)}, bf16[256,1024]{1,0:T(8,128)(2,1)S(1)}, u32[]{:S(2)}, u32[]{:S(2)}) collective-permute-start(bf16[256,1024]{1,0:T(8,128)(2,1)} %collective-permute-done.10.refs_11_), channel_id=1, source_target_pairs={{0,1},{1,0},{2,3},{3,2},{4,5},{5,4},{6,7},{7,6},{8,9},{9,8},{10,11... | collective-permute-start | bytes 1572872 | tf_op jit(solution)/shard_map/ppermute | solution.py:33
  75.3 2.1 %collective-permute-start.11 = (bf16[256,1024]{1,0:T(8,128)(2,1)S(1)}, bf16[256,1024]{1,0:T(8,128)(2,1)S(1)}, u32[]{:S(2)}, u32[]{:S(2)}) collective-permute-start(bf16[256,1024]{1,0:T(8,128)(2,1)S(1)} %collective-permute-done.9.refs_10_), channel_id=1, source_target_pairs={{0,1},{1,0},{2,3},{3,2},{4,5},{5,4},{6,7},{7,6},{8,9},{9,8},{10,11... | collective-permute-start | bytes 1572872 | tf_op jit(solution)/shard_map/ppermute | solution.py:33
  75.8 1.5 %copy-start.10 = (bf16[512,1024]{1,0:T(8,128)(2,1)}, bf16[512,1024]{1,0:T(8,128)(2,1)S(1)}, u32[]{:S(2)}) copy-start(bf16[512,1024]{1,0:T(8,128)(2,1)S(1)} %collective-permute-done.refs_1_) | copy-start | bytes 3145732
  75.9 1.5 copy-start.11
  77.4 0.8 copy-start.12
  92.7 0.8 copy-start.6
  93.5 1.0 copy-start.7
  102.1 2.0 %collective-permute-start.13 = (bf16[512,512]{1,0:T(8,128)(2,1)S(1)}, bf16[512,512]{1,0:T(8,128)(2,1)S(1)}, u32[]{:S(2)}, u32[]{:S(2)}) collective-permute-start(bf16[512,512]{1,0:T(8,128)(2,1)S(1)} %shard_map.103.a_ref), channel_id=1, source_target_pairs={{0,1},{1,0},{2,3},{3,2},{4,5},{5,4},{6,7},{7,6},{8,9},{9,8},{10,11... | collective-permute-start | bytes 1572872 | tf_op jit(solution)/shard_map/ppermute | solution.py:33
  104.1 3.4 %copy-start.1 = (bf16[512,8192]{1,0:T(8,128)(2,1)S(1)}, bf16[512,8192]{1,0:T(8,128)(2,1)}, u32[]{:S(2)}) copy-start(bf16[512,8192]{1,0:T(8,128)(2,1)} %wa_ref.15) | copy-start | bytes 25165828
  110.1 14.5 %collective-permute-start.15 = (bf16[256,1024]{1,0:T(8,128)(2,1)S(1)}, bf16[256,1024]{1,0:T(8,128)(2,1)S(1)}, u32[]{:S(2)}, u32[]{:S(2)}) collective-permute-start(bf16[256,1024]{1,0:T(8,128)(2,1)S(1)} %shard_map.105), channel_id=1, source_target_pairs={{0,2},{1,3},{2,4},{3,5},{4,6},{5,7},{6,0},{7,1},{8,10},{9,11},{10,... | collective-permute-start | bytes 1572872 | tf_op jit(solution)/shard_map/ppermute | solution.py:33
  112.7 14.5 %collective-permute-start.19 = (bf16[256,1024]{1,0:T(8,128)(2,1)S(1)}, bf16[256,1024]{1,0:T(8,128)(2,1)S(1)}, u32[]{:S(2)}, u32[]{:S(2)}) collective-permute-start(bf16[256,1024]{1,0:T(8,128)(2,1)S(1)} %shard_map.110), channel_id=1, source_target_pairs={{0,6},{1,7},{2,0},{3,1},{4,2},{5,3},{6,4},{7,5},{8,14},{9,15},{10,... | collective-permute-start | bytes 1572872 | tf_op jit(solution)/shard_map/ppermute | solution.py:33
  118.0 19.3 %collective-permute-start.17 = (bf16[256,1024]{1,0:T(8,128)(2,1)S(1)}, bf16[256,1024]{1,0:T(8,128)(2,1)S(1)}, u32[]{:S(2)}, u32[]{:S(2)}) collective-permute-start(bf16[256,1024]{1,0:T(8,128)(2,1)S(1)} %shard_map.107), channel_id=1, source_target_pairs={{0,6},{1,7},{2,0},{3,1},{4,2},{5,3},{6,4},{7,5},{8,14},{9,15},{10,... | collective-permute-start | bytes 1572872 | tf_op jit(solution)/shard_map/ppermute | solution.py:33
  120.9 27.9 %collective-permute-start.18 = (bf16[256,1024]{1,0:T(8,128)(2,1)S(1)}, bf16[256,1024]{1,0:T(8,128)(2,1)S(1)}, u32[]{:S(2)}, u32[]{:S(2)}) collective-permute-start(bf16[256,1024]{1,0:T(8,128)(2,1)S(1)} %shard_map.109), channel_id=1, source_target_pairs={{0,2},{1,3},{2,4},{3,5},{4,6},{5,7},{6,0},{7,1},{8,10},{9,11},{10,... | collective-permute-start | bytes 1572872 | tf_op jit(solution)/shard_map/ppermute | solution.py:33
  127.1 19.0 %collective-permute-start.16 = (bf16[256,1024]{1,0:T(8,128)(2,1)S(1)}, bf16[256,1024]{1,0:T(8,128)(2,1)S(1)}, u32[]{:S(2)}, u32[]{:S(2)}) collective-permute-start(bf16[256,1024]{1,0:T(8,128)(2,1)S(1)} %shard_map.106), channel_id=1, source_target_pairs={{0,2},{1,3},{2,4},{3,5},{4,6},{5,7},{6,0},{7,1},{8,10},{9,11},{10,... | collective-permute-start | bytes 1572872 | tf_op jit(solution)/shard_map/ppermute | solution.py:33
  129.8 19.0 %collective-permute-start.20 = (bf16[256,1024]{1,0:T(8,128)(2,1)S(1)}, bf16[256,1024]{1,0:T(8,128)(2,1)S(1)}, u32[]{:S(2)}, u32[]{:S(2)}) collective-permute-start(bf16[256,1024]{1,0:T(8,128)(2,1)S(1)} %shard_map.111), channel_id=1, source_target_pairs={{0,6},{1,7},{2,0},{3,1},{4,2},{5,3},{6,4},{7,5},{8,14},{9,15},{10,... | collective-permute-start | bytes 1572872 | tf_op jit(solution)/shard_map/ppermute | solution.py:33

commit v2 on v1

v2 whole, which is shorter than its diff:
```python
import functools
import math

import jax
import jax.numpy as jnp
import numpy as np
from jax import lax
from jax.experimental import pallas as pl
from jax.experimental.pallas import tpu as pltpu
from jax.sharding import PartitionSpec as P

QH = 32
KVH = 8
HD = 128
ROLL = 128
SEG_LEN = 256
DEPTH = 4
GROUP = QH // KVH
GRAN = 16

RING = 4


def y_shift(step):
    return [(y * 2 + c, ((y + step) % RING) * 2 + c) for y in range(RING) for c in range(2)]


SIBLING = [(h, h ^ 1) for h in range(2 * RING)]
UP = y_shift(1)
DOWN = y_shift(-1)


def send(x, pairs):
    return lax.ppermute(x, "head", pairs)


def params(mib):
    return pltpu.CompilerParams(vmem_limit_bytes=mib * 1024 * 1024)


def cost(flops, nbytes):
    return pl.CostEstimate(flops=int(flops), bytes_accessed=int(nbytes), transcendentals=0)


def index_table():
    rows = []
    for h in range(2 * RING):
        y, c = divmod(h, 2)
        row = []
        for other in (y, (y - 1) % RING, (y + 1) % RING, (y + 2) % RING):
            row += [2 * other + c, 2 * other + 1 - c]
        order = [(y + 2) % RING, (y + 1) % RING, (y - 1) % RING, y]
        row += [2 * t + c for t in order]
        rows.append(row)
    return np.asarray(rows, np.int32)


def ordered_kernel(*refs):
    pass


def ordered(xs, after):
    anywhere = pl.BlockSpec(memory_space=pl.ANY)
    return pl.pallas_call(
        ordered_kernel,
        in_specs=[anywhere] * (len(xs) + 1),
        out_specs=[anywhere] * len(xs),
        out_shape=[jax.ShapeDtypeStruct(x.shape, x.dtype) for x in xs],
        input_output_aliases={n: n for n in range(len(xs))},
        cost_estimate=cost(0, 0),
    )(*xs, after)


def spread_kernel(k_ref, v_ref, out_ref):
    out_ref[:, :, :GRAN, :] = pltpu.einshape("abcd->bacd", k_ref[...])
    out_ref[:, :, GRAN:, :] = pltpu.einshape("abcd->bacd", v_ref[...])


def spread(keys, values):
    segs = keys.shape[0] // SEG_LEN
    parts = SEG_LEN // GRAN
    step = 4
    view = (segs, parts, GRAN, HD)
    block = pl.BlockSpec((segs, step, GRAN, HD), lambda i: (0, i, 0, 0))
    return pl.pallas_call(
        spread_kernel,
        grid=(parts // step,),
        in_specs=[block, block],
        out_specs=pl.BlockSpec((step, segs, 2 * GRAN, HD), lambda i: (i, 0, 0, 0)),
        out_shape=jax.ShapeDtypeStruct((parts, segs, 2 * GRAN, HD), jnp.bfloat16),
        compiler_params=params(60),
        cost_estimate=cost(0, 4 * keys.size * 2),
    )(keys.reshape(view), values.reshape(view))


def pick_kernel(chain_ref, table_ref, *refs):
    out_ref = refs[-1]
    devices, slots = out_ref.shape[:2]
    first = pl.program_id(0) * devices

    def body(d, carry):
        for n in range(slots):
            out_ref[d, n] = table_ref[jnp.maximum(chain_ref[(first + d) * slots + n], 0)]
        return carry

    lax.fori_loop(0, devices, body, 0)


def pick(chain, table, devices, after):
    slots = chain.shape[0] // devices
    steps = 4
    block = (devices // steps, slots) + table.shape[1:]
    return pl.pallas_call(
        pick_kernel,
        grid_spec=pltpu.PrefetchScalarGridSpec(
            num_scalar_prefetch=1,
            grid=(steps,),
            in_specs=[pl.BlockSpec(table.shape, lambda i, s: (0, 0, 0))]
            + [pl.BlockSpec(memory_space=pl.ANY) for _ in after],
            out_specs=pl.BlockSpec(block, lambda i, s: (i, 0, 0, 0)),
        ),
        out_shape=jax.ShapeDtypeStruct((devices, slots) + table.shape[1:], jnp.bfloat16),
        compiler_params=params(60),
        cost_estimate=cost(0, 4 * table.size),
    )(chain, table, *after)


def exchange(x):
    return lax.all_to_all(x, "seq", 0, 0, tiled=True)


def project_kernel(plan, skip, has_acc, is_last, idx_ref, *refs):
    count = sum(len(pieces) for pieces in plan)
    xs = refs[:count]
    wq, wk, wv = refs[count : count + 3]
    rest = refs[count + 3 :]
    start = rest[0] if has_acc else None
    outs = rest[skip + has_acc :]
    acc = outs[-1]
    step = pl.program_id(0)
    nq = wq.shape[1]
    nk = wk.shape[1]
    at = 0
    for s, pieces in enumerate(plan):
        mine = xs[at : at + len(pieces)]
        at += len(pieces)

        @pl.when(step == s)
        def _():
            for (lo, hi), x in zip(pieces, mine):
                for w, c, n in ((wq, 0, nq), (wk, nq, nk), (wv, nq + nk, nk)):
                    d = jnp.dot(x[...], w[...], preferred_element_type=jnp.float32)
                    if s == 0 and has_acc:
                        acc[lo:hi, c : c + n] = start[lo:hi, c : c + n] + d
                    elif s == 0:
                        acc[lo:hi, c : c + n] = d
                    else:
                        acc[lo:hi, c : c + n] += d
            if is_last and s == len(plan) - 1:
                outs[0][...] = acc[:, :nq].astype(jnp.bfloat16)
                outs[1][...] = acc[:, nq : nq + nk].astype(jnp.bfloat16)
                outs[2][...] = acc[:, nq + nk :].astype(jnp.bfloat16)


def project(idx, first, rows, plan, xs, weights, after, start=None, is_last=False):
    depth = xs[0].shape[1]
    nq, nk = weights[0].shape[1], weights[1].shape[1]
    whole = lambda a: pl.BlockSpec(a.shape, lambda i, s: (0, 0))
    weight = lambda n: pl.BlockSpec((depth, n), lambda i, s: (s[first + i], 0))
    result = lambda n: pl.BlockSpec((rows, n), lambda i, s: (0, 0))
    total = nq + 2 * nk
    if is_last:
        out_specs = [result(n) for n in (nq, nk, nk)]
        out_shape = [jax.ShapeDtypeStruct((rows, n), jnp.bfloat16) for n in (nq, nk, nk)]
        scratch = [pltpu.VMEM((rows, total), jnp.float32)]
    else:
        out_specs = result(total)
        out_shape = jax.ShapeDtypeStruct((rows, total), jnp.float32)
        scratch = []
    extra = [] if start is None else [start]
    steps = len(plan)
    return pl.pallas_call(
        functools.partial(project_kernel, plan, len(after), start is not None, is_last),
        grid_spec=pltpu.PrefetchScalarGridSpec(
            num_scalar_prefetch=1,
            grid=(steps,),
            in_specs=[whole(a) for a in xs]
            + [weight(nq), weight(nk), weight(nk)]
            + [whole(a) for a in extra]
            + [pl.BlockSpec(memory_space=pl.ANY) for _ in after],
            out_specs=out_specs,
            scratch_shapes=scratch,
        ),
        out_shape=out_shape,
        compiler_params=params(48),
        cost_estimate=cost(2 * steps * rows * depth * total, 2 * steps * depth * (total + rows)),
    )(idx, *xs, *weights, *extra, *after)


def attend_kernel(first, rolls, chain_ref, len_ref, q_ref, k_ref, v_ref, far_ref, *refs):
    out_ref = refs[-1]
    base = (lax.axis_index("seq") * rolls + first + pl.program_id(0)) * DEPTH
    scale = math.log2(math.e) / math.sqrt(HD)
    slot = lax.broadcasted_iota(jnp.int32, (1, SEG_LEN), 1)
    masks, keys, values = [], [], []
    for level in range(DEPTH):
        seg = chain_ref[base + level]
        live = jnp.where(seg >= 0, len_ref[jnp.maximum(seg, 0)], 0)
        masks.append(jnp.where(slot < live, 0.0, -jnp.inf))
        keys.append(far_ref[:, level, :GRAN, :].reshape(SEG_LEN, HD))
        values.append(far_ref[:, level, GRAN:, :].reshape(SEG_LEN, HD))
    mask = jnp.concatenate(masks, axis=1)
    keys = jnp.concatenate(keys, axis=0)
    values = jnp.concatenate(values, axis=0)
    row = lax.broadcasted_iota(jnp.int32, (ROLL, ROLL), 0)
    causal = jnp.where(row >= lax.broadcasted_iota(jnp.int32, (ROLL, ROLL), 1), 0.0, -jnp.inf)
    causal = jnp.concatenate([causal] * GROUP, axis=0)
    q = jnp.concatenate([q_ref[:, g * HD : (g + 1) * HD] for g in range(GROUP)], axis=0)
    nt = (((1,), (1,)), ((), ()))
    far = lax.dot_general(q, keys, nt, preferred_element_type=jnp.float32) + mask
    own = lax.dot_general(q, k_ref[...], nt, preferred_element_type=jnp.float32) + causal
    m = jnp.maximum(jnp.max(far, axis=1, keepdims=True), jnp.max(own, axis=1, keepdims=True))
    far = jnp.exp2((far - m) * scale)
    own = jnp.exp2((own - m) * scale)
    total = jnp.sum(far, axis=1, keepdims=True) + jnp.sum(own, axis=1, keepdims=True)
    mix = jnp.dot(far.astype(jnp.bfloat16), values, preferred_element_type=jnp.float32)
    mix += jnp.dot(own.astype(jnp.bfloat16), v_ref[...], preferred_element_type=jnp.float32)
    mix = (mix / total).astype(jnp.bfloat16)
    for g in range(GROUP):
        out_ref[:, g * HD : (g + 1) * HD] = mix[g * ROLL : (g + 1) * ROLL]


def attend(chain, lengths, q, k, v, far, part, parts, after):
    rolls = q.shape[0] // ROLL // parts
    row = lambda n: pl.BlockSpec((ROLL, n), lambda i, a, b: (part * rolls + i, 0))
    far_block = (far.shape[0], DEPTH, 2 * GRAN, HD)
    return pl.pallas_call(
        functools.partial(attend_kernel, part * rolls, parts * rolls),
        grid_spec=pltpu.PrefetchScalarGridSpec(
            num_scalar_prefetch=2,
            grid=(rolls,),
            in_specs=[
                row(GROUP * HD),
                row(HD),
                row(HD),
                pl.BlockSpec(far_block, lambda i, a, b: (0, i, 0, 0)),
            ]
            + [pl.BlockSpec(memory_space=pl.ANY) for _ in after],
            out_specs=pl.BlockSpec((ROLL, GROUP * HD), lambda i, a, b: (i, 0)),
        ),
        out_shape=jax.ShapeDtypeStruct((rolls * ROLL, GROUP * HD), jnp.bfloat16),
        compiler_params=params(48),
        cost_estimate=cost(
            4 * rolls * ROLL * GROUP * HD * (DEPTH * SEG_LEN + ROLL), 2 * (2 * q.size + far.size)
        ),
    )(chain, lengths, q, k, v, far, *after)


def terms_kernel(count, skip, outs, idx_ref, a_ref, b_ref, *refs):
    w_own, w_sib, results = refs[:count], refs[count : 2 * count], refs[2 * count + skip :]
    for k in range(count):
        acc = jnp.dot(a_ref[...], w_own[k][...], preferred_element_type=jnp.float32)
        acc += jnp.dot(b_ref[...], w_sib[k][...], preferred_element_type=jnp.float32)
        for (which, lo, hi, dtype), out_ref in zip(outs, results):
            if which == k:
                out_ref[...] = acc[lo:hi].astype(dtype)


def terms(idx, first, count, outs, after, own, sib, w_own, w_sib):
    rows, depth = own.shape
    width = w_own.shape[1] // (2 * RING)
    cut = 2
    tile = width // cut
    left = pl.BlockSpec((rows, depth), lambda j, s: (0, 0))
    weight = lambda k: pl.BlockSpec((depth, tile), lambda j, s: (0, s[8 + first + k] * cut + j))
    return pl.pallas_call(
        functools.partial(terms_kernel, count, len(after), outs),
        grid_spec=pltpu.PrefetchScalarGridSpec(
            num_scalar_prefetch=1,
            grid=(cut,),
            in_specs=[left, left]
            + [weight(k) for k in range(count)] * 2
            + [pl.BlockSpec(memory_space=pl.ANY) for _ in after],
            out_specs=[pl.BlockSpec((hi - lo, tile), lambda j, s: (0, j)) for _, lo, hi, _ in outs],
        ),
        out_shape=[jax.ShapeDtypeStruct((hi - lo, width), dtype) for _, lo, hi, dtype in outs],
        compiler_params=params(56),
        cost_estimate=cost(
            4 * count * rows * depth * width, 4 * count * depth * width + 4 * count * rows * width
        ),
    )(idx, own, sib, *([w_own] * count), *([w_sib] * count), *after)


def add_terms(x, *received):
    for r in received:
        x = x + r.astype(jnp.float32)
    return x.astype(jnp.bfloat16)


def summed(idx, own, sib, w_own, w_sib):
    rows = own.shape[0]
    half = rows // 2
    f32, b16 = jnp.float32, jnp.bfloat16
    args = (own, sib, w_own, w_sib)
    far_outs = ((0, 0, half, b16), (0, half, rows, b16))
    far_top, far_bottom = terms(idx, 0, 1, far_outs, [], *args)
    via_up = send(far_top, UP)
    via_down = send(far_bottom, DOWN)
    near_outs = ((0, 0, half, f32), (0, half, rows, b16), (1, 0, half, b16), (1, half, rows, f32))
    next_top, next_bottom, prev_top, prev_bottom = terms(idx, 1, 2, near_outs, [far_top], *args)
    low_bottom = send(next_bottom, UP)
    up_top = send(prev_top, DOWN)
    mine_outs = ((0, 0, half, f32), (0, half, rows, f32))
    mine_top, mine_bottom = terms(idx, 3, 1, mine_outs, [low_bottom, up_top], *args)
    low_top = send(add_terms(next_top, via_up), UP)
    up_bottom = send(add_terms(prev_bottom, via_down), DOWN)
    top = add_terms(mine_top, low_top, up_top)
    return jnp.concatenate([top, add_terms(mine_bottom, low_bottom, up_bottom)], axis=0)


def per_device(
    hidden, w_query, w_key, w_value, w_out, prefix_keys, prefix_values, seg_lengths, ancestors
):
    head = lax.axis_index("head")
    idx = lax.dynamic_index_in_dim(jnp.asarray(index_table()), head, 0, keepdims=False)
    chain = ancestors.reshape(-1)
    rows = hidden.shape[0]
    half = rows // 2
    devices = prefix_keys.shape[0] // SEG_LEN
    weights = (w_query, w_key, w_value)
    whole = ((0, rows),)
    split = ((0, half), (half, rows))

    low = send(hidden, UP)
    up = send(hidden, DOWN)
    sib = send(hidden, SIBLING)

    w_sib = send(w_out, SIBLING)

    segs = spread(prefix_keys, prefix_values)
    table = exchange(segs).reshape(-1, 2 * GRAN, HD)

    low_half, up_half = low[:half], up[half:]
    far = exchange(pick(chain, table, devices, [low_half, up_half]))

    near_blocks = [hidden, sib, low, send(low, SIBLING), up, send(up, SIBLING)]
    acc = project(idx, 0, rows, (whole,) * 6, near_blocks, weights, [])

    far_top, far_bottom = ordered([send(low_half, UP), send(up_half, DOWN)], acc)
    far_blocks = [far_top, far_bottom, send(far_top, SIBLING), send(far_bottom, SIBLING)]
    q, k, v = project(idx, 6, rows, (split,) * 2, far_blocks, weights, [], acc, True)

    own = attend(chain, seg_lengths, q, k, v, far, 0, 1, [])
    return summed(idx, own, send(own, SIBLING), w_out, w_sib)


def solution(mesh):
    in_specs = (
        P("seq", "head"),
        P(None, "head"),
        P(None, "head"),
        P(None, "head"),
        P("head", None),
        P("seq", "head"),
        P("seq", "head"),
        P(),
        P(),
    )
    out_specs = P("seq", "head")
    return jax.shard_map(
        per_device, mesh=mesh, in_specs=in_specs, out_specs=out_specs, check_vma=False
    )
```

time: 154 us -> 146 us (0.948)
  local copies, waits for them, and re-layouts: 15 us -> 8.81 us
  other arithmetic: 1.04 us -> 4.41 us
  starting transfers between devices: 36.5 us -> 33.7 us
    unnamed x27 -> x33, local copies, waits for them, and re-layouts: 13.3 us -> 5.75 us
    pallas_call x11 -> x7, Pallas kernels: 46.1 us -> 39.6 us  [the longest x2 16.9 us: project(): pl.pallas_call(functools.partial(project_kernel, plan, len(after), start...]
    ppermute x21 -> x17, waiting for transfers between devices: 48.8 us -> 43.3 us  [send(): return lax.ppermute(x, 'head', pairs)]
    all_to_all x2, waiting for transfers between devices: 2.06 us -> 7.15 us  [exchange(): return lax.all_to_all(x, 'seq', 0, 0, tiled=True)]
    pallas_call x1, Pallas kernels: 0.37 us -> 3.77 us  [spread(): pl.pallas_call(spread_kernel, grid=(parts // step,), in_specs=[block, blo...]
    convert_element_type x0 -> x4, other arithmetic: none -> 3.37 us  [add_terms(): return x.astype(jnp.bfloat16)]
    ppermute x21 -> x17, starting transfers between devices: 23.1 us -> 20.4 us  [send(): return lax.ppermute(x, 'head', pairs)]
    pallas_call x1, Pallas kernels: 2.44 us -> 4.31 us  [pick(): pl.pallas_call(pick_kernel, grid_spec=pltpu.PrefetchScalarGridSpec(num_sc...]
  transfers between devices with their start and end apart: 23 -> 19, of which waited for: 10 -> 11; matrix products, arithmetic and copies ran while one was open for 1% -> 4% of each run, Pallas kernels for 28% -> 30%
where the time goes in v2:
time: 146 us; the launch traced here: 145 us
  waiting for transfers between devices  50.5 us (35%)
  Pallas kernels  47.7 us (33%)
  starting transfers between devices  33.7 us (23%)
  local copies, waits for them, and re-layouts  8.81 us (6%)
  other arithmetic  4.41 us (3%)
    ppermute x17, waiting for transfers between devices, send(): return lax.ppermute(x, 'head', pairs)  43.3 us
    ppermute x17, starting transfers between devices, send(): return lax.ppermute(x, 'head', pairs)  20.4 us
    pallas_call x2, Pallas kernels, project(): pl.pallas_call(functools.partial(project_kernel, plan, len(after), start...  16.9 us
    pallas_call x3, Pallas kernels, terms(): pl.pallas_call(functools.partial(terms_kernel, count, len(after), outs),...  15.1 us
    all_to_all x2, starting transfers between devices, exchange(): return lax.all_to_all(x, 'seq', 0, 0, tiled=True)  13.3 us
    pallas_call x1, Pallas kernels, attend(): pl.pallas_call(functools.partial(attend_kernel, part * rolls, parts * rol...  7.59 us
    all_to_all x2, waiting for transfers between devices, exchange(): return lax.all_to_all(x, 'seq', 0, 0, tiled=True)  7.15 us
    unnamed x33, local copies, waits for them, and re-layouts  5.75 us
  transfers between devices with their start and end apart: 19, of which 11 were waited for; matrix products, arithmetic and copies ran while one was open for 4% of the time, Pallas kernels for 30%

profile of v2, /device:TPU:1, one launch (start us, length us, event | category | flops | bytes accessed | tf_op | source)
XLA Modules:
  0.0 145.2 jit_solution(11064075917839532825)
XLA Ops:
  0.0 1.4 collective-permute-start.10
  1.4 3.8 %shard_map.103 = bf16[16,16,32,128]{3,2,1,0:T(8,128)(2,1)} custom-call(bf16[16,16,16,128]{3,2,1,0:T(8,128)(2,1)} %bitcast.5, bf16[16,16,16,128]{3,2,1,0:T(8,128)(2,1)} %bitcast.6), custom_call_target="tpu_custom_call" | custom-call | bytes 4194304 | tf_op jit(solution)/shard_map/pallas_call | solution.py:85
  5.2 7.9 %all-to-all-start = ((bf16[16,16,32,128]{3,2,1,0:T(8,128)(2,1)}), bf16[16,16,32,128]{3,2,1,0:T(8,128)(2,1)}, u32[]{:S(2)}, u32[]{:S(2)}) async-start(bf16[16,16,32,128]{3,2,1,0:T(8,128)(2,1)} %shard_map.103), calls=%async_computation | async-start | bytes 4194304 | tf_op jit(solution)/shard_map/all_to_all | solution.py:129
  13.1 2.8 %collective-permute-start.2 = (bf16[512,1024]{1,0:T(8,128)(2,1)}, bf16[512,1024]{1,0:T(8,128)(2,1)S(1)}, u32[]{:S(2)}, u32[]{:S(2)}) collective-permute-start(bf16[512,1024]{1,0:T(8,128)(2,1)} %refs_0_.4), channel_id=1, source_target_pairs={{0,6},{1,7},{2,0},{3,1},{4,2},{5,3},{6,4},{7,5},{8,14},{9,15},{10,... | collective-permute-start | bytes 3145736 | tf_op jit(solution)/shard_map/ppermute | solution.py:34
  15.9 0.6 collective-permute-start.4
  16.5 22.0 %collective-permute-done.2.refs_4_ = bf16[512,1024]{1,0:T(8,128)(2,1)S(1)} collective-permute-done((bf16[512,1024]{1,0:T(8,128)(2,1)}, bf16[512,1024]{1,0:T(8,128)(2,1)S(1)}, u32[]{:S(2)}, u32[]{:S(2)}) %collective-permute-start.2) | collective-permute-done | bytes 1048608 | tf_op jit(solution)/shard_map/ppermute | solution.py:34
  38.5 1.1 collective-permute-start.6
  39.6 1.9 %collective-permute-done.refs_2_ = bf16[512,1024]{1,0:T(8,128)(2,1)S(1)} collective-permute-done((bf16[512,1024]{1,0:T(8,128)(2,1)}, bf16[512,1024]{1,0:T(8,128)(2,1)S(1)}, u32[]{:S(2)}, u32[]{:S(2)}) %collective-permute-start) | collective-permute-done | bytes 1048608 | tf_op jit(solution)/shard_map/ppermute | solution.py:34
  41.4 1.4 collective-permute-start.5
  43.0 0.7 reshape.12.chain_ref
  43.7 0.9 slice.9.refs_1_
  44.5 0.8 slice.8.refs_0_
  45.3 1.2 all-to-all-done
  46.5 4.3 %shard_map.104 = bf16[16,16,32,128]{3,2,1,0:T(8,128)(2,1)} custom-call(s32[256]{0:T(256)} %reshape.12.chain_ref, bf16[256,32,128]{2,1,0:T(8,128)(2,1)} %bitcast.3.table_ref, bf16[256,1024]{1,0:T(8,128)(2,1)} %slice.8.refs_0_, bf16[256,1024]{1,0:T(8,128)(2,1)} %slice.9.refs_1_), custom_call_target="tpu_custom_call" | custom-call | bytes 4194304 | tf_op jit(solution)/shard_map/pallas_call | solution.py:113
  50.8 5.4 %all-to-all-start.1 = ((bf16[16,16,32,128]{3,2,1,0:T(8,128)(2,1)}), bf16[16,16,32,128]{3,2,1,0:T(8,128)(2,1)}, u32[]{:S(2)}, u32[]{:S(2)}) async-start(bf16[16,16,32,128]{3,2,1,0:T(8,128)(2,1)} %shard_map.104), calls=%async_computation.1 | async-start | bytes 4194304 | tf_op jit(solution)/shard_map/all_to_all | solution.py:129
  56.3 1.8 %collective-permute-start.3 = (bf16[256,1024]{1,0:T(8,128)(2,1)}, bf16[256,1024]{1,0:T(8,128)(2,1)S(1)}, u32[]{:S(2)}, u32[]{:S(2)}) collective-permute-start(bf16[256,1024]{1,0:T(8,128)(2,1)} %slice.9.refs_1_), channel_id=1, source_target_pairs={{0,6},{1,7},{2,0},{3,1},{4,2},{5,3},{6,4},{7,5},{8,14},{9,15},{10,... | collective-permute-start | bytes 1572872 | tf_op jit(solution)/shard_map/ppermute | solution.py:34
  58.1 0.7 dynamic-slice_bitcast_fusion.idx_ref
  58.8 12.4 %shard_map.100.refs_2_.refs_7_ = f32[512,768]{1,0:T(8,128)} custom-call(s32[12]{0:T(128)S(1)} %dynamic-slice_bitcast_fusion.idx_ref, bf16[512,1024]{1,0:T(8,128)(2,1)} %refs_0_.4, bf16[512,1024]{1,0:T(8,128)(2,1)} %collective-permute-done.4.refs_1_, bf16[512,1024]{1,0:T(8,128)(2,1)S(1)} %collective-permute-done.refs_2_, ...), custom_call_target="tpu_custom_call" | custom-call | flops 4831838208 | bytes 15728640 | tf_op jit(solution)/shard_map/pallas_call | solution.py:182
  71.2 0.4 collective-permute-done.1.refs_0_
  71.6 0.4 copy-done.2
  72.0 0.8 copy-done.4
  72.8 1.8 %collective-permute-start.7 = (bf16[256,1024]{1,0:T(8,128)(2,1)}, bf16[256,1024]{1,0:T(8,128)(2,1)S(1)}, u32[]{:S(2)}, u32[]{:S(2)}) collective-permute-start(bf16[256,1024]{1,0:T(8,128)(2,1)} %get-tuple-element.18.refs_0_), channel_id=1, source_target_pairs={{0,1},{1,0},{2,3},{3,2},{4,5},{5,4},{6,7},{7,6},{8,9},{9,8},{10,11... | collective-permute-start | bytes 1572872 | tf_op jit(solution)/shard_map/ppermute | solution.py:34
  74.6 1.7 %collective-permute-done.7.refs_2_ = bf16[256,1024]{1,0:T(8,128)(2,1)S(1)} collective-permute-done((bf16[256,1024]{1,0:T(8,128)(2,1)}, bf16[256,1024]{1,0:T(8,128)(2,1)S(1)}, u32[]{:S(2)}, u32[]{:S(2)}) %collective-permute-start.7) | collective-permute-done | bytes 524320 | tf_op jit(solution)/shard_map/ppermute | solution.py:34
  76.4 0.7 collective-permute-done.8.refs_3_
  77.1 1.0 copy-done.3
  78.2 1.0 copy-done.5
  79.2 4.5 %shard_map.102 = (bf16[512,512]{1,0:T(8,128)(2,1)S(1)}, bf16[512,128]{1,0:T(8,128)(2,1)S(1)}, bf16[512,128]{1,0:T(8,128)(2,1)S(1)}) custom-call(s32[12]{0:T(128)S(1)} %dynamic-slice_bitcast_fusion.idx_ref, bf16[256,1024]{1,0:T(8,128)(2,1)S(1)} %copy-done.5, bf16[256,1024]{1,0:T(8,128)(2,1)S(1)} %copy-done.3, ...), custom_call_target="tpu_custom_call" | custom-call | flops 1610612736 | bytes 5242880 | tf_op jit(solution)/shard_map/pallas_call | solution.py:182
  83.7 6.0 %all-to-all-done.1.far_ref = bf16[16,16,32,128]{3,2,1,0:T(8,128)(2,1)} async-done(((bf16[16,16,32,128]{3,2,1,0:T(8,128)(2,1)}), bf16[16,16,32,128]{3,2,1,0:T(8,128)(2,1)}, u32[]{:S(2)}, u32[]{:S(2)}) %all-to-all-start.1) | async-done | bytes 2097184 | tf_op jit(solution)/shard_map/all_to_all | solution.py:129
  89.7 7.6 %shard_map.105.a_ref = bf16[512,512]{1,0:T(8,128)(2,1)S(1)} custom-call(s32[256]{0:T(256)S(1)} %copy-done.7, s32[256]{0:T(256)S(1)} %copy-done.8, bf16[512,512]{1,0:T(8,128)(2,1)S(1)} %get-tuple-element.20.q_ref, bf16[512,128]{1,0:T(8,128)(2,1)S(1)} %get-tuple-element.21.k_ref, bf16[512,128]{1,0:T(8,128)(2,1)S(1)} %get-tuple-element.22.v_ref, ...), custom_call_target="tpu_custom_call" | custom-call | flops 1207959552 | bytes 3145728 | tf_op jit(solution)/shard_map/pallas_call | solution.py:237
  97.3 1.2 collective-permute-start.9
  98.5 1.5 %collective-permute-done.9.b_ref = bf16[512,512]{1,0:T(8,128)(2,1)S(1)} collective-permute-done((bf16[512,512]{1,0:T(8,128)(2,1)S(1)}, bf16[512,512]{1,0:T(8,128)(2,1)S(1)}, u32[]{:S(2)}, u32[]{:S(2)}) %collective-permute-start.9) | collective-permute-done | bytes 524320 | tf_op jit(solution)/shard_map/ppermute | solution.py:34
  100.1 0.8 copy-done.9
  100.9 4.4 %shard_map.106 = (bf16[256,1024]{1,0:T(8,128)(2,1)}, bf16[256,1024]{1,0:T(8,128)(2,1)}) custom-call(s32[12]{0:T(128)} %copy-done.6, bf16[512,512]{1,0:T(8,128)(2,1)} %copy-done.1, bf16[512,512]{1,0:T(8,128)(2,1)} %copy-done.9, bf16[512,8192]{1,0:T(8,128)(2,1)} %refs_0_.7, bf16[512,8192]{1,0:T(8,128)(2,1)} %collective-permute-done.10.refs_1_.refs_2_.refs_3_), custom_call_target="tpu_custom_call" | custom-call | flops 1073741824 | bytes 4194304 | tf_op jit(solution)/shard_map/pallas_call | solution.py:276
  105.3 2.7 %collective-permute-start.15 = (bf16[256,1024]{1,0:T(8,128)(2,1)}, bf16[256,1024]{1,0:T(8,128)(2,1)S(1)}, u32[]{:S(2)}, u32[]{:S(2)}) collective-permute-start(bf16[256,1024]{1,0:T(8,128)(2,1)} %get-tuple-element.30), channel_id=1, source_target_pairs={{0,6},{1,7},{2,0},{3,1},{4,2},{5,3},{6,4},{7,5},{8,14},{9,15},{10,... | collective-permute-start | bytes 1572872 | tf_op jit(solution)/shard_map/ppermute | solution.py:34
  108.0 6.1 %shard_map.107 = (f32[256,1024]{1,0:T(8,128)}, bf16[256,1024]{1,0:T(8,128)(2,1)}, bf16[256,1024]{1,0:T(8,128)(2,1)}, f32[256,1024]{1,0:T(8,128)}) custom-call(s32[12]{0:T(128)} %copy-done.6, bf16[512,512]{1,0:T(8,128)(2,1)} %copy-done.1, bf16[512,512]{1,0:T(8,128)(2,1)} %copy-done.9, bf16[512,8192]{1,0:T(8,128)(2,1)} %refs_0_.7, bf16[512,8192]{1,0:T(8,128)(2,1)} %refs_0_.7, ...), custom_call_target="tpu_custom_call" | custom-call | flops 2147483648 | bytes 8388608 | tf_op jit(solution)/shard_map/pallas_call | solution.py:276
  114.1 2.7 %collective-permute-start.12 = (bf16[256,1024]{1,0:T(8,128)(2,1)}, bf16[256,1024]{1,0:T(8,128)(2,1)S(1)}, u32[]{:S(2)}, u32[]{:S(2)}) collective-permute-start(bf16[256,1024]{1,0:T(8,128)(2,1)} %get-tuple-element.25), channel_id=1, source_target_pairs={{0,6},{1,7},{2,0},{3,1},{4,2},{5,3},{6,4},{7,5},{8,14},{9,15},{10,... | collective-permute-start | bytes 1572872 | tf_op jit(solution)/shard_map/ppermute | solution.py:34
  116.8 3.0 %collective-permute-done.13 = bf16[256,1024]{1,0:T(8,128)(2,1)S(1)} collective-permute-done((bf16[256,1024]{1,0:T(8,128)(2,1)}, bf16[256,1024]{1,0:T(8,128)(2,1)S(1)}, u32[]{:S(2)}, u32[]{:S(2)}) %collective-permute-start.13) | collective-permute-done | bytes 524320 | tf_op jit(solution)/shard_map/ppermute | solution.py:34
  119.8 1.4 add_convert_fusion.3
  121.3 0.1 add_convert_fusion.1
  121.4 2.7 %collective-permute-start.16 = (bf16[256,1024]{1,0:T(8,128)(2,1)S(1)}, bf16[256,1024]{1,0:T(8,128)(2,1)S(1)}, u32[]{:S(2)}, u32[]{:S(2)}) collective-permute-start(bf16[256,1024]{1,0:T(8,128)(2,1)S(1)} %add_convert_fusion.1), channel_id=1, source_target_pairs={{0,6},{1,7},{2,0},{3,1},{4,2},{5,3},{6,4},{7,5},{8,14},{9,15},{10,... | collective-permute-start | bytes 1572872 | tf_op jit(solution)/shard_map/ppermute | solution.py:34
  124.2 6.9 %collective-permute-done.11.refs_2_ = bf16[256,1024]{1,0:T(8,128)(2,1)S(1)} collective-permute-done((bf16[256,1024]{1,0:T(8,128)(2,1)}, bf16[256,1024]{1,0:T(8,128)(2,1)S(1)}, u32[]{:S(2)}, u32[]{:S(2)}) %collective-permute-start.11) | collective-permute-done | bytes 524320 | tf_op jit(solution)/shard_map/ppermute | solution.py:34
  131.1 0.8 copy-done.10
  131.8 0.8 copy-done.12
  132.6 4.6 %shard_map.108 = (f32[256,1024]{1,0:T(8,128)}, f32[256,1024]{1,0:T(8,128)}) custom-call(s32[12]{0:T(128)} %copy-done.6, bf16[512,512]{1,0:T(8,128)(2,1)} %copy-done.1, bf16[512,512]{1,0:T(8,128)(2,1)} %copy-done.9, bf16[512,8192]{1,0:T(8,128)(2,1)} %refs_0_.7, bf16[512,8192]{1,0:T(8,128)(2,1)} %collective-permute-done.10.refs_1_.refs_2_.refs_3_, ...), custom_call_target="tpu_custom_call" | custom-call | flops 1073741824 | bytes 4194304 | tf_op jit(solution)/shard_map/pallas_call | solution.py:276
  137.2 5.1 %collective-permute-done.14 = bf16[256,1024]{1,0:T(8,128)(2,1)S(1)} collective-permute-done((bf16[256,1024]{1,0:T(8,128)(2,1)S(1)}, bf16[256,1024]{1,0:T(8,128)(2,1)S(1)}, u32[]{:S(2)}, u32[]{:S(2)}) %collective-permute-start.14) | collective-permute-done | bytes 524320 | tf_op jit(solution)/shard_map/ppermute | solution.py:34
  142.3 1.6 %add_convert_fusion.2 = bf16[256,1024]{1,0:T(8,128)(2,1)S(1)} fusion(bf16[256,1024]{1,0:T(8,128)(2,1)} %copy-done.12, f32[256,1024]{1,0:T(8,128)} %get-tuple-element.26, bf16[256,1024]{1,0:T(8,128)(2,1)S(1)} %collective-permute-done.14), kind=kLoop, calls=%fused_computation.3 | loop fusion | flops 1310720 | bytes 2621440 | tf_op jit(solution)/shard_map/convert_element_type | solution.py:297
  144.0 0.2 add_convert_fusion
  144.2 1.0 pad_maximum_fusion
  (41 shorter events, 0.3 us)
Async XLA Ops:
  0.0 100.1 %collective-permute-start.10 = (bf16[512,8192]{1,0:T(8,128)(2,1)}, bf16[512,8192]{1,0:T(8,128)(2,1)}, u32[]{:S(2)}, u32[]{:S(2)}) collective-permute-start(bf16[512,8192]{1,0:T(8,128)(2,1)} %refs_0_.7), channel_id=1, source_target_pairs={{0,1},{1,0},{2,3},{3,2},{4,5},{5,4},{6,7},{7,6},{8,9},{9,8},{10,11... | collective-permute-start | bytes 25165832 | tf_op jit(solution)/shard_map/ppermute | solution.py:34
  5.2 37.7 %copy-start.15 = (s32[64,4]{0,1:T(4,128)S(1)}, s32[64,4]{0,1:T(4,128)}, u32[]{:S(2)}) copy-start(s32[64,4]{0,1:T(4,128)} %param.18) | copy-start | bytes 3076
  5.2 41.3 %all-to-all-start = ((bf16[16,16,32,128]{3,2,1,0:T(8,128)(2,1)}), bf16[16,16,32,128]{3,2,1,0:T(8,128)(2,1)}, u32[]{:S(2)}, u32[]{:S(2)}) async-start(bf16[16,16,32,128]{3,2,1,0:T(8,128)(2,1)} %shard_map.103), calls=%async_computation | async-start | bytes 4194304 | tf_op jit(solution)/shard_map/all_to_all | solution.py:129
  13.1 25.4 %collective-permute-start.2 = (bf16[512,1024]{1,0:T(8,128)(2,1)}, bf16[512,1024]{1,0:T(8,128)(2,1)S(1)}, u32[]{:S(2)}, u32[]{:S(2)}) collective-permute-start(bf16[512,1024]{1,0:T(8,128)(2,1)} %refs_0_.4), channel_id=1, source_target_pairs={{0,6},{1,7},{2,0},{3,1},{4,2},{5,3},{6,4},{7,5},{8,14},{9,15},{10,... | collective-permute-start | bytes 3145736 | tf_op jit(solution)/shard_map/ppermute | solution.py:34
  15.9 25.6 %collective-permute-start = (bf16[512,1024]{1,0:T(8,128)(2,1)}, bf16[512,1024]{1,0:T(8,128)(2,1)S(1)}, u32[]{:S(2)}, u32[]{:S(2)}) collective-permute-start(bf16[512,1024]{1,0:T(8,128)(2,1)} %refs_0_.4), channel_id=1, source_target_pairs={{0,2},{1,3},{2,4},{3,5},{4,6},{5,7},{6,0},{7,1},{8,10},{9,11},{10,... | collective-permute-start | bytes 3145736 | tf_op jit(solution)/shard_map/ppermute | solution.py:34
  15.9 42.2 %collective-permute-start.4 = (bf16[512,1024]{1,0:T(8,128)(2,1)}, bf16[512,1024]{1,0:T(8,128)(2,1)}, u32[]{:S(2)}, u32[]{:S(2)}) collective-permute-start(bf16[512,1024]{1,0:T(8,128)(2,1)} %refs_0_.4), channel_id=1, source_target_pairs={{0,1},{1,0},{2,3},{3,2},{4,5},{5,4},{6,7},{7,6},{8,9},{9,8},{10,11... | collective-permute-start | bytes 3145736 | tf_op jit(solution)/shard_map/ppermute | solution.py:34
  38.5 20.3 %collective-permute-start.6 = (bf16[512,1024]{1,0:T(8,128)(2,1)S(1)}, bf16[512,1024]{1,0:T(8,128)(2,1)}, u32[]{:S(2)}, u32[]{:S(2)}) collective-permute-start(bf16[512,1024]{1,0:T(8,128)(2,1)S(1)} %collective-permute-done.2.refs_4_), channel_id=1, source_target_pairs={{0,1},{1,0},{2,3},{3,2},{4,5},{5,4},{6,7},{7,6},{8,9},{9,8},{10,11... | collective-permute-start | bytes 3145736 | tf_op jit(solution)/shard_map/ppermute | solution.py:34
  41.4 17.3 %collective-permute-start.5 = (bf16[512,1024]{1,0:T(8,128)(2,1)S(1)}, bf16[512,1024]{1,0:T(8,128)(2,1)}, u32[]{:S(2)}, u32[]{:S(2)}) collective-permute-start(bf16[512,1024]{1,0:T(8,128)(2,1)S(1)} %collective-permute-done.refs_2_), channel_id=1, source_target_pairs={{0,1},{1,0},{2,3},{3,2},{4,5},{5,4},{6,7},{7,6},{8,9},{9,8},{10,11... | collective-permute-start | bytes 3145736 | tf_op jit(solution)/shard_map/ppermute | solution.py:34
  50.8 38.9 %all-to-all-start.1 = ((bf16[16,16,32,128]{3,2,1,0:T(8,128)(2,1)}), bf16[16,16,32,128]{3,2,1,0:T(8,128)(2,1)}, u32[]{:S(2)}, u32[]{:S(2)}) async-start(bf16[16,16,32,128]{3,2,1,0:T(8,128)(2,1)} %shard_map.104), calls=%async_computation.1 | async-start | bytes 4194304 | tf_op jit(solution)/shard_map/all_to_all | solution.py:129
  56.3 14.9 %collective-permute-start.3 = (bf16[256,1024]{1,0:T(8,128)(2,1)}, bf16[256,1024]{1,0:T(8,128)(2,1)S(1)}, u32[]{:S(2)}, u32[]{:S(2)}) collective-permute-start(bf16[256,1024]{1,0:T(8,128)(2,1)} %slice.9.refs_1_), channel_id=1, source_target_pairs={{0,6},{1,7},{2,0},{3,1},{4,2},{5,3},{6,4},{7,5},{8,14},{9,15},{10,... | collective-permute-start | bytes 1572872 | tf_op jit(solution)/shard_map/ppermute | solution.py:34
  58.1 13.6 %collective-permute-start.1 = (bf16[256,1024]{1,0:T(8,128)(2,1)}, bf16[256,1024]{1,0:T(8,128)(2,1)S(1)}, u32[]{:S(2)}, u32[]{:S(2)}) collective-permute-start(bf16[256,1024]{1,0:T(8,128)(2,1)} %slice.8.refs_0_), channel_id=1, source_target_pairs={{0,2},{1,3},{2,4},{3,5},{4,6},{5,7},{6,0},{7,1},{8,10},{9,11},{10,... | collective-permute-start | bytes 1572872 | tf_op jit(solution)/shard_map/ppermute | solution.py:34
  58.8 18.4 %copy-start.6 = (s32[12]{0:T(128)}, s32[12]{0:T(128)S(1)}, u32[]{:S(2)}) copy-start(s32[12]{0:T(128)S(1)} %dynamic-slice_bitcast_fusion.idx_ref) | copy-start | bytes 148
  71.2 6.0 %copy-start = (f32[512,768]{1,0:T(8,128)S(1)}, f32[512,768]{1,0:T(8,128)}, u32[]{:S(2)}) copy-start(f32[512,768]{1,0:T(8,128)} %shard_map.100.refs_2_.refs_7_) | copy-start | bytes 4718596
  71.2 0.8 copy-start.2
  72.0 0.8 copy-start.4
  72.8 3.6 %collective-permute-start.7 = (bf16[256,1024]{1,0:T(8,128)(2,1)}, bf16[256,1024]{1,0:T(8,128)(2,1)S(1)}, u32[]{:S(2)}, u32[]{:S(2)}) collective-permute-start(bf16[256,1024]{1,0:T(8,128)(2,1)} %get-tuple-element.18.refs_0_), channel_id=1, source_target_pairs={{0,1},{1,0},{2,3},{3,2},{4,5},{5,4},{6,7},{7,6},{8,9},{9,8},{10,11... | collective-permute-start | bytes 1572872 | tf_op jit(solution)/shard_map/ppermute | solution.py:34
  74.6 15.1 %copy-start.7 = (s32[256]{0:T(256)S(1)}, s32[256]{0:T(256)}, u32[]{:S(2)}) copy-start(s32[256]{0:T(256)} %reshape.12.chain_ref) | copy-start | bytes 3076
  74.6 2.5 %collective-permute-start.8 = (bf16[256,1024]{1,0:T(8,128)(2,1)}, bf16[256,1024]{1,0:T(8,128)(2,1)S(1)}, u32[]{:S(2)}, u32[]{:S(2)}) collective-permute-start(bf16[256,1024]{1,0:T(8,128)(2,1)} %get-tuple-element.19.refs_1_), channel_id=1, source_target_pairs={{0,1},{1,0},{2,3},{3,2},{4,5},{5,4},{6,7},{7,6},{8,9},{9,8},{10,11... | collective-permute-start | bytes 1572872 | tf_op jit(solution)/shard_map/ppermute | solution.py:34
  77.1 1.0 copy-start.3
  78.2 1.0 copy-start.5
  79.2 10.5 %copy-start.8 = (s32[256]{0:T(256)S(1)}, s32[256]{0:T(256)}, u32[]{:S(2)}) copy-start(s32[256]{0:T(256)} %len_ref.1) | copy-start | bytes 3076
  97.3 2.7 %copy-start.1 = (bf16[512,512]{1,0:T(8,128)(2,1)}, bf16[512,512]{1,0:T(8,128)(2,1)S(1)}, u32[]{:S(2)}) copy-start(bf16[512,512]{1,0:T(8,128)(2,1)S(1)} %shard_map.105.a_ref) | copy-start | bytes 1572868
  97.3 2.7 %collective-permute-start.9 = (bf16[512,512]{1,0:T(8,128)(2,1)S(1)}, bf16[512,512]{1,0:T(8,128)(2,1)S(1)}, u32[]{:S(2)}, u32[]{:S(2)}) collective-permute-start(bf16[512,512]{1,0:T(8,128)(2,1)S(1)} %shard_map.105.a_ref), channel_id=1, source_target_pairs={{0,1},{1,0},{2,3},{3,2},{4,5},{5,4},{6,7},{7,6},{8,9},{9,8},{10,11... | collective-permute-start | bytes 1572872 | tf_op jit(solution)/shard_map/ppermute | solution.py:34
  100.0 0.8 copy-start.9
  105.3 14.5 %collective-permute-start.13 = (bf16[256,1024]{1,0:T(8,128)(2,1)}, bf16[256,1024]{1,0:T(8,128)(2,1)S(1)}, u32[]{:S(2)}, u32[]{:S(2)}) collective-permute-start(bf16[256,1024]{1,0:T(8,128)(2,1)} %get-tuple-element.23.refs_4_), channel_id=1, source_target_pairs={{0,2},{1,3},{2,4},{3,5},{4,6},{5,7},{6,0},{7,1},{8,10},{9,11},{10,... | collective-permute-start | bytes 1572872 | tf_op jit(solution)/shard_map/ppermute | solution.py:34
  105.3 16.0 %collective-permute-start.15 = (bf16[256,1024]{1,0:T(8,128)(2,1)}, bf16[256,1024]{1,0:T(8,128)(2,1)S(1)}, u32[]{:S(2)}, u32[]{:S(2)}) collective-permute-start(bf16[256,1024]{1,0:T(8,128)(2,1)} %get-tuple-element.30), channel_id=1, source_target_pairs={{0,6},{1,7},{2,0},{3,1},{4,2},{5,3},{6,4},{7,5},{8,14},{9,15},{10,... | collective-permute-start | bytes 1572872 | tf_op jit(solution)/shard_map/ppermute | solution.py:34
  114.1 7.2 %copy-start.13 = (f32[256,1024]{1,0:T(8,128)S(1)}, f32[256,1024]{1,0:T(8,128)}, u32[]{:S(2)}) copy-start(f32[256,1024]{1,0:T(8,128)} %get-tuple-element.29) | copy-start | bytes 3145732
  114.1 17.0 %collective-permute-start.11 = (bf16[256,1024]{1,0:T(8,128)(2,1)}, bf16[256,1024]{1,0:T(8,128)(2,1)S(1)}, u32[]{:S(2)}, u32[]{:S(2)}) collective-permute-start(bf16[256,1024]{1,0:T(8,128)(2,1)} %get-tuple-element.24), channel_id=1, source_target_pairs={{0,2},{1,3},{2,4},{3,5},{4,6},{5,7},{6,0},{7,1},{8,10},{9,11},{10,... | collective-permute-start | bytes 1572872 | tf_op jit(solution)/shard_map/ppermute | solution.py:34
  114.1 16.9 %collective-permute-start.12 = (bf16[256,1024]{1,0:T(8,128)(2,1)}, bf16[256,1024]{1,0:T(8,128)(2,1)S(1)}, u32[]{:S(2)}, u32[]{:S(2)}) collective-permute-start(bf16[256,1024]{1,0:T(8,128)(2,1)} %get-tuple-element.25), channel_id=1, source_target_pairs={{0,6},{1,7},{2,0},{3,1},{4,2},{5,3},{6,4},{7,5},{8,14},{9,15},{10,... | collective-permute-start | bytes 1572872 | tf_op jit(solution)/shard_map/ppermute | solution.py:34
  121.2 21.1 %collective-permute-start.14 = (bf16[256,1024]{1,0:T(8,128)(2,1)S(1)}, bf16[256,1024]{1,0:T(8,128)(2,1)S(1)}, u32[]{:S(2)}, u32[]{:S(2)}) collective-permute-start(bf16[256,1024]{1,0:T(8,128)(2,1)S(1)} %add_convert_fusion.3), channel_id=1, source_target_pairs={{0,2},{1,3},{2,4},{3,5},{4,6},{5,7},{6,0},{7,1},{8,10},{9,11},{10,... | collective-permute-start | bytes 1572872 | tf_op jit(solution)/shard_map/ppermute | solution.py:34
  121.4 22.5 %collective-permute-start.16 = (bf16[256,1024]{1,0:T(8,128)(2,1)S(1)}, bf16[256,1024]{1,0:T(8,128)(2,1)S(1)}, u32[]{:S(2)}, u32[]{:S(2)}) collective-permute-start(bf16[256,1024]{1,0:T(8,128)(2,1)S(1)} %add_convert_fusion.1), channel_id=1, source_target_pairs={{0,6},{1,7},{2,0},{3,1},{4,2},{5,3},{6,4},{7,5},{8,14},{9,15},{10,... | collective-permute-start | bytes 1572872 | tf_op jit(solution)/shard_map/ppermute | solution.py:34
  131.1 0.8 copy-start.10
  131.8 0.8 copy-start.12
  137.2 6.7 %copy-start.11 = (bf16[256,1024]{1,0:T(8,128)(2,1)S(1)}, bf16[256,1024]{1,0:T(8,128)(2,1)}, u32[]{:S(2)}) copy-start(bf16[256,1024]{1,0:T(8,128)(2,1)} %copy-done.10) | copy-start | bytes 1572868
  137.2 6.7 %copy-start.14 = (f32[256,1024]{1,0:T(8,128)S(1)}, f32[256,1024]{1,0:T(8,128)}, u32[]{:S(2)}) copy-start(f32[256,1024]{1,0:T(8,128)} %get-tuple-element.28) | copy-start | bytes 3145732

commit v3 on v2

--- a/solution.py
+++ b/solution.py
@@ -71,58 +71,187 @@
     )(*xs, after)
 
 
-def spread_kernel(k_ref, v_ref, out_ref):
-    out_ref[:, :, :GRAN, :] = pltpu.einshape("abcd->bacd", k_ref[...])
-    out_ref[:, :, GRAN:, :] = pltpu.einshape("abcd->bacd", v_ref[...])
-
-
-def spread(keys, values):
+FIRST = 10
+SECOND = 13
+PARTS = SEG_LEN // GRAN
+BATCH = 8
+
+
+def table_kernel(chain_ref, len_ref, pack_ref, pick_ref, attend_ref, most_ref):
+    f32, b16 = jnp.float32, jnp.bfloat16
+    me = lax.axis_index("seq")
+    chain = chain_ref[...]
+    count = chain.shape[1]
+    segs = len_ref.shape[1]
+    iota = lambda shape, axis: lax.broadcasted_iota(jnp.int32, shape, axis)
+    exact = lambda x, y: jnp.dot(x.astype(b16), y, preferred_element_type=f32)
+    wants = jnp.where(iota((segs, count), 0) == chain, 1.0, 0.0).astype(b16)
+    uses = lax.dot_general(
+        jnp.ones((8, count), b16), wants, (((1,), (1,)), ((), ())), preferred_element_type=f32
+    )[:1]
+    lengths = len_ref[...].astype(f32)
+    pieces = jnp.floor((lengths + (GRAN - 1)) * (1.0 / GRAN))
+    live = exact(jnp.broadcast_to(lengths, (8, segs)), wants)
+    row, col = iota((segs, segs), 0), iota((segs, segs), 1)
+    earlier = jnp.where((row // PARTS == col // PARTS) & (row < col), 1.0, 0.0).astype(b16)
+    mine = iota((segs, 128), 1)
+    mine = jnp.where((iota((segs, 128), 0) == me * PARTS + mine) & (mine < PARTS), 1.0, 0.0)
+    mine = mine.astype(b16)
+
+    def number(level, held):
+        device = iota((PARTS, segs), 0).astype(f32)
+        piece = jnp.where(level % 2 == 1, (PARTS - 1) - device, device)
+        counts = jnp.where(piece < held, 1.0, 0.0)
+        before = exact(counts, earlier)
+        return before, jnp.max(before + counts).astype(jnp.int32)
+
+    def kept(x):
+        return jnp.sum(jnp.where(iota(x.shape, 0) == me, x, 0.0), axis=0, keepdims=True)
+
+    first, most_first = number(iota((1, segs), 1), jnp.where(uses > 0.0, pieces, 0.0))
+    slot_pieces = jnp.floor((live[:1] + (GRAN - 1)) * (1.0 / GRAN))
+    second, most_second = number(jnp.maximum(chain, 0), slot_pieces)
+    source = jnp.maximum(chain, 0) // PARTS
+    place = source * PARTS + kept(exact(first, wants)).astype(jnp.int32)
+    to = kept(second).astype(jnp.int32)
+    most = [jnp.full((1, segs), m, jnp.int32) for m in (most_first, most_second)]
+    pick_ref[...] = jnp.concatenate([place, to] + most + [to] * 4, axis=0)
+    pack_ref[:PARTS] = exact(first, mine).astype(jnp.int32)
+    pack_ref[PARTS:] = jnp.full((8, 128), most_first, jnp.int32)
+    attend_ref[:PARTS] = exact(second, mine).astype(jnp.int32)
+    attend_ref[PARTS:] = exact(live, mine).astype(jnp.int32)
+    most_ref[0] = most_first
+    most_ref[1] = most_second
+
+
+def number_pieces(chain, lengths):
+    vmem = pl.BlockSpec(memory_space=pltpu.VMEM)
+    own = jax.ShapeDtypeStruct((PARTS + 8, 128), jnp.int32)
+    return pl.pallas_call(
+        table_kernel,
+        out_specs=[vmem, vmem, vmem, pl.BlockSpec(memory_space=pltpu.SMEM)],
+        out_shape=[
+            own,
+            jax.ShapeDtypeStruct((8, chain.size), jnp.int32),
+            own,
+            jax.ShapeDtypeStruct((2,), jnp.int32),
+        ],
+        compiler_params=params(32),
+        cost_estimate=cost(0, 0),
+    )(chain.reshape(1, -1), lengths.reshape(1, -1))
+
+
+def pack_kernel(lo, hi, first_ref, k0_ref, k1_ref, v0_ref, v1_ref, out_ref):
+    pairs, _, step = k0_ref.shape[:3]
+    block = pl.program_id(0) * step
+
+    def piece_of(j, i):
+        odd = j % 2
+        piece = step - 1 - i if odd else i
+        return (k0_ref, k1_ref)[odd][j // 2, 0, piece], (v0_ref, v1_ref)[odd][j // 2, 0, piece]
+
+    def put(i, at, pair):
+        out_ref[i, at, :GRAN] = pair[0]
+        out_ref[i, at, GRAN:] = pair[1]
+
+    def guarded(i, carry):
+        for j in range(2 * pairs):
+            at = first_ref[block + i, j]
+            pl.when((at >= lo) & (at < hi))(lambda: put(i, at - lo, piece_of(j, i)))
+        return carry
+
+    def plain(i, carry):
+        for j0 in range(0, 2 * pairs, BATCH):
+            batch = range(j0, j0 + BATCH)
+            at = [first_ref[block + i, j] for j in batch]
+            for a, pair in zip(at, [piece_of(j, i) for j in batch]):
+                put(i, a, pair)
+        return carry
+
+    most = first_ref[PARTS, 0]
+    spare = (most < hi) if lo == 0 else (most < 0)
+    pl.when(spare)(lambda: lax.fori_loop(0, step, plain, None))
+    pl.when(jnp.logical_not(spare))(lambda: lax.fori_loop(0, step, guarded, None))
+
+
+def pack(lo, hi, first, keys, values):
     segs = keys.shape[0] // SEG_LEN
-    parts = SEG_LEN // GRAN
-    step = 4
-    view = (segs, parts, GRAN, HD)
-    block = pl.BlockSpec((segs, step, GRAN, HD), lambda i: (0, i, 0, 0))
-    return pl.pallas_call(
-        spread_kernel,
-        grid=(parts // step,),
-        in_specs=[block, block],
-        out_specs=pl.BlockSpec((step, segs, 2 * GRAN, HD), lambda i: (i, 0, 0, 0)),
-        out_shape=jax.ShapeDtypeStruct((parts, segs, 2 * GRAN, HD), jnp.bfloat16),
-        compiler_params=params(60),
-        cost_estimate=cost(0, 4 * keys.size * 2),
-    )(keys.reshape(view), values.reshape(view))
-
-
-def pick_kernel(chain_ref, table_ref, *refs):
-    out_ref = refs[-1]
-    devices, slots = out_ref.shape[:2]
-    first = pl.program_id(0) * devices
-
-    def body(d, carry):
-        for n in range(slots):
-            out_ref[d, n] = table_ref[jnp.maximum(chain_ref[(first + d) * slots + n], 0)]
-        return carry
-
-    lax.fori_loop(0, devices, body, 0)
-
-
-def pick(chain, table, devices, after):
-    slots = chain.shape[0] // devices
     steps = 4
-    block = (devices // steps, slots) + table.shape[1:]
-    return pl.pallas_call(
-        pick_kernel,
+    step = PARTS // steps
+    view = (segs // 2, 2, PARTS, GRAN, HD)
+    block = (segs // 2, 1, step, GRAN, HD)
+    even = pl.BlockSpec(block, lambda i, *s: (0, 0, i, 0, 0))
+    odd = pl.BlockSpec(block, lambda i, *s: (0, 1, steps - 1 - i, 0, 0))
+    shape = (PARTS, hi - lo, 2 * GRAN, HD)
+    keys, values = keys.reshape(view), values.reshape(view)
+    return pl.pallas_call(
+        functools.partial(pack_kernel, lo, hi),
         grid_spec=pltpu.PrefetchScalarGridSpec(
             num_scalar_prefetch=1,
             grid=(steps,),
-            in_specs=[pl.BlockSpec(table.shape, lambda i, s: (0, 0, 0))]
+            in_specs=[even, odd, even, odd],
+            out_specs=pl.BlockSpec((step,) + shape[1:], lambda i, *s: (i, 0, 0, 0)),
+        ),
+        out_shape=jax.ShapeDtypeStruct(shape, jnp.bfloat16),
+        compiler_params=params(60),
+        cost_estimate=cost(0, 4 * keys.size * 2),
+    )(first, keys, keys, values, values)
+
+
+def pick_kernel(lo, hi, split, slot_ref, *refs):
+    table_ref, out_ref = refs[0], refs[-1]
+    devices = out_ref.shape[0]
+    slots = slot_ref.shape[1] // PARTS
+    base = pl.program_id(0) * devices
+
+    def piece_of(place):
+        source, at = place // PARTS, place % PARTS
+        piece = table_ref[source, jnp.minimum(at, FIRST - 1)]
+        if split:
+            rest = refs[1][source, jnp.maximum(at - FIRST, 0)]
+            piece = jnp.where(at < FIRST, piece, rest)
+        return piece
+
+    def put(d, to, piece):
+        out_ref[d, to] = piece
+
+    def guarded(d, carry):
+        for n in range(slots):
+            slot = (base + d) * slots + n
+            to = slot_ref[1, slot]
+            pl.when((to >= lo) & (to < hi))(lambda: put(d, to - lo, piece_of(slot_ref[0, slot])))
+        return carry
+
+    def plain(d, carry):
+        for n0 in range(0, slots, BATCH):
+            batch = [(base + d) * slots + n for n in range(n0, n0 + BATCH)]
+            to = [slot_ref[1, slot] for slot in batch]
+            for t, piece in zip(to, [piece_of(slot_ref[0, slot]) for slot in batch]):
+                put(d, t, piece)
+        return carry
+
+    most = slot_ref[3, 0]
+    spare = (most < hi) if lo == 0 else (most < 0)
+    pl.when(spare)(lambda: lax.fori_loop(0, devices, plain, None))
+    pl.when(jnp.logical_not(spare))(lambda: lax.fori_loop(0, devices, guarded, None))
+
+
+def pick(lo, hi, slots, tables, after):
+    steps = 4
+    shape = (PARTS, hi - lo, 2 * GRAN, HD)
+    return pl.pallas_call(
+        functools.partial(pick_kernel, lo, hi, len(tables) > 1),
+        grid_spec=pltpu.PrefetchScalarGridSpec(
+            num_scalar_prefetch=1,
+            grid=(steps,),
+            in_specs=[pl.BlockSpec(t.shape, lambda i, *s: (0, 0, 0, 0)) for t in tables]
             + [pl.BlockSpec(memory_space=pl.ANY) for _ in after],
-            out_specs=pl.BlockSpec(block, lambda i, s: (i, 0, 0, 0)),
-        ),
-        out_shape=jax.ShapeDtypeStruct((devices, slots) + table.shape[1:], jnp.bfloat16),
+            out_specs=pl.BlockSpec((PARTS // steps,) + shape[1:], lambda i, *s: (i, 0, 0, 0)),
+        ),
+        out_shape=jax.ShapeDtypeStruct(shape, jnp.bfloat16),
         compiler_params=params(60),
-        cost_estimate=cost(0, 4 * table.size),
-    )(chain, table, *after)
+        cost_estimate=cost(0, 4 * tables[0].size),
+    )(slots, *tables, *after)
 
 
 def exchange(x):
@@ -197,63 +326,76 @@
     )(idx, *xs, *weights, *extra, *after)
 
 
-def attend_kernel(first, rolls, chain_ref, len_ref, q_ref, k_ref, v_ref, far_ref, *refs):
-    out_ref = refs[-1]
-    base = (lax.axis_index("seq") * rolls + first + pl.program_id(0)) * DEPTH
+HEADS = 2
+
+
+def attend_kernel(slot_ref, q_ref, k_ref, v_ref, *refs):
+    *tables, out_ref, keys, values = refs
+    roll = pl.program_id(0)
     scale = math.log2(math.e) / math.sqrt(HD)
     slot = lax.broadcasted_iota(jnp.int32, (1, SEG_LEN), 1)
-    masks, keys, values = [], [], []
+    masks = []
     for level in range(DEPTH):
-        seg = chain_ref[base + level]
-        live = jnp.where(seg >= 0, len_ref[jnp.maximum(seg, 0)], 0)
-        masks.append(jnp.where(slot < live, 0.0, -jnp.inf))
-        keys.append(far_ref[:, level, :GRAN, :].reshape(SEG_LEN, HD))
-        values.append(far_ref[:, level, GRAN:, :].reshape(SEG_LEN, HD))
+        at = roll * DEPTH + level
+        live = slot_ref[PARTS, at]
+        row = slot
+        if level % 2:
+            row = (PARTS - 1 - slot // GRAN) * GRAN + slot % GRAN
+        masks.append(jnp.where(row < live, 0.0, -jnp.inf))
+        pieces = []
+        for i in range(PARTS):
+            to = slot_ref[i, at]
+            piece = tables[0][i, jnp.minimum(to, SECOND - 1)]
+            if len(tables) > 1:
+                rest = tables[1][i, jnp.maximum(to - SECOND, 0)]
+                piece = jnp.where(to < SECOND, piece, rest)
+            pieces.append(piece)
+        lo = level * SEG_LEN
+        keys[lo : lo + SEG_LEN] = jnp.concatenate([p[:GRAN] for p in pieces], axis=0)
+        values[lo : lo + SEG_LEN] = jnp.concatenate([p[GRAN:] for p in pieces], axis=0)
     mask = jnp.concatenate(masks, axis=1)
-    keys = jnp.concatenate(keys, axis=0)
-    values = jnp.concatenate(values, axis=0)
     row = lax.broadcasted_iota(jnp.int32, (ROLL, ROLL), 0)
     causal = jnp.where(row >= lax.broadcasted_iota(jnp.int32, (ROLL, ROLL), 1), 0.0, -jnp.inf)
-    causal = jnp.concatenate([causal] * GROUP, axis=0)
-    q = jnp.concatenate([q_ref[:, g * HD : (g + 1) * HD] for g in range(GROUP)], axis=0)
+    causal = jnp.concatenate([causal] * HEADS, axis=0)
     nt = (((1,), (1,)), ((), ()))
-    far = lax.dot_general(q, keys, nt, preferred_element_type=jnp.float32) + mask
-    own = lax.dot_general(q, k_ref[...], nt, preferred_element_type=jnp.float32) + causal
-    m = jnp.maximum(jnp.max(far, axis=1, keepdims=True), jnp.max(own, axis=1, keepdims=True))
-    far = jnp.exp2((far - m) * scale)
-    own = jnp.exp2((own - m) * scale)
-    total = jnp.sum(far, axis=1, keepdims=True) + jnp.sum(own, axis=1, keepdims=True)
-    mix = jnp.dot(far.astype(jnp.bfloat16), values, preferred_element_type=jnp.float32)
-    mix += jnp.dot(own.astype(jnp.bfloat16), v_ref[...], preferred_element_type=jnp.float32)
-    mix = (mix / total).astype(jnp.bfloat16)
-    for g in range(GROUP):
-        out_ref[:, g * HD : (g + 1) * HD] = mix[g * ROLL : (g + 1) * ROLL]
-
-
-def attend(chain, lengths, q, k, v, far, part, parts, after):
-    rolls = q.shape[0] // ROLL // parts
-    row = lambda n: pl.BlockSpec((ROLL, n), lambda i, a, b: (part * rolls + i, 0))
-    far_block = (far.shape[0], DEPTH, 2 * GRAN, HD)
-    return pl.pallas_call(
-        functools.partial(attend_kernel, part * rolls, parts * rolls),
+    for g0 in range(0, GROUP, HEADS):
+        heads = range(g0, g0 + HEADS)
+        q = jnp.concatenate([q_ref[:, g * HD : (g + 1) * HD] for g in heads], axis=0)
+        far = lax.dot_general(q, keys[...], nt, preferred_element_type=jnp.float32) + mask
+        own = lax.dot_general(q, k_ref[...], nt, preferred_element_type=jnp.float32) + causal
+        m = jnp.maximum(jnp.max(far, axis=1, keepdims=True), jnp.max(own, axis=1, keepdims=True))
+        far = jnp.exp2((far - m) * scale)
+        own = jnp.exp2((own - m) * scale)
+        total = jnp.sum(far, axis=1, keepdims=True) + jnp.sum(own, axis=1, keepdims=True)
+        mix = jnp.dot(far.astype(jnp.bfloat16), values[...], preferred_element_type=jnp.float32)
+        mix += jnp.dot(own.astype(jnp.bfloat16), v_ref[...], preferred_element_type=jnp.float32)
+        mix = (mix / total).astype(jnp.bfloat16)
+        for n, g in enumerate(heads):
+            out_ref[:, g * HD : (g + 1) * HD] = mix[n * ROLL : (n + 1) * ROLL]
+
+
+def attend(slots, q, k, v, tables):
+    rolls = q.shape[0] // ROLL
+    row = lambda n: pl.BlockSpec((ROLL, n), lambda i, *s: (i, 0))
+    return pl.pallas_call(
+        attend_kernel,
         grid_spec=pltpu.PrefetchScalarGridSpec(
-            num_scalar_prefetch=2,
+            num_scalar_prefetch=1,
             grid=(rolls,),
-            in_specs=[
-                row(GROUP * HD),
-                row(HD),
-                row(HD),
-                pl.BlockSpec(far_block, lambda i, a, b: (0, i, 0, 0)),
-            ]
-            + [pl.BlockSpec(memory_space=pl.ANY) for _ in after],
-            out_specs=pl.BlockSpec((ROLL, GROUP * HD), lambda i, a, b: (i, 0)),
-        ),
-        out_shape=jax.ShapeDtypeStruct((rolls * ROLL, GROUP * HD), jnp.bfloat16),
+            in_specs=[row(GROUP * HD), row(HD), row(HD)]
+            + [pl.BlockSpec(t.shape, lambda i, *s: (0, 0, 0, 0)) for t in tables],
+            out_specs=row(GROUP * HD),
+            scratch_shapes=[
+                pltpu.VMEM((DEPTH * SEG_LEN, HD), jnp.bfloat16),
+                pltpu.VMEM((DEPTH * SEG_LEN, HD), jnp.bfloat16),
+            ],
+        ),
+        out_shape=jax.ShapeDtypeStruct(q.shape, jnp.bfloat16),
         compiler_params=params(48),
         cost_estimate=cost(
-            4 * rolls * ROLL * GROUP * HD * (DEPTH * SEG_LEN + ROLL), 2 * (2 * q.size + far.size)
-        ),
-    )(chain, lengths, q, k, v, far, *after)
+            4 * q.size * (DEPTH * SEG_LEN + ROLL), 4 * (q.size + tables[0].size)
+        ),
+    )(slots, q, k, v, *tables)
 
 
 def terms_kernel(count, skip, outs, idx_ref, a_ref, b_ref, *refs):
@@ -326,7 +468,6 @@
     chain = ancestors.reshape(-1)
     rows = hidden.shape[0]
     half = rows // 2
-    devices = prefix_keys.shape[0] // SEG_LEN
     weights = (w_query, w_key, w_value)
     whole = ((0, rows),)
     split = ((0, half), (half, rows))
@@ -337,20 +478,40 @@
 
     w_sib = send(w_out, SIBLING)
 
-    segs = spread(prefix_keys, prefix_values)
-    table = exchange(segs).reshape(-1, 2 * GRAN, HD)
-
+    for_pack, for_pick, for_attend, most = number_pieces(chain, seg_lengths)
+    table = exchange(pack(0, FIRST, for_pack, prefix_keys, prefix_values))
+
+    acc = project(idx, 0, rows, (whole,) * 2, [hidden, sib], weights, [low])
     low_half, up_half = low[:half], up[half:]
-    far = exchange(pick(chain, table, devices, [low_half, up_half]))
-
-    near_blocks = [hidden, sib, low, send(low, SIBLING), up, send(up, SIBLING)]
-    acc = project(idx, 0, rows, (whole,) * 6, near_blocks, weights, [])
+
+    def rest():
+        return exchange(pack(FIRST, PARTS, for_pack, prefix_keys, prefix_values))
+
+    def pick_all(lo, hi, tables):
+        return pick(lo, hi, for_pick, tables, [acc])
+
+    picked = lax.cond(
+        most[0] > FIRST,
+        lambda: pick_all(0, SECOND, [table, rest()]),
+        lambda: pick_all(0, SECOND, [table]),
+    )
+    far = exchange(picked)
+
+    near_blocks = [low, send(low, SIBLING), up, send(up, SIBLING)]
+    acc = project(idx, 2, rows, (whole,) * 4, near_blocks, weights, [], acc)
 
     far_top, far_bottom = ordered([send(low_half, UP), send(up_half, DOWN)], acc)
     far_blocks = [far_top, far_bottom, send(far_top, SIBLING), send(far_bottom, SIBLING)]
     q, k, v = project(idx, 6, rows, (split,) * 2, far_blocks, weights, [], acc, True)
 
-    own = attend(chain, seg_lengths, q, k, v, far, 0, 1, [])
+    def attend_rest():
+        far_rest = exchange(pick_all(SECOND, PARTS, [table, rest()]))
+        return attend(for_attend, q, k, v, [far, far_rest])
+
+    def attend_all():
+        return attend(for_attend, q, k, v, [far])
+
+    own = lax.cond(most[1] > SECOND, attend_rest, attend_all)
     return summed(idx, own, send(own, SIBLING), w_out, w_sib)
 
 

time: 146 us -> 139 us (0.952)
  waiting for transfers between devices: 50.5 us -> 33.3 us
  Pallas kernels: 47.7 us -> 55.7 us
  starting transfers between devices: 33.7 us -> 35.3 us
    ppermute x17, waiting for transfers between devices: 43.3 us -> 30.9 us  [send(): return lax.ppermute(x, 'head', pairs)]
    all_to_all x2, waiting for transfers between devices: 7.15 us -> 2.31 us  [exchange(): return lax.all_to_all(x, 'seq', 0, 0, tiled=True)]
    pallas_call x2 -> x3, Pallas kernels: 16.9 us -> 21.4 us  [project(): pl.pallas_call(functools.partial(project_kernel, plan, len(after), start...]
    pallas_call x3 -> x4, Pallas kernels: 15.7 us -> 19.6 us  [the longest x1 8.11 us: attend(): pl.pallas_call(attend_kernel, grid_spec=pltpu.PrefetchScalarGridSpec(num_...]
    all_to_all x2, starting transfers between devices: 13.3 us -> 15.6 us  [exchange(): return lax.all_to_all(x, 'seq', 0, 0, tiled=True)]
    unnamed x33 -> x27, local copies, waits for them, and re-layouts: 5.75 us -> 5.11 us
  transfers between devices with their start and end apart: 19 -> 19, of which waited for: 11 -> 11; matrix products, arithmetic and copies ran while one was open for 4% -> 5% of each run, Pallas kernels for 30% -> 37%
where the time goes in v3:
time: 139 us; the launch traced here: 138 us
  Pallas kernels  55.7 us (40%)
  starting transfers between devices  35.3 us (25%)
  waiting for transfers between devices  33.3 us (24%)
  local copies, waits for them, and re-layouts  7.66 us (6%)
  other arithmetic  4.41 us (3%)
  between operations  1.47 us (1%)
    ppermute x17, waiting for transfers between devices, send(): return lax.ppermute(x, 'head', pairs)  30.9 us
    pallas_call x3, Pallas kernels, project(): pl.pallas_call(functools.partial(project_kernel, plan, len(after), start...  21.4 us
    ppermute x17, starting transfers between devices, send(): return lax.ppermute(x, 'head', pairs)  19.7 us
    all_to_all x2, starting transfers between devices, exchange(): return lax.all_to_all(x, 'seq', 0, 0, tiled=True)  15.6 us
    pallas_call x3, Pallas kernels, terms(): pl.pallas_call(functools.partial(terms_kernel, count, len(after), outs),...  14.7 us
    pallas_call x1, Pallas kernels, attend(): pl.pallas_call(attend_kernel, grid_spec=pltpu.PrefetchScalarGridSpec(num_...  8.11 us
    pallas_call x1, Pallas kernels, pick(): pl.pallas_call(functools.partial(pick_kernel, lo, hi, len(tables) > 1), g...  5.78 us
    unnamed x27, local copies, waits for them, and re-layouts  5.11 us
  transfers between devices with their start and end apart: 19, of which 11 were waited for; matrix products, arithmetic and copies ran while one was open for 5% of the time, Pallas kernels for 37%

profile of v3, /device:TPU:1, one launch (start us, length us, event | category | flops | bytes accessed | tf_op | source)
XLA Modules:
  0.0 137.8 jit_solution(16127895372093928311)
XLA Ops:
  0.0 1.4 %collective-permute-start.10 = (bf16[512,8192]{1,0:T(8,128)(2,1)}, bf16[512,8192]{1,0:T(8,128)(2,1)}, u32[]{:S(2)}, u32[]{:S(2)}) collective-permute-start(bf16[512,8192]{1,0:T(8,128)(2,1)} %refs_0_.7), channel_id=1, source_target_pairs={{0,1},{1,0},{2,3},{3,2},{4,5},{5,4},{6,7},{7,6},{8,9},{9,8},{10,11... | collective-permute-start | bytes 25165832 | tf_op jit(solution)/shard_map/ppermute | solution.py:34
  1.4 2.8 %collective-permute-start.2 = (bf16[512,1024]{1,0:T(8,128)(2,1)}, bf16[512,1024]{1,0:T(8,128)(2,1)}, u32[]{:S(2)}, u32[]{:S(2)}) collective-permute-start(bf16[512,1024]{1,0:T(8,128)(2,1)} %refs_0_.4), channel_id=1, source_target_pairs={{0,6},{1,7},{2,0},{3,1},{4,2},{5,3},{6,4},{7,5},{8,14},{9,15},{10,... | collective-permute-start | bytes 3145736 | tf_op jit(solution)/shard_map/ppermute | solution.py:34
  4.2 0.8 copy.14
  5.1 0.7 copy-done.4
  5.8 1.0 shard_map.100
  6.8 4.7 %shard_map.105 = bf16[16,10,32,128]{3,2,1,0:T(8,128)(2,1)} custom-call(s32[24,128]{1,0:T(8,128)S(1)} %get-tuple-element.111.first_ref, bf16[8,2,16,16,128]{4,3,2,1,0:T(8,128)(2,1)} %bitcast.12, bf16[8,2,16,16,128]{4,3,2,1,0:T(8,128)(2,1)} %bitcast.13, bf16[8,2,16,16,128]{4,3,2,1,0:T(8,128)(2,1)} %bitcast.18, bf16[8,2,16,16,128]{4,3,2,1,0:T(8,128)(2,1)} %bitcast.19), custom_call_target="tpu_custom_call" | custom-call | bytes 4194304 | tf_op jit(solution)/shard_map/pallas_call | solution.py:187
  11.6 7.8 %all-to-all-start.3 = ((bf16[16,10,32,128]{3,2,1,0:T(8,128)(2,1)}), bf16[16,10,32,128]{3,2,1,0:T(8,128)(2,1)}, u32[]{:S(2)}, u32[]{:S(2)}) async-start(bf16[16,10,32,128]{3,2,1,0:T(8,128)(2,1)} %shard_map.105), calls=%async_computation.3 | async-start | bytes 2621440 | tf_op jit(solution)/shard_map/all_to_all | solution.py:258
  19.3 0.6 collective-permute-start.6
  20.0 7.2 %collective-permute-done.2.refs_2_ = bf16[512,1024]{1,0:T(8,128)(2,1)} collective-permute-done((bf16[512,1024]{1,0:T(8,128)(2,1)}, bf16[512,1024]{1,0:T(8,128)(2,1)}, u32[]{:S(2)}, u32[]{:S(2)}) %collective-permute-start.2) | collective-permute-done | bytes 1048608 | tf_op jit(solution)/shard_map/ppermute | solution.py:34
  27.1 0.8 collective-permute-start.5
  27.9 2.2 %collective-permute-done.refs_5_.refs_0_ = bf16[512,1024]{1,0:T(8,128)(2,1)S(1)} collective-permute-done((bf16[512,1024]{1,0:T(8,128)(2,1)}, bf16[512,1024]{1,0:T(8,128)(2,1)S(1)}, u32[]{:S(2)}, u32[]{:S(2)}) %collective-permute-start) | collective-permute-done | bytes 1048608 | tf_op jit(solution)/shard_map/ppermute | solution.py:34
  30.1 1.1 collective-permute-start.4
  31.2 0.6 fusion
  32.5 0.7 dynamic-slice_bitcast_fusion.idx_ref
  33.2 1.2 copy-done.2
  34.5 5.9 %shard_map.101.refs_7_ = f32[512,768]{1,0:T(8,128)} custom-call(s32[12]{0:T(128)S(1)} %dynamic-slice_bitcast_fusion.idx_ref, bf16[512,1024]{1,0:T(8,128)(2,1)S(1)} %copy-done.2, bf16[512,1024]{1,0:T(8,128)(2,1)} %collective-permute-done.6.refs_1_, bf16[8192,512]{1,0:T(8,128)(2,1)} %refs_4_.5, bf16[8192,128]{1,0:T(8,128)(2,1)S(1)} %copy-done, ...), custom_call_target="tpu_custom_call" | custom-call | flops 1610612736 | bytes 5242880 | tf_op jit(solution)/shard_map/pallas_call | solution.py:311
  40.4 5.8 %conditional.2 = (bf16[16,13,32,128]{3,2,1,0:T(8,128)(2,1)}) conditional(s32[]{:T(128)} %bitcast.7, (s32[8,256]{1,0:T(8,128)S(1)}, bf16[16,10,32,128]{3,2,1,0:T(8,128)(2,1)}, f32[512,768]{1,0:T(8,128)}) %tuple.17, (bf16[4096,128]{1,0:T(8,128)(2,1)}, bf16[4096,128]{1,0:T(8,128)(2,1)}, s32[24,128]{1,0:T(8,128)S(1)}, s32[8,256]{1,0:T(8,128)S(1)}, ...), branch_computations={%region_0.1_spmd, %region_1.2_spmd} | conditional | bytes 14680100 | solution.py:493
  40.4 5.8 %branch_0_fun.2 = bf16[16,13,32,128]{3,2,1,0:T(8,128)(2,1)} custom-call(s32[8,256]{1,0:T(8,128)S(1)} %get-tuple-element.60.slot_ref, bf16[16,10,32,128]{3,2,1,0:T(8,128)(2,1)} %get-tuple-element.62.refs_0_, f32[512,768]{1,0:T(8,128)} %get-tuple-element.63.refs_1_), custom_call_target="tpu_custom_call" | custom-call | bytes 2621440 | tf_op jit(solution)/shard_map/cond/branch_0_fun/pallas_call | solution.py:242
  46.2 7.8 %all-to-all-start.4 = ((bf16[16,13,32,128]{3,2,1,0:T(8,128)(2,1)}), bf16[16,13,32,128]{3,2,1,0:T(8,128)(2,1)}, u32[]{:S(2)}, u32[]{:S(2)}) async-start(bf16[16,13,32,128]{3,2,1,0:T(8,128)(2,1)} %get-tuple-element.122), calls=%async_computation.4 | async-start | bytes 3407872 | tf_op jit(solution)/shard_map/all_to_all | solution.py:258
  54.0 1.1 slice.17
  55.3 1.4 %collective-permute-start.1 = (bf16[256,1024]{1,0:T(8,128)(2,1)S(1)}, bf16[256,1024]{1,0:T(8,128)(2,1)}, u32[]{:S(2)}, u32[]{:S(2)}) collective-permute-start(bf16[256,1024]{1,0:T(8,128)(2,1)S(1)} %slice.16), channel_id=1, source_target_pairs={{0,2},{1,3},{2,4},{3,5},{4,6},{5,7},{6,0},{7,1},{8,10},{9,11},{10,... | collective-permute-start | bytes 1572872 | tf_op jit(solution)/shard_map/ppermute | solution.py:34
  56.7 9.4 %shard_map.102.refs_2_.refs_7_ = f32[512,768]{1,0:T(8,128)} custom-call(s32[12]{0:T(128)S(1)} %dynamic-slice_bitcast_fusion.idx_ref, bf16[512,1024]{1,0:T(8,128)(2,1)S(1)} %collective-permute-done.refs_5_.refs_0_, bf16[512,1024]{1,0:T(8,128)(2,1)} %collective-permute-done.4.refs_1_, bf16[512,1024]{1,0:T(8,128)(2,1)} %collective-permute-done.2.refs_2_, ...), custom_call_target="tpu_custom_call" | custom-call | flops 3221225472 | bytes 10485760 | tf_op jit(solution)/shard_map/pallas_call | solution.py:311
  66.1 2.4 %collective-permute-done.3.refs_1_ = bf16[256,1024]{1,0:T(8,128)(2,1)} collective-permute-done((bf16[256,1024]{1,0:T(8,128)(2,1)S(1)}, bf16[256,1024]{1,0:T(8,128)(2,1)}, u32[]{:S(2)}, u32[]{:S(2)}) %collective-permute-start.3) | collective-permute-done | bytes 524320 | tf_op jit(solution)/shard_map/ppermute | solution.py:34
  68.5 0.5 collective-permute-done.1.refs_0_
  69.0 2.0 %collective-permute-start.7 = (bf16[256,1024]{1,0:T(8,128)(2,1)}, bf16[256,1024]{1,0:T(8,128)(2,1)S(1)}, u32[]{:S(2)}, u32[]{:S(2)}) collective-permute-start(bf16[256,1024]{1,0:T(8,128)(2,1)} %get-tuple-element.105.refs_0_), channel_id=1, source_target_pairs={{0,1},{1,0},{2,3},{3,2},{4,5},{5,4},{6,7},{7,6},{8,9},{9,8},{10,11... | collective-permute-start | bytes 1572872 | tf_op jit(solution)/shard_map/ppermute | solution.py:34
  71.6 1.1 collective-permute-done.7.refs_2_
  72.7 0.7 collective-permute-done.8.refs_3_
  73.5 6.1 %shard_map.104 = (bf16[512,512]{1,0:T(8,128)(2,1)}, bf16[512,128]{1,0:T(8,128)(2,1)S(1)}, bf16[512,128]{1,0:T(8,128)(2,1)S(1)}) custom-call(s32[12]{0:T(128)S(1)} %dynamic-slice_bitcast_fusion.idx_ref, bf16[256,1024]{1,0:T(8,128)(2,1)} %get-tuple-element.105.refs_0_, bf16[256,1024]{1,0:T(8,128)(2,1)} %get-tuple-element.106.refs_1_, ...), custom_call_target="tpu_custom_call" | custom-call | flops 1610612736 | bytes 5242880 | tf_op jit(solution)/shard_map/pallas_call | solution.py:311
  79.6 2.3 %all-to-all-done.4 = bf16[16,13,32,128]{3,2,1,0:T(8,128)(2,1)} async-done(((bf16[16,13,32,128]{3,2,1,0:T(8,128)(2,1)}), bf16[16,13,32,128]{3,2,1,0:T(8,128)(2,1)}, u32[]{:S(2)}, u32[]{:S(2)}) %all-to-all-start.4) | async-done | bytes 1703968 | tf_op jit(solution)/shard_map/all_to_all | solution.py:258
  81.9 8.1 %conditional.3 = (bf16[512,512]{1,0:T(8,128)(2,1)S(1)}) conditional(s32[]{:T(128)} %bitcast.6, (s32[24,128]{1,0:T(8,128)S(1)}, bf16[512,512]{1,0:T(8,128)(2,1)}, bf16[512,128]{1,0:T(8,128)(2,1)S(1)}, bf16[512,128]{1,0:T(8,128)(2,1)S(1)}, bf16[16,13,32,128]{3,2,1,0:T(8,128)(2,1)}) %tuple.19, (bf16[4096,128]{1,0:T(8,128)(2,1)S(1)}, ...), branch_computations={%region_2.3_spmd, %region_3.4_spmd} | conditional | flops 1207959552 | bytes 22020160 | solution.py:514
  81.9 8.1 %branch_0_fun.3 = bf16[512,512]{1,0:T(8,128)(2,1)S(1)} custom-call(s32[24,128]{1,0:T(8,128)S(1)} %get-tuple-element.70.slot_ref, bf16[512,512]{1,0:T(8,128)(2,1)} %get-tuple-element.71.q_ref, bf16[512,128]{1,0:T(8,128)(2,1)S(1)} %get-tuple-element.72.k_ref, bf16[512,128]{1,0:T(8,128)(2,1)S(1)} %get-tuple-element.73.v_ref, ...), custom_call_target="tpu_custom_call" | custom-call | flops 1207959552 | bytes 4456448 | tf_op jit(solution)/shard_map/cond/branch_0_fun/pallas_call | solution.py:380
  90.0 1.2 collective-permute-start.9
  91.2 1.5 %collective-permute-done.9.b_ref = bf16[512,512]{1,0:T(8,128)(2,1)S(1)} collective-permute-done((bf16[512,512]{1,0:T(8,128)(2,1)S(1)}, bf16[512,512]{1,0:T(8,128)(2,1)S(1)}, u32[]{:S(2)}, u32[]{:S(2)}) %collective-permute-start.9) | collective-permute-done | bytes 524320 | tf_op jit(solution)/shard_map/ppermute | solution.py:34
  92.7 0.8 copy-done.9
  93.6 4.2 %shard_map.106 = (bf16[256,1024]{1,0:T(8,128)(2,1)}, bf16[256,1024]{1,0:T(8,128)(2,1)}) custom-call(s32[12]{0:T(128)} %copy-done.3, bf16[512,512]{1,0:T(8,128)(2,1)S(1)} %get-tuple-element.123.a_ref, bf16[512,512]{1,0:T(8,128)(2,1)} %copy-done.9, bf16[512,8192]{1,0:T(8,128)(2,1)} %refs_0_.7, bf16[512,8192]{1,0:T(8,128)(2,1)} %collective-permute-done.10.refs_1_.refs_2_.refs_3_), custom_call_target="tpu_custom_call" | custom-call | flops 1073741824 | bytes 4194304 | tf_op jit(solution)/shard_map/pallas_call | solution.py:418
  97.8 2.7 %collective-permute-start.15 = (bf16[256,1024]{1,0:T(8,128)(2,1)}, bf16[256,1024]{1,0:T(8,128)(2,1)S(1)}, u32[]{:S(2)}, u32[]{:S(2)}) collective-permute-start(bf16[256,1024]{1,0:T(8,128)(2,1)} %get-tuple-element.119), channel_id=1, source_target_pairs={{0,6},{1,7},{2,0},{3,1},{4,2},{5,3},{6,4},{7,5},{8,14},{9,15},{10,... | collective-permute-start | bytes 1572872 | tf_op jit(solution)/shard_map/ppermute | solution.py:34
  100.5 6.0 %shard_map.107 = (f32[256,1024]{1,0:T(8,128)}, bf16[256,1024]{1,0:T(8,128)(2,1)}, bf16[256,1024]{1,0:T(8,128)(2,1)}, f32[256,1024]{1,0:T(8,128)}) custom-call(s32[12]{0:T(128)} %copy-done.3, bf16[512,512]{1,0:T(8,128)(2,1)S(1)} %get-tuple-element.123.a_ref, bf16[512,512]{1,0:T(8,128)(2,1)} %copy-done.9, bf16[512,8192]{1,0:T(8,128)(2,1)} %refs_0_.7, ...), custom_call_target="tpu_custom_call" | custom-call | flops 2147483648 | bytes 8388608 | tf_op jit(solution)/shard_map/pallas_call | solution.py:418
  106.5 2.7 %collective-permute-start.12 = (bf16[256,1024]{1,0:T(8,128)(2,1)}, bf16[256,1024]{1,0:T(8,128)(2,1)S(1)}, u32[]{:S(2)}, u32[]{:S(2)}) collective-permute-start(bf16[256,1024]{1,0:T(8,128)(2,1)} %get-tuple-element.114), channel_id=1, source_target_pairs={{0,6},{1,7},{2,0},{3,1},{4,2},{5,3},{6,4},{7,5},{8,14},{9,15},{10,... | collective-permute-start | bytes 1572872 | tf_op jit(solution)/shard_map/ppermute | solution.py:34
  109.2 3.2 %collective-permute-done.13 = bf16[256,1024]{1,0:T(8,128)(2,1)S(1)} collective-permute-done((bf16[256,1024]{1,0:T(8,128)(2,1)}, bf16[256,1024]{1,0:T(8,128)(2,1)S(1)}, u32[]{:S(2)}, u32[]{:S(2)}) %collective-permute-start.13) | collective-permute-done | bytes 524320 | tf_op jit(solution)/shard_map/ppermute | solution.py:34
  112.4 1.4 add_convert_fusion.3
  114.0 2.7 %collective-permute-start.16 = (bf16[256,1024]{1,0:T(8,128)(2,1)S(1)}, bf16[256,1024]{1,0:T(8,128)(2,1)S(1)}, u32[]{:S(2)}, u32[]{:S(2)}) collective-permute-start(bf16[256,1024]{1,0:T(8,128)(2,1)S(1)} %add_convert_fusion.1), channel_id=1, source_target_pairs={{0,6},{1,7},{2,0},{3,1},{4,2},{5,3},{6,4},{7,5},{8,14},{9,15},{10,... | collective-permute-start | bytes 1572872 | tf_op jit(solution)/shard_map/ppermute | solution.py:34
  116.7 6.9 %collective-permute-done.11.refs_2_ = bf16[256,1024]{1,0:T(8,128)(2,1)S(1)} collective-permute-done((bf16[256,1024]{1,0:T(8,128)(2,1)}, bf16[256,1024]{1,0:T(8,128)(2,1)S(1)}, u32[]{:S(2)}, u32[]{:S(2)}) %collective-permute-start.11) | collective-permute-done | bytes 524320 | tf_op jit(solution)/shard_map/ppermute | solution.py:34
  123.6 0.8 copy-done.10
  124.4 0.8 copy-done.12
  125.2 4.4 %shard_map.108 = (f32[256,1024]{1,0:T(8,128)}, f32[256,1024]{1,0:T(8,128)}) custom-call(s32[12]{0:T(128)} %copy-done.3, bf16[512,512]{1,0:T(8,128)(2,1)S(1)} %get-tuple-element.123.a_ref, bf16[512,512]{1,0:T(8,128)(2,1)} %copy-done.9, bf16[512,8192]{1,0:T(8,128)(2,1)} %refs_0_.7, bf16[512,8192]{1,0:T(8,128)(2,1)} %collective-permute-done.10.refs_1_.refs_2_.refs_3_, ...), custom_call_target="tpu_custom_call" | custom-call | flops 1073741824 | bytes 4194304 | tf_op jit(solution)/shard_map/pallas_call | solution.py:418
  129.6 5.2 %collective-permute-done.14 = bf16[256,1024]{1,0:T(8,128)(2,1)S(1)} collective-permute-done((bf16[256,1024]{1,0:T(8,128)(2,1)S(1)}, bf16[256,1024]{1,0:T(8,128)(2,1)S(1)}, u32[]{:S(2)}, u32[]{:S(2)}) %collective-permute-start.14) | collective-permute-done | bytes 524320 | tf_op jit(solution)/shard_map/ppermute | solution.py:34
  134.8 1.6 %add_convert_fusion.2 = bf16[256,1024]{1,0:T(8,128)(2,1)S(1)} fusion(bf16[256,1024]{1,0:T(8,128)(2,1)} %copy-done.12, f32[256,1024]{1,0:T(8,128)} %get-tuple-element.115, bf16[256,1024]{1,0:T(8,128)(2,1)S(1)} %collective-permute-done.14), kind=kLoop, calls=%fused_computation.3 | loop fusion | flops 1310720 | bytes 2621440 | tf_op jit(solution)/shard_map/convert_element_type | solution.py:439
  136.7 1.0 pad_maximum_fusion
  (40 shorter events, 0.9 us)
Async XLA Ops:
  0.0 92.7 %collective-permute-start.10 = (bf16[512,8192]{1,0:T(8,128)(2,1)}, bf16[512,8192]{1,0:T(8,128)(2,1)}, u32[]{:S(2)}, u32[]{:S(2)}) collective-permute-start(bf16[512,8192]{1,0:T(8,128)(2,1)} %refs_0_.7), channel_id=1, source_target_pairs={{0,1},{1,0},{2,3},{3,2},{4,5},{5,4},{6,7},{7,6},{8,9},{9,8},{10,11... | collective-permute-start | bytes 25165832 | tf_op jit(solution)/shard_map/ppermute | solution.py:34
  1.4 25.7 %collective-permute-start.2 = (bf16[512,1024]{1,0:T(8,128)(2,1)}, bf16[512,1024]{1,0:T(8,128)(2,1)}, u32[]{:S(2)}, u32[]{:S(2)}) collective-permute-start(bf16[512,1024]{1,0:T(8,128)(2,1)} %refs_0_.4), channel_id=1, source_target_pairs={{0,6},{1,7},{2,0},{3,1},{4,2},{5,3},{6,4},{7,5},{8,14},{9,15},{10,... | collective-permute-start | bytes 3145736 | tf_op jit(solution)/shard_map/ppermute | solution.py:34
  4.2 25.9 %collective-permute-start = (bf16[512,1024]{1,0:T(8,128)(2,1)}, bf16[512,1024]{1,0:T(8,128)(2,1)S(1)}, u32[]{:S(2)}, u32[]{:S(2)}) collective-permute-start(bf16[512,1024]{1,0:T(8,128)(2,1)} %refs_0_.4), channel_id=1, source_target_pairs={{0,2},{1,3},{2,4},{3,5},{4,6},{5,7},{6,0},{7,1},{8,10},{9,11},{10,... | collective-permute-start | bytes 3145736 | tf_op jit(solution)/shard_map/ppermute | solution.py:34
  5.1 0.7 copy-start.4
  11.6 21.7 %copy-start = (bf16[8192,128]{1,0:T(8,128)(2,1)S(1)}, bf16[8192,128]{1,0:T(8,128)(2,1)}, u32[]{:S(2)}) copy-start(bf16[8192,128]{1,0:T(8,128)(2,1)} %refs_5_.3) | copy-start | bytes 6291460
  11.6 28.8 %all-to-all-start.3 = ((bf16[16,10,32,128]{3,2,1,0:T(8,128)(2,1)}), bf16[16,10,32,128]{3,2,1,0:T(8,128)(2,1)}, u32[]{:S(2)}, u32[]{:S(2)}) async-start(bf16[16,10,32,128]{3,2,1,0:T(8,128)(2,1)} %shard_map.105), calls=%async_computation.3 | async-start | bytes 2621440 | tf_op jit(solution)/shard_map/all_to_all | solution.py:258
  19.3 13.9 %collective-permute-start.6 = (bf16[512,1024]{1,0:T(8,128)(2,1)}, bf16[512,1024]{1,0:T(8,128)(2,1)}, u32[]{:S(2)}, u32[]{:S(2)}) collective-permute-start(bf16[512,1024]{1,0:T(8,128)(2,1)} %refs_0_.4), channel_id=1, source_target_pairs={{0,1},{1,0},{2,3},{3,2},{4,5},{5,4},{6,7},{7,6},{8,9},{9,8},{10,11... | collective-permute-start | bytes 3145736 | tf_op jit(solution)/shard_map/ppermute | solution.py:34
  27.1 29.5 %collective-permute-start.5 = (bf16[512,1024]{1,0:T(8,128)(2,1)}, bf16[512,1024]{1,0:T(8,128)(2,1)}, u32[]{:S(2)}, u32[]{:S(2)}) collective-permute-start(bf16[512,1024]{1,0:T(8,128)(2,1)} %collective-permute-done.2.refs_2_), channel_id=1, source_target_pairs={{0,1},{1,0},{2,3},{3,2},{4,5},{5,4},{6,7},{7,6},{8,9},{9,8},{10,11... | collective-permute-start | bytes 3145736 | tf_op jit(solution)/shard_map/ppermute | solution.py:34
  30.1 26.6 %collective-permute-start.4 = (bf16[512,1024]{1,0:T(8,128)(2,1)S(1)}, bf16[512,1024]{1,0:T(8,128)(2,1)}, u32[]{:S(2)}, u32[]{:S(2)}) collective-permute-start(bf16[512,1024]{1,0:T(8,128)(2,1)S(1)} %collective-permute-done.refs_5_.refs_0_), channel_id=1, source_target_pairs={{0,1},{1,0},{2,3},{3,2},{4,5},{5,4},{6,7},{7,6},{8,9},{9,8},{10,11... | collective-permute-start | bytes 3145736 | tf_op jit(solution)/shard_map/ppermute | solution.py:34
  33.2 40.3 %copy-start.3 = (s32[12]{0:T(128)}, s32[12]{0:T(128)S(1)}, u32[]{:S(2)}) copy-start(s32[12]{0:T(128)S(1)} %dynamic-slice_bitcast_fusion.idx_ref) | copy-start | bytes 148
  33.2 1.2 copy-start.2
  46.2 10.5 %copy-start.7 = (f32[512,768]{1,0:T(8,128)S(1)}, f32[512,768]{1,0:T(8,128)}, u32[]{:S(2)}) copy-start(f32[512,768]{1,0:T(8,128)} %shard_map.101.refs_7_) | copy-start | bytes 4718596
  46.2 35.7 %all-to-all-start.4 = ((bf16[16,13,32,128]{3,2,1,0:T(8,128)(2,1)}), bf16[16,13,32,128]{3,2,1,0:T(8,128)(2,1)}, u32[]{:S(2)}, u32[]{:S(2)}) async-start(bf16[16,13,32,128]{3,2,1,0:T(8,128)(2,1)} %get-tuple-element.122), calls=%async_computation.4 | async-start | bytes 3407872 | tf_op jit(solution)/shard_map/all_to_all | solution.py:258
  55.0 13.4 %collective-permute-start.3 = (bf16[256,1024]{1,0:T(8,128)(2,1)S(1)}, bf16[256,1024]{1,0:T(8,128)(2,1)}, u32[]{:S(2)}, u32[]{:S(2)}) collective-permute-start(bf16[256,1024]{1,0:T(8,128)(2,1)S(1)} %slice.17), channel_id=1, source_target_pairs={{0,6},{1,7},{2,0},{3,1},{4,2},{5,3},{6,4},{7,5},{8,14},{9,15},{10,... | collective-permute-start | bytes 1572872 | tf_op jit(solution)/shard_map/ppermute | solution.py:34
  55.3 13.7 %collective-permute-start.1 = (bf16[256,1024]{1,0:T(8,128)(2,1)S(1)}, bf16[256,1024]{1,0:T(8,128)(2,1)}, u32[]{:S(2)}, u32[]{:S(2)}) collective-permute-start(bf16[256,1024]{1,0:T(8,128)(2,1)S(1)} %slice.16), channel_id=1, source_target_pairs={{0,2},{1,3},{2,4},{3,5},{4,6},{5,7},{6,0},{7,1},{8,10},{9,11},{10,... | collective-permute-start | bytes 1572872 | tf_op jit(solution)/shard_map/ppermute | solution.py:34
  66.1 7.4 %copy-start.1 = (bf16[8192,128]{1,0:T(8,128)(2,1)S(1)}, bf16[8192,128]{1,0:T(8,128)(2,1)}, u32[]{:S(2)}) copy-start(bf16[8192,128]{1,0:T(8,128)(2,1)} %refs_5_.3) | copy-start | bytes 6291460
  69.0 3.7 %collective-permute-start.7 = (bf16[256,1024]{1,0:T(8,128)(2,1)}, bf16[256,1024]{1,0:T(8,128)(2,1)S(1)}, u32[]{:S(2)}, u32[]{:S(2)}) collective-permute-start(bf16[256,1024]{1,0:T(8,128)(2,1)} %get-tuple-element.105.refs_0_), channel_id=1, source_target_pairs={{0,1},{1,0},{2,3},{3,2},{4,5},{5,4},{6,7},{7,6},{8,9},{9,8},{10,11... | collective-permute-start | bytes 1572872 | tf_op jit(solution)/shard_map/ppermute | solution.py:34
  71.0 2.5 %collective-permute-start.8 = (bf16[256,1024]{1,0:T(8,128)(2,1)}, bf16[256,1024]{1,0:T(8,128)(2,1)S(1)}, u32[]{:S(2)}, u32[]{:S(2)}) collective-permute-start(bf16[256,1024]{1,0:T(8,128)(2,1)} %get-tuple-element.106.refs_1_), channel_id=1, source_target_pairs={{0,1},{1,0},{2,3},{3,2},{4,5},{5,4},{6,7},{7,6},{8,9},{9,8},{10,11... | collective-permute-start | bytes 1572872 | tf_op jit(solution)/shard_map/ppermute | solution.py:34
  71.6 10.3 %copy-start.5 = (bf16[4096,128]{1,0:T(8,128)(2,1)S(1)}, bf16[4096,128]{1,0:T(8,128)(2,1)}, u32[]{:S(2)}) copy-start(bf16[4096,128]{1,0:T(8,128)(2,1)} %param.19) | copy-start | bytes 3145732
  90.0 2.7 %collective-permute-start.9 = (bf16[512,512]{1,0:T(8,128)(2,1)S(1)}, bf16[512,512]{1,0:T(8,128)(2,1)S(1)}, u32[]{:S(2)}, u32[]{:S(2)}) collective-permute-start(bf16[512,512]{1,0:T(8,128)(2,1)S(1)} %get-tuple-element.123.a_ref), channel_id=1, source_target_pairs={{0,1},{1,0},{2,3},{3,2},{4,5},{5,4},{6,7},{7,6},{8,9},{9,8},{10,11... | collective-permute-start | bytes 1572872 | tf_op jit(solution)/shard_map/ppermute | solution.py:34
  92.7 0.8 copy-start.9
  97.8 14.6 %collective-permute-start.13 = (bf16[256,1024]{1,0:T(8,128)(2,1)}, bf16[256,1024]{1,0:T(8,128)(2,1)S(1)}, u32[]{:S(2)}, u32[]{:S(2)}) collective-permute-start(bf16[256,1024]{1,0:T(8,128)(2,1)} %get-tuple-element.112.refs_4_), channel_id=1, source_target_pairs={{0,2},{1,3},{2,4},{3,5},{4,6},{5,7},{6,0},{7,1},{8,10},{9,11},{10,... | collective-permute-start | bytes 1572872 | tf_op jit(solution)/shard_map/ppermute | solution.py:34
  97.8 16.0 %collective-permute-start.15 = (bf16[256,1024]{1,0:T(8,128)(2,1)}, bf16[256,1024]{1,0:T(8,128)(2,1)S(1)}, u32[]{:S(2)}, u32[]{:S(2)}) collective-permute-start(bf16[256,1024]{1,0:T(8,128)(2,1)} %get-tuple-element.119), channel_id=1, source_target_pairs={{0,6},{1,7},{2,0},{3,1},{4,2},{5,3},{6,4},{7,5},{8,14},{9,15},{10,... | collective-permute-start | bytes 1572872 | tf_op jit(solution)/shard_map/ppermute | solution.py:34
  106.4 7.4 %copy-start.13 = (f32[256,1024]{1,0:T(8,128)S(1)}, f32[256,1024]{1,0:T(8,128)}, u32[]{:S(2)}) copy-start(f32[256,1024]{1,0:T(8,128)} %get-tuple-element.118) | copy-start | bytes 3145732
  106.5 17.1 %collective-permute-start.11 = (bf16[256,1024]{1,0:T(8,128)(2,1)}, bf16[256,1024]{1,0:T(8,128)(2,1)S(1)}, u32[]{:S(2)}, u32[]{:S(2)}) collective-permute-start(bf16[256,1024]{1,0:T(8,128)(2,1)} %get-tuple-element.113), channel_id=1, source_target_pairs={{0,2},{1,3},{2,4},{3,5},{4,6},{5,7},{6,0},{7,1},{8,10},{9,11},{10,... | collective-permute-start | bytes 1572872 | tf_op jit(solution)/shard_map/ppermute | solution.py:34
  106.5 17.1 %collective-permute-start.12 = (bf16[256,1024]{1,0:T(8,128)(2,1)}, bf16[256,1024]{1,0:T(8,128)(2,1)S(1)}, u32[]{:S(2)}, u32[]{:S(2)}) collective-permute-start(bf16[256,1024]{1,0:T(8,128)(2,1)} %get-tuple-element.114), channel_id=1, source_target_pairs={{0,6},{1,7},{2,0},{3,1},{4,2},{5,3},{6,4},{7,5},{8,14},{9,15},{10,... | collective-permute-start | bytes 1572872 | tf_op jit(solution)/shard_map/ppermute | solution.py:34
  113.7 21.1 %collective-permute-start.14 = (bf16[256,1024]{1,0:T(8,128)(2,1)S(1)}, bf16[256,1024]{1,0:T(8,128)(2,1)S(1)}, u32[]{:S(2)}, u32[]{:S(2)}) collective-permute-start(bf16[256,1024]{1,0:T(8,128)(2,1)S(1)} %add_convert_fusion.3), channel_id=1, source_target_pairs={{0,2},{1,3},{2,4},{3,5},{4,6},{5,7},{6,0},{7,1},{8,10},{9,11},{10,... | collective-permute-start | bytes 1572872 | tf_op jit(solution)/shard_map/ppermute | solution.py:34
  114.0 22.5 %collective-permute-start.16 = (bf16[256,1024]{1,0:T(8,128)(2,1)S(1)}, bf16[256,1024]{1,0:T(8,128)(2,1)S(1)}, u32[]{:S(2)}, u32[]{:S(2)}) collective-permute-start(bf16[256,1024]{1,0:T(8,128)(2,1)S(1)} %add_convert_fusion.1), channel_id=1, source_target_pairs={{0,6},{1,7},{2,0},{3,1},{4,2},{5,3},{6,4},{7,5},{8,14},{9,15},{10,... | collective-permute-start | bytes 1572872 | tf_op jit(solution)/shard_map/ppermute | solution.py:34
  123.6 0.8 copy-start.10
  124.4 0.8 copy-start.12
  129.6 6.8 %copy-start.11 = (bf16[256,1024]{1,0:T(8,128)(2,1)S(1)}, bf16[256,1024]{1,0:T(8,128)(2,1)}, u32[]{:S(2)}) copy-start(bf16[256,1024]{1,0:T(8,128)(2,1)} %copy-done.10) | copy-start | bytes 1572868
  129.6 6.9 %copy-start.14 = (f32[256,1024]{1,0:T(8,128)S(1)}, f32[256,1024]{1,0:T(8,128)}, u32[]{:S(2)}) copy-start(f32[256,1024]{1,0:T(8,128)} %get-tuple-element.117) | copy-start | bytes 3145732

commit v4 on v3

--- a/solution.py
+++ b/solution.py
@@ -74,6 +74,7 @@
 FIRST = 10
 SECOND = 13
 PARTS = SEG_LEN // GRAN
+STEPS = 4
 BATCH = 8
 
 
@@ -115,7 +116,10 @@
     place = source * PARTS + kept(exact(first, wants)).astype(jnp.int32)
     to = kept(second).astype(jnp.int32)
     most = [jnp.full((1, segs), m, jnp.int32) for m in (most_first, most_second)]
-    pick_ref[...] = jnp.concatenate([place, to] + most + [to] * 4, axis=0)
+    at = place - source * PARTS
+    from_row = source * FIRST + jnp.minimum(at, FIRST - 1)
+    to_row = (iota((1, segs), 1) // PARTS) % (PARTS // STEPS) * SECOND + to
+    pick_ref[...] = jnp.concatenate([place, to] + most + [from_row, to_row] * 2, axis=0)
     pack_ref[:PARTS] = exact(first, mine).astype(jnp.int32)
     pack_ref[PARTS:] = jnp.full((8, 128), most_first, jnp.int32)
     attend_ref[:PARTS] = exact(second, mine).astype(jnp.int32)
@@ -160,18 +164,20 @@
             pl.when((at >= lo) & (at < hi))(lambda: put(i, at - lo, piece_of(j, i)))
         return carry
 
-    def plain(i, carry):
-        for j0 in range(0, 2 * pairs, BATCH):
-            batch = range(j0, j0 + BATCH)
-            at = [first_ref[block + i, j] for j in batch]
-            for a, pair in zip(at, [piece_of(j, i) for j in batch]):
-                put(i, a, pair)
-        return carry
+    def plain():
+        for i in range(step):
+            for j0 in range(0, 2 * pairs, BATCH):
+                batch = range(j0, j0 + BATCH)
+                at = [first_ref[block + i, j] for j in batch]
+                for a, pair in zip(at, [piece_of(j, i) for j in batch]):
+                    put(i, a, pair)
 
     most = first_ref[PARTS, 0]
-    spare = (most < hi) if lo == 0 else (most < 0)
-    pl.when(spare)(lambda: lax.fori_loop(0, step, plain, None))
-    pl.when(jnp.logical_not(spare))(lambda: lax.fori_loop(0, step, guarded, None))
+    if lo == 0:
+        pl.when(most < hi)(plain)
+        pl.when(most >= hi)(lambda: lax.fori_loop(0, step, guarded, None))
+    else:
+        lax.fori_loop(0, step, guarded, None)
 
 
 def pack(lo, hi, first, keys, values):
@@ -222,22 +228,25 @@
             pl.when((to >= lo) & (to < hi))(lambda: put(d, to - lo, piece_of(slot_ref[0, slot])))
         return carry
 
-    def plain(d, carry):
-        for n0 in range(0, slots, BATCH):
-            batch = [(base + d) * slots + n for n in range(n0, n0 + BATCH)]
-            to = [slot_ref[1, slot] for slot in batch]
-            for t, piece in zip(to, [piece_of(slot_ref[0, slot]) for slot in batch]):
-                put(d, t, piece)
-        return carry
+    def plain():
+        flat = table_ref.reshape(PARTS * FIRST, 2 * GRAN, HD)
+        out = out_ref.reshape(devices * (hi - lo), 2 * GRAN, HD)
+        for n0 in range(0, devices * slots, BATCH):
+            batch = [base * slots + n for n in range(n0, n0 + BATCH)]
+            pieces = [flat[slot_ref[4, slot]] for slot in batch]
+            for slot, piece in zip(batch, pieces):
+                out[slot_ref[5, slot]] = piece
 
     most = slot_ref[3, 0]
-    spare = (most < hi) if lo == 0 else (most < 0)
-    pl.when(spare)(lambda: lax.fori_loop(0, devices, plain, None))
-    pl.when(jnp.logical_not(spare))(lambda: lax.fori_loop(0, devices, guarded, None))
+    if lo == 0 and not split:
+        pl.when(most < hi)(plain)
+        pl.when(most >= hi)(lambda: lax.fori_loop(0, devices, guarded, None))
+    else:
+        lax.fori_loop(0, devices, guarded, None)
 
 
 def pick(lo, hi, slots, tables, after):
-    steps = 4
+    steps = STEPS
     shape = (PARTS, hi - lo, 2 * GRAN, HD)
     return pl.pallas_call(
         functools.partial(pick_kernel, lo, hi, len(tables) > 1),
@@ -291,7 +300,7 @@
                 outs[2][...] = acc[:, nq + nk :].astype(jnp.bfloat16)
 
 
-def project(idx, first, rows, plan, xs, weights, after, start=None, is_last=False):
+def project(idx, first, rows, plan, xs, weights, after, start=None, is_last=False, grant=48):
     depth = xs[0].shape[1]
     nq, nk = weights[0].shape[1], weights[1].shape[1]
     whole = lambda a: pl.BlockSpec(a.shape, lambda i, s: (0, 0))
@@ -321,11 +330,12 @@
             scratch_shapes=scratch,
         ),
         out_shape=out_shape,
-        compiler_params=params(48),
+        compiler_params=params(grant),
         cost_estimate=cost(2 * steps * rows * depth * total, 2 * steps * depth * (total + rows)),
     )(idx, *xs, *weights, *extra, *after)
 
 
+FAR = DEPTH * SEG_LEN
 HEADS = 2
 
 
@@ -358,18 +368,20 @@
     causal = jnp.where(row >= lax.broadcasted_iota(jnp.int32, (ROLL, ROLL), 1), 0.0, -jnp.inf)
     causal = jnp.concatenate([causal] * HEADS, axis=0)
     nt = (((1,), (1,)), ((), ()))
+    ones = jnp.ones((FAR, HD), jnp.bfloat16)
     for g0 in range(0, GROUP, HEADS):
         heads = range(g0, g0 + HEADS)
         q = jnp.concatenate([q_ref[:, g * HD : (g + 1) * HD] for g in heads], axis=0)
         far = lax.dot_general(q, keys[...], nt, preferred_element_type=jnp.float32) + mask
         own = lax.dot_general(q, k_ref[...], nt, preferred_element_type=jnp.float32) + causal
         m = jnp.maximum(jnp.max(far, axis=1, keepdims=True), jnp.max(own, axis=1, keepdims=True))
-        far = jnp.exp2((far - m) * scale)
-        own = jnp.exp2((own - m) * scale)
-        total = jnp.sum(far, axis=1, keepdims=True) + jnp.sum(own, axis=1, keepdims=True)
-        mix = jnp.dot(far.astype(jnp.bfloat16), values[...], preferred_element_type=jnp.float32)
-        mix += jnp.dot(own.astype(jnp.bfloat16), v_ref[...], preferred_element_type=jnp.float32)
-        mix = (mix / total).astype(jnp.bfloat16)
+        far = jnp.exp2((far - m) * scale).astype(jnp.bfloat16)
+        own = jnp.exp2((own - m) * scale).astype(jnp.bfloat16)
+        far_values = jnp.concatenate([values[...], ones], axis=1)
+        own_values = jnp.concatenate([v_ref[...], ones[:ROLL]], axis=1)
+        mix = jnp.dot(far, far_values, preferred_element_type=jnp.float32)
+        mix += jnp.dot(own, own_values, preferred_element_type=jnp.float32)
+        mix = (mix[:, :HD] / mix[:, HD:]).astype(jnp.bfloat16)
         for n, g in enumerate(heads):
             out_ref[:, g * HD : (g + 1) * HD] = mix[n * ROLL : (n + 1) * ROLL]
 
@@ -386,8 +398,8 @@
             + [pl.BlockSpec(t.shape, lambda i, *s: (0, 0, 0, 0)) for t in tables],
             out_specs=row(GROUP * HD),
             scratch_shapes=[
-                pltpu.VMEM((DEPTH * SEG_LEN, HD), jnp.bfloat16),
-                pltpu.VMEM((DEPTH * SEG_LEN, HD), jnp.bfloat16),
+                pltpu.VMEM((FAR, HD), jnp.bfloat16),
+                pltpu.VMEM((FAR, HD), jnp.bfloat16),
             ],
         ),
         out_shape=jax.ShapeDtypeStruct(q.shape, jnp.bfloat16),
@@ -398,17 +410,21 @@
     )(slots, q, k, v, *tables)
 
 
-def terms_kernel(count, skip, outs, idx_ref, a_ref, b_ref, *refs):
-    w_own, w_sib, results = refs[:count], refs[count : 2 * count], refs[2 * count + skip :]
+def terms_kernel(count, added, skip, outs, idx_ref, a_ref, b_ref, *refs):
+    w_own, w_sib, refs = refs[:count], refs[count : 2 * count], refs[2 * count :]
+    more, results = refs[:added], refs[added + skip :]
     for k in range(count):
         acc = jnp.dot(a_ref[...], w_own[k][...], preferred_element_type=jnp.float32)
         acc += jnp.dot(b_ref[...], w_sib[k][...], preferred_element_type=jnp.float32)
-        for (which, lo, hi, dtype), out_ref in zip(outs, results):
+        for n, ((which, lo, hi, dtype), out_ref) in enumerate(zip(outs, results)):
             if which == k:
-                out_ref[...] = acc[lo:hi].astype(dtype)
-
-
-def terms(idx, first, count, outs, after, own, sib, w_own, w_sib):
+                term = acc[lo:hi]
+                if added:
+                    term += more[n][...].astype(jnp.float32)
+                out_ref[...] = term.astype(dtype)
+
+
+def terms(idx, first, count, outs, added, after, own, sib, w_own, w_sib):
     rows, depth = own.shape
     width = w_own.shape[1] // (2 * RING)
     cut = 2
@@ -416,12 +432,13 @@
     left = pl.BlockSpec((rows, depth), lambda j, s: (0, 0))
     weight = lambda k: pl.BlockSpec((depth, tile), lambda j, s: (0, s[8 + first + k] * cut + j))
     return pl.pallas_call(
-        functools.partial(terms_kernel, count, len(after), outs),
+        functools.partial(terms_kernel, count, len(added), len(after), outs),
         grid_spec=pltpu.PrefetchScalarGridSpec(
             num_scalar_prefetch=1,
             grid=(cut,),
             in_specs=[left, left]
             + [weight(k) for k in range(count)] * 2
+            + [pl.BlockSpec((x.shape[0], tile), lambda j, s: (0, j)) for x in added]
             + [pl.BlockSpec(memory_space=pl.ANY) for _ in after],
             out_specs=[pl.BlockSpec((hi - lo, tile), lambda j, s: (0, j)) for _, lo, hi, _ in outs],
         ),
@@ -430,7 +447,7 @@
         cost_estimate=cost(
             4 * count * rows * depth * width, 4 * count * depth * width + 4 * count * rows * width
         ),
-    )(idx, own, sib, *([w_own] * count), *([w_sib] * count), *after)
+    )(idx, own, sib, *([w_own] * count), *([w_sib] * count), *added, *after)
 
 
 def add_terms(x, *received):
@@ -445,19 +462,19 @@
     f32, b16 = jnp.float32, jnp.bfloat16
     args = (own, sib, w_own, w_sib)
     far_outs = ((0, 0, half, b16), (0, half, rows, b16))
-    far_top, far_bottom = terms(idx, 0, 1, far_outs, [], *args)
+    far_top, far_bottom = terms(idx, 0, 1, far_outs, [], [], *args)
     via_up = send(far_top, UP)
     via_down = send(far_bottom, DOWN)
     near_outs = ((0, 0, half, f32), (0, half, rows, b16), (1, 0, half, b16), (1, half, rows, f32))
-    next_top, next_bottom, prev_top, prev_bottom = terms(idx, 1, 2, near_outs, [far_top], *args)
+    next_top, next_bottom, prev_top, prev_bottom = terms(idx, 1, 2, near_outs, [], [far_top], *args)
     low_bottom = send(next_bottom, UP)
     up_top = send(prev_top, DOWN)
     mine_outs = ((0, 0, half, f32), (0, half, rows, f32))
-    mine_top, mine_bottom = terms(idx, 3, 1, mine_outs, [low_bottom, up_top], *args)
+    mine_top, mine_bottom = terms(idx, 3, 1, mine_outs, [up_top, low_bottom], [], *args)
     low_top = send(add_terms(next_top, via_up), UP)
     up_bottom = send(add_terms(prev_bottom, via_down), DOWN)
-    top = add_terms(mine_top, low_top, up_top)
-    return jnp.concatenate([top, add_terms(mine_bottom, low_bottom, up_bottom)], axis=0)
+    out = [add_terms(mine_top, low_top), add_terms(mine_bottom, up_bottom)]
+    return jnp.concatenate(out, axis=0)
 
 
 def per_device(
@@ -481,14 +498,13 @@
     for_pack, for_pick, for_attend, most = number_pieces(chain, seg_lengths)
     table = exchange(pack(0, FIRST, for_pack, prefix_keys, prefix_values))
 
-    acc = project(idx, 0, rows, (whole,) * 2, [hidden, sib], weights, [low])
     low_half, up_half = low[:half], up[half:]
 
     def rest():
         return exchange(pack(FIRST, PARTS, for_pack, prefix_keys, prefix_values))
 
     def pick_all(lo, hi, tables):
-        return pick(lo, hi, for_pick, tables, [acc])
+        return pick(lo, hi, for_pick, tables, [low_half, up_half, idx])
 
     picked = lax.cond(
         most[0] > FIRST,
@@ -497,12 +513,12 @@
     )
     far = exchange(picked)
 
-    near_blocks = [low, send(low, SIBLING), up, send(up, SIBLING)]
-    acc = project(idx, 2, rows, (whole,) * 4, near_blocks, weights, [], acc)
+    near_blocks = [hidden, sib, low, send(low, SIBLING), up, send(up, SIBLING)]
+    acc = project(idx, 0, rows, (whole,) * 6, near_blocks, weights, [])
 
     far_top, far_bottom = ordered([send(low_half, UP), send(up_half, DOWN)], acc)
     far_blocks = [far_top, far_bottom, send(far_top, SIBLING), send(far_bottom, SIBLING)]
-    q, k, v = project(idx, 6, rows, (split,) * 2, far_blocks, weights, [], acc, True)
+    q, k, v = project(idx, 6, rows, (split,) * 2, far_blocks, weights, [], acc, True, 60)
 
     def attend_rest():
         far_rest = exchange(pick_all(SECOND, PARTS, [table, rest()]))

time: 139 us -> 131 us (0.942)
  Pallas kernels: 55.7 us -> 49.9 us
  starting transfers between devices: 35.3 us -> 31.7 us
  waiting for transfers between devices: 33.3 us -> 35.8 us
    all_to_all x2, starting transfers between devices: 15.6 us -> 12.2 us  [exchange(): return lax.all_to_all(x, 'seq', 0, 0, tiled=True)]
    pallas_call x3 -> x2, Pallas kernels: 21.4 us -> 18.6 us  [project(): pl.pallas_call(functools.partial(project_kernel, plan, len(after), start...]
    all_to_all x2, waiting for transfers between devices: 2.31 us -> 4.93 us  [exchange(): return lax.all_to_all(x, 'seq', 0, 0, tiled=True)]
    pallas_call x1, Pallas kernels: 5.78 us -> 4.26 us  [pick(): pl.pallas_call(functools.partial(pick_kernel, lo, hi, len(tables) > 1), g...]
    unnamed x27 -> x25, local copies, waits for them, and re-layouts: 5.11 us -> 3.71 us
  transfers between devices with their start and end apart: 19 -> 19, of which waited for: 11 -> 11; matrix products, arithmetic and copies ran while one was open for 5% -> 5% of each run, Pallas kernels for 37% -> 35%
where the time goes in v4:
time: 131 us; the launch traced here: 130 us
  Pallas kernels  49.9 us (38%)
  waiting for transfers between devices  35.8 us (27%)
  starting transfers between devices  31.7 us (24%)
  local copies, waits for them, and re-layouts  6.8 us (5%)
  other arithmetic  4.06 us (3%)
  between operations  1.5 us (1%)
    ppermute x17, waiting for transfers between devices, send(): return lax.ppermute(x, 'head', pairs)  30.9 us
    ppermute x17, starting transfers between devices, send(): return lax.ppermute(x, 'head', pairs)  19.5 us
    pallas_call x2, Pallas kernels, project(): pl.pallas_call(functools.partial(project_kernel, plan, len(after), start...  18.6 us
    pallas_call x3, Pallas kernels, terms(): pl.pallas_call(functools.partial(terms_kernel, count, len(added), len(aft...  14.6 us
    all_to_all x2, starting transfers between devices, exchange(): return lax.all_to_all(x, 'seq', 0, 0, tiled=True)  12.2 us
    pallas_call x1, Pallas kernels, attend(): pl.pallas_call(attend_kernel, grid_spec=pltpu.PrefetchScalarGridSpec(num_...  6.85 us
    all_to_all x2, waiting for transfers between devices, exchange(): return lax.all_to_all(x, 'seq', 0, 0, tiled=True)  4.93 us
    pallas_call x1, Pallas kernels, pack(): pl.pallas_call(functools.partial(pack_kernel, lo, hi), grid_spec=pltpu.Pr...  4.6 us
  transfers between devices with their start and end apart: 19, of which 11 were waited for; matrix products, arithmetic and copies ran while one was open for 5% of the time, Pallas kernels for 35%

profile of v4, /device:TPU:1, one launch (start us, length us, event | category | flops | bytes accessed | tf_op | source)
XLA Modules:
  0.0 129.9 jit_solution(10253217962458697611)
XLA Ops:
  0.0 1.4 %collective-permute-start.10 = (bf16[512,8192]{1,0:T(8,128)(2,1)}, bf16[512,8192]{1,0:T(8,128)(2,1)}, u32[]{:S(2)}, u32[]{:S(2)}) collective-permute-start(bf16[512,8192]{1,0:T(8,128)(2,1)} %refs_0_.7), channel_id=1, source_target_pairs={{0,1},{1,0},{2,3},{3,2},{4,5},{5,4},{6,7},{7,6},{8,9},{9,8},{10,11... | collective-permute-start | bytes 25165832 | tf_op jit(solution)/shard_map/ppermute | solution.py:34
  1.4 2.8 %collective-permute-start.2 = (bf16[512,1024]{1,0:T(8,128)(2,1)}, bf16[512,1024]{1,0:T(8,128)(2,1)S(1)}, u32[]{:S(2)}, u32[]{:S(2)}) collective-permute-start(bf16[512,1024]{1,0:T(8,128)(2,1)} %refs_0_.4), channel_id=1, source_target_pairs={{0,6},{1,7},{2,0},{3,1},{4,2},{5,3},{6,4},{7,5},{8,14},{9,15},{10,... | collective-permute-start | bytes 3145736 | tf_op jit(solution)/shard_map/ppermute | solution.py:34
  4.2 0.8 copy.14
  5.1 0.7 copy-done.1
  5.8 1.0 shard_map.100
  6.8 4.6 %shard_map.104 = bf16[16,10,32,128]{3,2,1,0:T(8,128)(2,1)} custom-call(s32[24,128]{1,0:T(8,128)S(1)} %get-tuple-element.129.first_ref, bf16[8,2,16,16,128]{4,3,2,1,0:T(8,128)(2,1)} %bitcast.12, bf16[8,2,16,16,128]{4,3,2,1,0:T(8,128)(2,1)} %bitcast.13, bf16[8,2,16,16,128]{4,3,2,1,0:T(8,128)(2,1)} %bitcast.18, bf16[8,2,16,16,128]{4,3,2,1,0:T(8,128)(2,1)} %bitcast.19), custom_call_target="tpu_custom_call" | custom-call | bytes 4194304 | tf_op jit(solution)/shard_map/pallas_call | solution.py:193
  11.4 7.8 %all-to-all-start.3 = ((bf16[16,10,32,128]{3,2,1,0:T(8,128)(2,1)}), bf16[16,10,32,128]{3,2,1,0:T(8,128)(2,1)}, u32[]{:S(2)}, u32[]{:S(2)}) async-start(bf16[16,10,32,128]{3,2,1,0:T(8,128)(2,1)} %shard_map.104), calls=%async_computation.3 | async-start | bytes 2621440 | tf_op jit(solution)/shard_map/all_to_all | solution.py:267
  19.2 0.6 collective-permute-start.4
  19.9 7.3 %collective-permute-done.2.refs_4_ = bf16[512,1024]{1,0:T(8,128)(2,1)S(1)} collective-permute-done((bf16[512,1024]{1,0:T(8,128)(2,1)}, bf16[512,1024]{1,0:T(8,128)(2,1)S(1)}, u32[]{:S(2)}, u32[]{:S(2)}) %collective-permute-start.2) | collective-permute-done | bytes 1048608 | tf_op jit(solution)/shard_map/ppermute | solution.py:34
  27.1 0.8 collective-permute-start.6
  27.9 2.3 %collective-permute-done.refs_2_ = bf16[512,1024]{1,0:T(8,128)(2,1)S(1)} collective-permute-done((bf16[512,1024]{1,0:T(8,128)(2,1)}, bf16[512,1024]{1,0:T(8,128)(2,1)S(1)}, u32[]{:S(2)}, u32[]{:S(2)}) %collective-permute-start) | collective-permute-done | bytes 1048608 | tf_op jit(solution)/shard_map/ppermute | solution.py:34
  30.2 1.0 collective-permute-start.5
  31.2 0.6 fusion
  32.5 0.7 dynamic-slice_bitcast_fusion.idx_ref
  33.2 0.8 slice.17
  34.0 0.8 slice.16
  34.9 4.9 %all-to-all-done.3 = bf16[16,10,32,128]{3,2,1,0:T(8,128)(2,1)} async-done(((bf16[16,10,32,128]{3,2,1,0:T(8,128)(2,1)}), bf16[16,10,32,128]{3,2,1,0:T(8,128)(2,1)}, u32[]{:S(2)}, u32[]{:S(2)}) %all-to-all-start.3) | async-done | bytes 1310752 | tf_op jit(solution)/shard_map/all_to_all | solution.py:267
  39.8 4.3 %conditional.2 = (bf16[16,13,32,128]{3,2,1,0:T(8,128)(2,1)}) conditional(s32[]{:T(128)} %bitcast.7, (s32[8,256]{1,0:T(8,128)S(1)}, bf16[16,10,32,128]{3,2,1,0:T(8,128)(2,1)}, bf16[256,1024]{1,0:T(8,128)(2,1)}, bf16[256,1024]{1,0:T(8,128)(2,1)}, s32[12]{0:T(128)S(1)}) %tuple.17, (bf16[4096,128]{1,0:T(8,128)(2,1)}, bf16[4096,128]{1,0:T(8,128)(2,1)}, ...), branch_computations={%region_0.1_spmd, %region_1.2_spmd} | conditional | bytes 10485796 | solution.py:509
  39.8 4.3 %branch_0_fun.2 = bf16[16,13,32,128]{3,2,1,0:T(8,128)(2,1)} custom-call(s32[8,256]{1,0:T(8,128)S(1)} %get-tuple-element.72.slot_ref, bf16[16,10,32,128]{3,2,1,0:T(8,128)(2,1)} %get-tuple-element.74.refs_0_, bf16[256,1024]{1,0:T(8,128)(2,1)} %get-tuple-element.75.refs_1_, bf16[256,1024]{1,0:T(8,128)(2,1)} %get-tuple-element.76.refs_2_, ...), custom_call_target="tpu_custom_call" | custom-call | bytes 2621440 | tf_op jit(solution)/shard_map/cond/branch_0_fun/pallas_call | solution.py:251
  44.1 4.4 %all-to-all-start.4 = ((bf16[16,13,32,128]{3,2,1,0:T(8,128)(2,1)}), bf16[16,13,32,128]{3,2,1,0:T(8,128)(2,1)}, u32[]{:S(2)}, u32[]{:S(2)}) async-start(bf16[16,13,32,128]{3,2,1,0:T(8,128)(2,1)} %get-tuple-element.140), calls=%async_computation.4 | async-start | bytes 3407872 | tf_op jit(solution)/shard_map/all_to_all | solution.py:267
  48.5 2.2 %collective-permute-start.3 = (bf16[256,1024]{1,0:T(8,128)(2,1)}, bf16[256,1024]{1,0:T(8,128)(2,1)}, u32[]{:S(2)}, u32[]{:S(2)}) collective-permute-start(bf16[256,1024]{1,0:T(8,128)(2,1)} %slice.17), channel_id=1, source_target_pairs={{0,6},{1,7},{2,0},{3,1},{4,2},{5,3},{6,4},{7,5},{8,14},{9,15},{10,... | collective-permute-start | bytes 1572872 | tf_op jit(solution)/shard_map/ppermute | solution.py:34
  50.7 12.0 %shard_map.101.refs_2_.refs_7_ = f32[512,768]{1,0:T(8,128)} custom-call(s32[12]{0:T(128)S(1)} %dynamic-slice_bitcast_fusion.idx_ref, bf16[512,1024]{1,0:T(8,128)(2,1)S(1)} %copy-done, bf16[512,1024]{1,0:T(8,128)(2,1)} %collective-permute-done.4.refs_1_, bf16[512,1024]{1,0:T(8,128)(2,1)S(1)} %collective-permute-done.refs_2_, ...), custom_call_target="tpu_custom_call" | custom-call | flops 4831838208 | bytes 15728640 | tf_op jit(solution)/shard_map/pallas_call | solution.py:320
  62.7 0.6 collective-permute-done.1.refs_0_
  63.4 3.2 %collective-permute-start.7 = (bf16[256,1024]{1,0:T(8,128)(2,1)}, bf16[256,1024]{1,0:T(8,128)(2,1)S(1)}, u32[]{:S(2)}, u32[]{:S(2)}) collective-permute-start(bf16[256,1024]{1,0:T(8,128)(2,1)} %get-tuple-element.123.refs_0_), channel_id=1, source_target_pairs={{0,1},{1,0},{2,3},{3,2},{4,5},{5,4},{6,7},{7,6},{8,9},{9,8},{10,11... | collective-permute-start | bytes 1572872 | tf_op jit(solution)/shard_map/ppermute | solution.py:34
  67.2 1.8 %collective-permute-done.7.refs_2_ = bf16[256,1024]{1,0:T(8,128)(2,1)S(1)} collective-permute-done((bf16[256,1024]{1,0:T(8,128)(2,1)}, bf16[256,1024]{1,0:T(8,128)(2,1)S(1)}, u32[]{:S(2)}, u32[]{:S(2)}) %collective-permute-start.7) | collective-permute-done | bytes 524320 | tf_op jit(solution)/shard_map/ppermute | solution.py:34
  69.0 0.2 collective-permute-done.8.refs_3_
  69.2 0.6 copy-done.12
  69.8 6.6 %shard_map.103 = (bf16[512,512]{1,0:T(8,128)(2,1)}, bf16[512,128]{1,0:T(8,128)(2,1)S(1)}, bf16[512,128]{1,0:T(8,128)(2,1)S(1)}) custom-call(s32[12]{0:T(128)S(1)} %dynamic-slice_bitcast_fusion.idx_ref, bf16[256,1024]{1,0:T(8,128)(2,1)} %get-tuple-element.123.refs_0_, bf16[256,1024]{1,0:T(8,128)(2,1)} %get-tuple-element.124.refs_1_, ...), custom_call_target="tpu_custom_call" | custom-call | flops 1610612736 | bytes 5242880 | tf_op jit(solution)/shard_map/pallas_call | solution.py:320
  76.4 6.9 %conditional.3 = (bf16[512,512]{1,0:T(8,128)(2,1)S(1)}) conditional(s32[]{:T(128)} %bitcast.6, (s32[24,128]{1,0:T(8,128)S(1)}, bf16[512,512]{1,0:T(8,128)(2,1)}, bf16[512,128]{1,0:T(8,128)(2,1)S(1)}, bf16[512,128]{1,0:T(8,128)(2,1)S(1)}, bf16[16,13,32,128]{3,2,1,0:T(8,128)(2,1)}) %tuple.19, (bf16[4096,128]{1,0:T(8,128)(2,1)S(1)}, ...), branch_computations={%region_2.3_spmd, %region_3.4_spmd} | conditional | flops 1207959552 | bytes 15728676 | solution.py:530
  76.4 6.9 %branch_0_fun.3 = bf16[512,512]{1,0:T(8,128)(2,1)S(1)} custom-call(s32[24,128]{1,0:T(8,128)S(1)} %get-tuple-element.86.slot_ref, bf16[512,512]{1,0:T(8,128)(2,1)} %get-tuple-element.87.q_ref, bf16[512,128]{1,0:T(8,128)(2,1)S(1)} %get-tuple-element.88.k_ref, bf16[512,128]{1,0:T(8,128)(2,1)S(1)} %get-tuple-element.89.v_ref, ...), custom_call_target="tpu_custom_call" | custom-call | flops 1207959552 | bytes 4456448 | tf_op jit(solution)/shard_map/cond/branch_0_fun/pallas_call | solution.py:392
  83.3 0.5 collective-permute-start.9
  83.8 1.5 %collective-permute-done.9.b_ref = bf16[512,512]{1,0:T(8,128)(2,1)S(1)} collective-permute-done((bf16[512,512]{1,0:T(8,128)(2,1)S(1)}, bf16[512,512]{1,0:T(8,128)(2,1)S(1)}, u32[]{:S(2)}, u32[]{:S(2)}) %collective-permute-start.9) | collective-permute-done | bytes 524320 | tf_op jit(solution)/shard_map/ppermute | solution.py:34
  85.3 0.8 copy-done.7
  86.1 4.1 %shard_map.105 = (bf16[256,1024]{1,0:T(8,128)(2,1)}, bf16[256,1024]{1,0:T(8,128)(2,1)}) custom-call(s32[12]{0:T(128)S(1)} %dynamic-slice_bitcast_fusion.idx_ref, bf16[512,512]{1,0:T(8,128)(2,1)S(1)} %get-tuple-element.141.a_ref, bf16[512,512]{1,0:T(8,128)(2,1)} %copy-done.7, bf16[512,8192]{1,0:T(8,128)(2,1)} %refs_0_.7, ...), custom_call_target="tpu_custom_call" | custom-call | flops 1073741824 | bytes 4194304 | tf_op jit(solution)/shard_map/pallas_call | solution.py:434
  90.2 2.7 %collective-permute-start.15 = (bf16[256,1024]{1,0:T(8,128)(2,1)}, bf16[256,1024]{1,0:T(8,128)(2,1)S(1)}, u32[]{:S(2)}, u32[]{:S(2)}) collective-permute-start(bf16[256,1024]{1,0:T(8,128)(2,1)} %get-tuple-element.137), channel_id=1, source_target_pairs={{0,6},{1,7},{2,0},{3,1},{4,2},{5,3},{6,4},{7,5},{8,14},{9,15},{10,... | collective-permute-start | bytes 1572872 | tf_op jit(solution)/shard_map/ppermute | solution.py:34
  92.9 5.8 %shard_map.106 = (f32[256,1024]{1,0:T(8,128)}, bf16[256,1024]{1,0:T(8,128)(2,1)}, bf16[256,1024]{1,0:T(8,128)(2,1)}, f32[256,1024]{1,0:T(8,128)}) custom-call(s32[12]{0:T(128)S(1)} %dynamic-slice_bitcast_fusion.idx_ref, bf16[512,512]{1,0:T(8,128)(2,1)S(1)} %get-tuple-element.141.a_ref, bf16[512,512]{1,0:T(8,128)(2,1)} %copy-done.7, ...), custom_call_target="tpu_custom_call" | custom-call | flops 2147483648 | bytes 8388608 | tf_op jit(solution)/shard_map/pallas_call | solution.py:434
  98.8 1.5 %collective-permute-start.12 = (bf16[256,1024]{1,0:T(8,128)(2,1)}, bf16[256,1024]{1,0:T(8,128)(2,1)S(1)}, u32[]{:S(2)}, u32[]{:S(2)}) collective-permute-start(bf16[256,1024]{1,0:T(8,128)(2,1)} %get-tuple-element.132), channel_id=1, source_target_pairs={{0,2},{1,3},{2,4},{3,5},{4,6},{5,7},{6,0},{7,1},{8,10},{9,11},{10,... | collective-permute-start | bytes 1572872 | tf_op jit(solution)/shard_map/ppermute | solution.py:34
  100.3 4.5 %collective-permute-done.13 = bf16[256,1024]{1,0:T(8,128)(2,1)S(1)} collective-permute-done((bf16[256,1024]{1,0:T(8,128)(2,1)}, bf16[256,1024]{1,0:T(8,128)(2,1)S(1)}, u32[]{:S(2)}, u32[]{:S(2)}) %collective-permute-start.13) | collective-permute-done | bytes 524320 | tf_op jit(solution)/shard_map/ppermute | solution.py:34
  104.8 1.4 %add_convert_fusion.3 = bf16[256,1024]{1,0:T(8,128)(2,1)S(1)} fusion(f32[256,1024]{1,0:T(8,128)} %get-tuple-element.134, bf16[256,1024]{1,0:T(8,128)(2,1)S(1)} %collective-permute-done.13), kind=kLoop, calls=%fused_computation.4 | loop fusion | flops 786432 | bytes 2097152 | tf_op jit(solution)/shard_map/convert_element_type | solution.py:456
  106.4 2.7 %collective-permute-start.16 = (bf16[256,1024]{1,0:T(8,128)(2,1)S(1)}, bf16[256,1024]{1,0:T(8,128)(2,1)S(1)}, u32[]{:S(2)}, u32[]{:S(2)}) collective-permute-start(bf16[256,1024]{1,0:T(8,128)(2,1)S(1)} %add_convert_fusion.1), channel_id=1, source_target_pairs={{0,6},{1,7},{2,0},{3,1},{4,2},{5,3},{6,4},{7,5},{8,14},{9,15},{10,... | collective-permute-start | bytes 1572872 | tf_op jit(solution)/shard_map/ppermute | solution.py:34
  109.1 5.9 %collective-permute-done.11.refs_2_ = bf16[256,1024]{1,0:T(8,128)(2,1)S(1)} collective-permute-done((bf16[256,1024]{1,0:T(8,128)(2,1)}, bf16[256,1024]{1,0:T(8,128)(2,1)S(1)}, u32[]{:S(2)}, u32[]{:S(2)}) %collective-permute-start.11) | collective-permute-done | bytes 524320 | tf_op jit(solution)/shard_map/ppermute | solution.py:34
  115.1 0.9 collective-permute-done.12.refs_3_
  116.0 0.8 copy-done.11
  116.8 4.7 %shard_map.107 = (f32[256,1024]{1,0:T(8,128)}, f32[256,1024]{1,0:T(8,128)}) custom-call(s32[12]{0:T(128)S(1)} %dynamic-slice_bitcast_fusion.idx_ref, bf16[512,512]{1,0:T(8,128)(2,1)S(1)} %get-tuple-element.141.a_ref, bf16[512,512]{1,0:T(8,128)(2,1)} %copy-done.7, bf16[512,8192]{1,0:T(8,128)(2,1)} %refs_0_.7, ...), custom_call_target="tpu_custom_call" | custom-call | flops 1073741824 | bytes 4194304 | tf_op jit(solution)/shard_map/pallas_call | solution.py:434
  121.5 5.8 %collective-permute-done.14 = bf16[256,1024]{1,0:T(8,128)(2,1)S(1)} collective-permute-done((bf16[256,1024]{1,0:T(8,128)(2,1)S(1)}, bf16[256,1024]{1,0:T(8,128)(2,1)S(1)}, u32[]{:S(2)}, u32[]{:S(2)}) %collective-permute-start.14) | collective-permute-done | bytes 524320 | tf_op jit(solution)/shard_map/ppermute | solution.py:34
  127.3 1.4 %add_convert_fusion.2 = bf16[256,1024]{1,0:T(8,128)(2,1)S(1)} fusion(f32[256,1024]{1,0:T(8,128)} %get-tuple-element.133, bf16[256,1024]{1,0:T(8,128)(2,1)S(1)} %collective-permute-done.14), kind=kLoop, calls=%fused_computation.3 | loop fusion | flops 786432 | bytes 2097152 | tf_op jit(solution)/shard_map/convert_element_type | solution.py:456
  128.7 0.1 add_convert_fusion
  128.8 1.0 pad_maximum_fusion
  (37 shorter events, 0.5 us)
Async XLA Ops:
  0.0 85.3 %collective-permute-start.10 = (bf16[512,8192]{1,0:T(8,128)(2,1)}, bf16[512,8192]{1,0:T(8,128)(2,1)}, u32[]{:S(2)}, u32[]{:S(2)}) collective-permute-start(bf16[512,8192]{1,0:T(8,128)(2,1)} %refs_0_.7), channel_id=1, source_target_pairs={{0,1},{1,0},{2,3},{3,2},{4,5},{5,4},{6,7},{7,6},{8,9},{9,8},{10,11... | collective-permute-start | bytes 25165832 | tf_op jit(solution)/shard_map/ppermute | solution.py:34
  1.4 25.7 %collective-permute-start.2 = (bf16[512,1024]{1,0:T(8,128)(2,1)}, bf16[512,1024]{1,0:T(8,128)(2,1)S(1)}, u32[]{:S(2)}, u32[]{:S(2)}) collective-permute-start(bf16[512,1024]{1,0:T(8,128)(2,1)} %refs_0_.4), channel_id=1, source_target_pairs={{0,6},{1,7},{2,0},{3,1},{4,2},{5,3},{6,4},{7,5},{8,14},{9,15},{10,... | collective-permute-start | bytes 3145736 | tf_op jit(solution)/shard_map/ppermute | solution.py:34
  4.2 26.0 %collective-permute-start = (bf16[512,1024]{1,0:T(8,128)(2,1)}, bf16[512,1024]{1,0:T(8,128)(2,1)S(1)}, u32[]{:S(2)}, u32[]{:S(2)}) collective-permute-start(bf16[512,1024]{1,0:T(8,128)(2,1)} %refs_0_.4), channel_id=1, source_target_pairs={{0,2},{1,3},{2,4},{3,5},{4,6},{5,7},{6,0},{7,1},{8,10},{9,11},{10,... | collective-permute-start | bytes 3145736 | tf_op jit(solution)/shard_map/ppermute | solution.py:34
  5.1 0.7 copy-start.1
  11.4 7.8 %copy-start = (bf16[512,1024]{1,0:T(8,128)(2,1)S(1)}, bf16[512,1024]{1,0:T(8,128)(2,1)}, u32[]{:S(2)}) copy-start(bf16[512,1024]{1,0:T(8,128)(2,1)} %refs_0_.4) | copy-start | bytes 3145732
  11.4 28.4 %all-to-all-start.3 = ((bf16[16,10,32,128]{3,2,1,0:T(8,128)(2,1)}), bf16[16,10,32,128]{3,2,1,0:T(8,128)(2,1)}, u32[]{:S(2)}, u32[]{:S(2)}) async-start(bf16[16,10,32,128]{3,2,1,0:T(8,128)(2,1)} %shard_map.104), calls=%async_computation.3 | async-start | bytes 2621440 | tf_op jit(solution)/shard_map/all_to_all | solution.py:267
  19.2 31.5 %collective-permute-start.4 = (bf16[512,1024]{1,0:T(8,128)(2,1)S(1)}, bf16[512,1024]{1,0:T(8,128)(2,1)}, u32[]{:S(2)}, u32[]{:S(2)}) collective-permute-start(bf16[512,1024]{1,0:T(8,128)(2,1)S(1)} %copy-done), channel_id=1, source_target_pairs={{0,1},{1,0},{2,3},{3,2},{4,5},{5,4},{6,7},{7,6},{8,9},{9,8},{10,11... | collective-permute-start | bytes 3145736 | tf_op jit(solution)/shard_map/ppermute | solution.py:34
  27.1 23.5 %collective-permute-start.6 = (bf16[512,1024]{1,0:T(8,128)(2,1)S(1)}, bf16[512,1024]{1,0:T(8,128)(2,1)}, u32[]{:S(2)}, u32[]{:S(2)}) collective-permute-start(bf16[512,1024]{1,0:T(8,128)(2,1)S(1)} %collective-permute-done.2.refs_4_), channel_id=1, source_target_pairs={{0,1},{1,0},{2,3},{3,2},{4,5},{5,4},{6,7},{7,6},{8,9},{9,8},{10,11... | collective-permute-start | bytes 3145736 | tf_op jit(solution)/shard_map/ppermute | solution.py:34
  30.2 20.5 %collective-permute-start.5 = (bf16[512,1024]{1,0:T(8,128)(2,1)S(1)}, bf16[512,1024]{1,0:T(8,128)(2,1)}, u32[]{:S(2)}, u32[]{:S(2)}) collective-permute-start(bf16[512,1024]{1,0:T(8,128)(2,1)S(1)} %collective-permute-done.refs_2_), channel_id=1, source_target_pairs={{0,1},{1,0},{2,3},{3,2},{4,5},{5,4},{6,7},{7,6},{8,9},{9,8},{10,11... | collective-permute-start | bytes 3145736 | tf_op jit(solution)/shard_map/ppermute | solution.py:34
  44.1 32.3 %all-to-all-start.4 = ((bf16[16,13,32,128]{3,2,1,0:T(8,128)(2,1)}), bf16[16,13,32,128]{3,2,1,0:T(8,128)(2,1)}, u32[]{:S(2)}, u32[]{:S(2)}) async-start(bf16[16,13,32,128]{3,2,1,0:T(8,128)(2,1)} %get-tuple-element.140), calls=%async_computation.4 | async-start | bytes 3407872 | tf_op jit(solution)/shard_map/all_to_all | solution.py:267
  48.5 14.2 %collective-permute-start.3 = (bf16[256,1024]{1,0:T(8,128)(2,1)}, bf16[256,1024]{1,0:T(8,128)(2,1)}, u32[]{:S(2)}, u32[]{:S(2)}) collective-permute-start(bf16[256,1024]{1,0:T(8,128)(2,1)} %slice.17), channel_id=1, source_target_pairs={{0,6},{1,7},{2,0},{3,1},{4,2},{5,3},{6,4},{7,5},{8,14},{9,15},{10,... | collective-permute-start | bytes 1572872 | tf_op jit(solution)/shard_map/ppermute | solution.py:34
  50.7 12.7 %collective-permute-start.1 = (bf16[256,1024]{1,0:T(8,128)(2,1)}, bf16[256,1024]{1,0:T(8,128)(2,1)}, u32[]{:S(2)}, u32[]{:S(2)}) collective-permute-start(bf16[256,1024]{1,0:T(8,128)(2,1)} %slice.16), channel_id=1, source_target_pairs={{0,2},{1,3},{2,4},{3,5},{4,6},{5,7},{6,0},{7,1},{8,10},{9,11},{10,... | collective-permute-start | bytes 1572872 | tf_op jit(solution)/shard_map/ppermute | solution.py:34
  63.4 5.6 %collective-permute-start.7 = (bf16[256,1024]{1,0:T(8,128)(2,1)}, bf16[256,1024]{1,0:T(8,128)(2,1)S(1)}, u32[]{:S(2)}, u32[]{:S(2)}) collective-permute-start(bf16[256,1024]{1,0:T(8,128)(2,1)} %get-tuple-element.123.refs_0_), channel_id=1, source_target_pairs={{0,1},{1,0},{2,3},{3,2},{4,5},{5,4},{6,7},{7,6},{8,9},{9,8},{10,11... | collective-permute-start | bytes 1572872 | tf_op jit(solution)/shard_map/ppermute | solution.py:34
  66.6 2.6 %collective-permute-start.8 = (bf16[256,1024]{1,0:T(8,128)(2,1)}, bf16[256,1024]{1,0:T(8,128)(2,1)}, u32[]{:S(2)}, u32[]{:S(2)}) collective-permute-start(bf16[256,1024]{1,0:T(8,128)(2,1)} %get-tuple-element.124.refs_1_), channel_id=1, source_target_pairs={{0,1},{1,0},{2,3},{3,2},{4,5},{5,4},{6,7},{7,6},{8,9},{9,8},{10,11... | collective-permute-start | bytes 1572872 | tf_op jit(solution)/shard_map/ppermute | solution.py:34
  67.2 9.2 %copy-start.2 = (bf16[4096,128]{1,0:T(8,128)(2,1)S(1)}, bf16[4096,128]{1,0:T(8,128)(2,1)}, u32[]{:S(2)}) copy-start(bf16[4096,128]{1,0:T(8,128)(2,1)} %param.19) | copy-start | bytes 3145732
  67.2 9.2 %copy-start.3 = (bf16[4096,128]{1,0:T(8,128)(2,1)S(1)}, bf16[4096,128]{1,0:T(8,128)(2,1)}, u32[]{:S(2)}) copy-start(bf16[4096,128]{1,0:T(8,128)(2,1)} %param.20) | copy-start | bytes 3145732
  67.2 9.2 %copy-start.4 = (bf16[256,1024]{1,0:T(8,128)(2,1)S(1)}, bf16[256,1024]{1,0:T(8,128)(2,1)}, u32[]{:S(2)}) copy-start(bf16[256,1024]{1,0:T(8,128)(2,1)} %slice.17) | copy-start | bytes 1572868
  67.2 9.2 %copy-start.6 = (bf16[256,1024]{1,0:T(8,128)(2,1)S(1)}, bf16[256,1024]{1,0:T(8,128)(2,1)}, u32[]{:S(2)}) copy-start(bf16[256,1024]{1,0:T(8,128)(2,1)} %slice.16) | copy-start | bytes 1572868
  69.0 0.8 copy-start.12
  83.3 2.0 %collective-permute-start.9 = (bf16[512,512]{1,0:T(8,128)(2,1)S(1)}, bf16[512,512]{1,0:T(8,128)(2,1)S(1)}, u32[]{:S(2)}, u32[]{:S(2)}) collective-permute-start(bf16[512,512]{1,0:T(8,128)(2,1)S(1)} %get-tuple-element.141.a_ref), channel_id=1, source_target_pairs={{0,1},{1,0},{2,3},{3,2},{4,5},{5,4},{6,7},{7,6},{8,9},{9,8},{10,11... | collective-permute-start | bytes 1572872 | tf_op jit(solution)/shard_map/ppermute | solution.py:34
  85.3 0.8 copy-start.7
  90.2 14.6 %collective-permute-start.13 = (bf16[256,1024]{1,0:T(8,128)(2,1)}, bf16[256,1024]{1,0:T(8,128)(2,1)S(1)}, u32[]{:S(2)}, u32[]{:S(2)}) collective-permute-start(bf16[256,1024]{1,0:T(8,128)(2,1)} %get-tuple-element.130.refs_4_), channel_id=1, source_target_pairs={{0,2},{1,3},{2,4},{3,5},{4,6},{5,7},{6,0},{7,1},{8,10},{9,11},{10,... | collective-permute-start | bytes 1572872 | tf_op jit(solution)/shard_map/ppermute | solution.py:34
  90.2 16.0 %collective-permute-start.15 = (bf16[256,1024]{1,0:T(8,128)(2,1)}, bf16[256,1024]{1,0:T(8,128)(2,1)S(1)}, u32[]{:S(2)}, u32[]{:S(2)}) collective-permute-start(bf16[256,1024]{1,0:T(8,128)(2,1)} %get-tuple-element.137), channel_id=1, source_target_pairs={{0,6},{1,7},{2,0},{3,1},{4,2},{5,3},{6,4},{7,5},{8,14},{9,15},{10,... | collective-permute-start | bytes 1572872 | tf_op jit(solution)/shard_map/ppermute | solution.py:34
  98.7 7.5 %copy-start.8 = (f32[256,1024]{1,0:T(8,128)S(1)}, f32[256,1024]{1,0:T(8,128)}, u32[]{:S(2)}) copy-start(f32[256,1024]{1,0:T(8,128)} %get-tuple-element.136) | copy-start | bytes 3145732
  98.7 16.3 %collective-permute-start.11 = (bf16[256,1024]{1,0:T(8,128)(2,1)}, bf16[256,1024]{1,0:T(8,128)(2,1)S(1)}, u32[]{:S(2)}, u32[]{:S(2)}) collective-permute-start(bf16[256,1024]{1,0:T(8,128)(2,1)} %get-tuple-element.131), channel_id=1, source_target_pairs={{0,6},{1,7},{2,0},{3,1},{4,2},{5,3},{6,4},{7,5},{8,14},{9,15},{10,... | collective-permute-start | bytes 1572872 | tf_op jit(solution)/shard_map/ppermute | solution.py:34
  98.8 17.2 %collective-permute-start.12 = (bf16[256,1024]{1,0:T(8,128)(2,1)}, bf16[256,1024]{1,0:T(8,128)(2,1)S(1)}, u32[]{:S(2)}, u32[]{:S(2)}) collective-permute-start(bf16[256,1024]{1,0:T(8,128)(2,1)} %get-tuple-element.132), channel_id=1, source_target_pairs={{0,2},{1,3},{2,4},{3,5},{4,6},{5,7},{6,0},{7,1},{8,10},{9,11},{10,... | collective-permute-start | bytes 1572872 | tf_op jit(solution)/shard_map/ppermute | solution.py:34
  106.2 21.1 %collective-permute-start.14 = (bf16[256,1024]{1,0:T(8,128)(2,1)S(1)}, bf16[256,1024]{1,0:T(8,128)(2,1)S(1)}, u32[]{:S(2)}, u32[]{:S(2)}) collective-permute-start(bf16[256,1024]{1,0:T(8,128)(2,1)S(1)} %add_convert_fusion.3), channel_id=1, source_target_pairs={{0,2},{1,3},{2,4},{3,5},{4,6},{5,7},{6,0},{7,1},{8,10},{9,11},{10,... | collective-permute-start | bytes 1572872 | tf_op jit(solution)/shard_map/ppermute | solution.py:34
  106.4 22.2 %collective-permute-start.16 = (bf16[256,1024]{1,0:T(8,128)(2,1)S(1)}, bf16[256,1024]{1,0:T(8,128)(2,1)S(1)}, u32[]{:S(2)}, u32[]{:S(2)}) collective-permute-start(bf16[256,1024]{1,0:T(8,128)(2,1)S(1)} %add_convert_fusion.1), channel_id=1, source_target_pairs={{0,6},{1,7},{2,0},{3,1},{4,2},{5,3},{6,4},{7,5},{8,14},{9,15},{10,... | collective-permute-start | bytes 1572872 | tf_op jit(solution)/shard_map/ppermute | solution.py:34
  115.1 0.9 copy-start.10
  116.0 0.8 copy-start.11
  121.5 7.2 %copy-start.9 = (f32[256,1024]{1,0:T(8,128)S(1)}, f32[256,1024]{1,0:T(8,128)}, u32[]{:S(2)}) copy-start(f32[256,1024]{1,0:T(8,128)} %get-tuple-element.135) | copy-start | bytes 3145732

commit v5 on v4

--- a/solution.py
+++ b/solution.py
@@ -71,7 +71,7 @@
     )(*xs, after)
 
 
-FIRST = 10
+FIRST = 9
 SECOND = 13
 PARTS = SEG_LEN // GRAN
 STEPS = 4
@@ -341,67 +341,66 @@
 
 def attend_kernel(slot_ref, q_ref, k_ref, v_ref, *refs):
     *tables, out_ref, keys, values = refs
-    roll = pl.program_id(0)
     scale = math.log2(math.e) / math.sqrt(HD)
     slot = lax.broadcasted_iota(jnp.int32, (1, SEG_LEN), 1)
-    masks = []
-    for level in range(DEPTH):
-        at = roll * DEPTH + level
-        live = slot_ref[PARTS, at]
-        row = slot
-        if level % 2:
-            row = (PARTS - 1 - slot // GRAN) * GRAN + slot % GRAN
-        masks.append(jnp.where(row < live, 0.0, -jnp.inf))
-        pieces = []
-        for i in range(PARTS):
-            to = slot_ref[i, at]
-            piece = tables[0][i, jnp.minimum(to, SECOND - 1)]
-            if len(tables) > 1:
-                rest = tables[1][i, jnp.maximum(to - SECOND, 0)]
-                piece = jnp.where(to < SECOND, piece, rest)
-            pieces.append(piece)
-        lo = level * SEG_LEN
-        keys[lo : lo + SEG_LEN] = jnp.concatenate([p[:GRAN] for p in pieces], axis=0)
-        values[lo : lo + SEG_LEN] = jnp.concatenate([p[GRAN:] for p in pieces], axis=0)
-    mask = jnp.concatenate(masks, axis=1)
-    row = lax.broadcasted_iota(jnp.int32, (ROLL, ROLL), 0)
-    causal = jnp.where(row >= lax.broadcasted_iota(jnp.int32, (ROLL, ROLL), 1), 0.0, -jnp.inf)
-    causal = jnp.concatenate([causal] * HEADS, axis=0)
-    nt = (((1,), (1,)), ((), ()))
-    ones = jnp.ones((FAR, HD), jnp.bfloat16)
-    for g0 in range(0, GROUP, HEADS):
-        heads = range(g0, g0 + HEADS)
-        q = jnp.concatenate([q_ref[:, g * HD : (g + 1) * HD] for g in heads], axis=0)
-        far = lax.dot_general(q, keys[...], nt, preferred_element_type=jnp.float32) + mask
-        own = lax.dot_general(q, k_ref[...], nt, preferred_element_type=jnp.float32) + causal
-        m = jnp.maximum(jnp.max(far, axis=1, keepdims=True), jnp.max(own, axis=1, keepdims=True))
-        far = jnp.exp2((far - m) * scale).astype(jnp.bfloat16)
-        own = jnp.exp2((own - m) * scale).astype(jnp.bfloat16)
-        far_values = jnp.concatenate([values[...], ones], axis=1)
-        own_values = jnp.concatenate([v_ref[...], ones[:ROLL]], axis=1)
-        mix = jnp.dot(far, far_values, preferred_element_type=jnp.float32)
-        mix += jnp.dot(own, own_values, preferred_element_type=jnp.float32)
-        mix = (mix[:, :HD] / mix[:, HD:]).astype(jnp.bfloat16)
-        for n, g in enumerate(heads):
-            out_ref[:, g * HD : (g + 1) * HD] = mix[n * ROLL : (n + 1) * ROLL]
+
+    def rollout(roll, carry):
+        tokens = pl.ds(pl.multiple_of(roll * ROLL, ROLL), ROLL)
+        masks = []
+        for level in range(DEPTH):
+            at = roll * DEPTH + level
+            live = slot_ref[PARTS, at]
+            row = slot
+            if level % 2:
+                row = (PARTS - 1 - slot // GRAN) * GRAN + slot % GRAN
+            masks.append(jnp.where(row < live, 0.0, -jnp.inf))
+            pieces = []
+            for i in range(PARTS):
+                to = slot_ref[i, at]
+                piece = tables[0][i, jnp.minimum(to, SECOND - 1)]
+                if len(tables) > 1:
+                    rest = tables[1][i, jnp.maximum(to - SECOND, 0)]
+                    piece = jnp.where(to < SECOND, piece, rest)
+                pieces.append(piece)
+            lo = level * SEG_LEN
+            keys[lo : lo + SEG_LEN] = jnp.concatenate([p[:GRAN] for p in pieces], axis=0)
+            values[lo : lo + SEG_LEN] = jnp.concatenate([p[GRAN:] for p in pieces], axis=0)
+        mask = jnp.concatenate(masks, axis=1)
+        row = lax.broadcasted_iota(jnp.int32, (ROLL, ROLL), 0)
+        causal = jnp.where(row >= lax.broadcasted_iota(jnp.int32, (ROLL, ROLL), 1), 0.0, -jnp.inf)
+        causal = jnp.concatenate([causal] * HEADS, axis=0)
+        nt = (((1,), (1,)), ((), ()))
+        ones = jnp.ones((FAR, HD), jnp.bfloat16)
+        for g0 in range(0, GROUP, HEADS):
+            heads = range(g0, g0 + HEADS)
+            q = jnp.concatenate([q_ref[tokens, g * HD : (g + 1) * HD] for g in heads], axis=0)
+            far = lax.dot_general(q, keys[...], nt, preferred_element_type=jnp.float32) + mask
+            own = lax.dot_general(q, k_ref[tokens], nt, preferred_element_type=jnp.float32) + causal
+            m = jnp.maximum(jnp.max(far, axis=1, keepdims=True), jnp.max(own, axis=1, keepdims=True))
+            far = jnp.exp2((far - m) * scale).astype(jnp.bfloat16)
+            own = jnp.exp2((own - m) * scale).astype(jnp.bfloat16)
+            far_values = jnp.concatenate([values[...], ones], axis=1)
+            own_values = jnp.concatenate([v_ref[tokens], ones[:ROLL]], axis=1)
+            mix = jnp.dot(far, far_values, preferred_element_type=jnp.float32)
+            mix += jnp.dot(own, own_values, preferred_element_type=jnp.float32)
+            mix = (mix[:, :HD] / mix[:, HD:]).astype(jnp.bfloat16)
+            for n, g in enumerate(heads):
+                out_ref[tokens, g * HD : (g + 1) * HD] = mix[n * ROLL : (n + 1) * ROLL]
+        return carry
+
+    lax.fori_loop(0, q_ref.shape[0] // ROLL, rollout, None)
 
 
 def attend(slots, q, k, v, tables):
-    rolls = q.shape[0] // ROLL
-    row = lambda n: pl.BlockSpec((ROLL, n), lambda i, *s: (i, 0))
+    vmem = pl.BlockSpec(memory_space=pltpu.VMEM)
     return pl.pallas_call(
         attend_kernel,
-        grid_spec=pltpu.PrefetchScalarGridSpec(
-            num_scalar_prefetch=1,
-            grid=(rolls,),
-            in_specs=[row(GROUP * HD), row(HD), row(HD)]
-            + [pl.BlockSpec(t.shape, lambda i, *s: (0, 0, 0, 0)) for t in tables],
-            out_specs=row(GROUP * HD),
-            scratch_shapes=[
-                pltpu.VMEM((FAR, HD), jnp.bfloat16),
-                pltpu.VMEM((FAR, HD), jnp.bfloat16),
-            ],
-        ),
+        in_specs=[pl.BlockSpec(memory_space=pltpu.SMEM)] + [vmem] * (3 + len(tables)),
+        out_specs=vmem,
+        scratch_shapes=[
+            pltpu.VMEM((FAR, HD), jnp.bfloat16),
+            pltpu.VMEM((FAR, HD), jnp.bfloat16),
+        ],
         out_shape=jax.ShapeDtypeStruct(q.shape, jnp.bfloat16),
         compiler_params=params(48),
         cost_estimate=cost(
@@ -443,17 +442,88 @@
             out_specs=[pl.BlockSpec((hi - lo, tile), lambda j, s: (0, j)) for _, lo, hi, _ in outs],
         ),
         out_shape=[jax.ShapeDtypeStruct((hi - lo, width), dtype) for _, lo, hi, dtype in outs],
-        compiler_params=params(56),
+        compiler_params=params(53),
         cost_estimate=cost(
             4 * count * rows * depth * width, 4 * count * depth * width + 4 * count * rows * width
         ),
     )(idx, own, sib, *([w_own] * count), *([w_sib] * count), *added, *after)
 
 
+def own_term_kernel(low_rows, own_ref, sib_ref, wa_ref, wb_ref, up_ref, low_ref, top_ref, bottom_ref, w_ref, sems):
+    width = w_ref.shape[-1] // 2
+    head = lax.axis_index("head")
+    loads = []
+    for part in range(2):
+        at = pl.ds(pl.multiple_of(head * (2 * width) + part * width, width), width)
+        to = pl.ds(part * width, width)
+        for n, ref in enumerate((wa_ref, wb_ref)):
+            loads.append(pltpu.make_async_copy(ref.at[:, at], w_ref.at[n, :, to], sems.at[part, n]))
+            loads[-1].start()
+    for part in range(2):
+        for load in loads[2 * part : 2 * part + 2]:
+            load.wait()
+        to = slice(part * width, (part + 1) * width)
+        acc = jnp.dot(own_ref[...], w_ref[0, :, to], preferred_element_type=jnp.float32)
+        acc += jnp.dot(sib_ref[...], w_ref[1, :, to], preferred_element_type=jnp.float32)
+        top_ref[:, to] = acc[:low_rows] + up_ref[:, to].astype(jnp.float32)
+        bottom_ref[:, to] = acc[low_rows:] + low_ref[:, to].astype(jnp.float32)
+
+
+def own_term(own, sib, w_own, w_sib, up_top, low_bottom):
+    rows, depth = own.shape
+    half, width = up_top.shape
+    vmem = pl.BlockSpec(memory_space=pltpu.VMEM)
+    hbm = pl.BlockSpec(memory_space=pl.ANY)
+    return pl.pallas_call(
+        functools.partial(own_term_kernel, half),
+        in_specs=[vmem, vmem, hbm, hbm, vmem, vmem],
+        out_specs=[vmem, vmem],
+        out_shape=[jax.ShapeDtypeStruct((half, width), jnp.float32)] * 2,
+        scratch_shapes=[
+            pltpu.VMEM((2, depth, width), jnp.bfloat16),
+            pltpu.SemaphoreType.DMA((2, 2)),
+        ],
+        compiler_params=params(16),
+        cost_estimate=cost(4 * rows * depth * width, 4 * depth * width + 4 * rows * width),
+    )(own, sib, w_own, w_sib, up_top, low_bottom)
+
+
 def add_terms(x, *received):
     for r in received:
         x = x + r.astype(jnp.float32)
     return x.astype(jnp.bfloat16)
+
+
+def finish_kernel(mine_top, low_top, mine_bottom, up_bottom, out_ref, rows_ref, sems):
+    half = mine_top.shape[0]
+    tile = half // 2
+    stores = []
+    for n, (mine, received) in enumerate(((mine_top, low_top), (mine_bottom, up_bottom))):
+        for part in range(2):
+            rows = slice(part * tile, (part + 1) * tile)
+            to = pl.ds(n * half + part * tile, tile)
+            total = mine[rows] + received[rows].astype(jnp.float32)
+            rows_ref[to] = total.astype(jnp.bfloat16)
+            store = pltpu.make_async_copy(rows_ref.at[to], out_ref.at[to], sems.at[n, part])
+            store.start()
+            stores.append(store)
+    for store in stores:
+        store.wait()
+
+
+def finish(mine_top, low_top, mine_bottom, up_bottom):
+    vmem = pl.BlockSpec(memory_space=pltpu.VMEM)
+    half, width = mine_top.shape
+    shape = (2 * half, width)
+    return pl.pallas_call(
+        finish_kernel,
+        in_specs=[vmem] * 4,
+        out_specs=pl.BlockSpec(memory_space=pl.ANY),
+        out_shape=jax.ShapeDtypeStruct(shape, jnp.bfloat16),
+        scratch_shapes=[pltpu.VMEM(shape, jnp.bfloat16), pltpu.SemaphoreType.DMA((2, 2))],
+        compiler_params=params(16),
+        cost_estimate=cost(0, 16 * mine_top.size),
+    )(mine_top, low_top, mine_bottom, up_bottom)
 
 
 def summed(idx, own, sib, w_own, w_sib):
@@ -469,12 +539,10 @@
     next_top, next_bottom, prev_top, prev_bottom = terms(idx, 1, 2, near_outs, [], [far_top], *args)
     low_bottom = send(next_bottom, UP)
     up_top = send(prev_top, DOWN)
-    mine_outs = ((0, 0, half, f32), (0, half, rows, f32))
-    mine_top, mine_bottom = terms(idx, 3, 1, mine_outs, [up_top, low_bottom], [], *args)
+    mine_top, mine_bottom = own_term(*args, up_top, low_bottom)
     low_top = send(add_terms(next_top, via_up), UP)
     up_bottom = send(add_terms(prev_bottom, via_down), DOWN)
-    out = [add_terms(mine_top, low_top), add_terms(mine_bottom, up_bottom)]
-    return jnp.concatenate(out, axis=0)
+    return finish(mine_top, low_top, mine_bottom, up_bottom)
 
 
 def per_device(

time: 131 us -> 127 us (0.969)
  other arithmetic: 4.06 us -> 1.59 us
    pallas_call x3 -> x2, Pallas kernels: 14.6 us -> 10.5 us  [terms(): pl.pallas_call(functools.partial(terms_kernel, count, len(added), len(aft...]
    pallas_call x1 -> x3, Pallas kernels: 6.85 us -> 9.78 us  [the longest x1 6.13 us: attend(): pl.pallas_call(attend_kernel, in_specs=[pl.BlockSpec(memory_space=pltpu.S...]
    ppermute x17, waiting for transfers between devices: 30.9 us -> 33.1 us  [send(): return lax.ppermute(x, 'head', pairs)]
    all_to_all x2, waiting for transfers between devices: 4.93 us -> 2.79 us  [exchange(): return lax.all_to_all(x, 'seq', 0, 0, tiled=True)]
    convert_element_type x4 -> x2, other arithmetic: 3.02 us -> 1.59 us  [add_terms(): return x.astype(jnp.bfloat16)]
    unnamed x25 -> x31, local copies, waits for them, and re-layouts: 3.71 us -> 2.91 us
  transfers between devices with their start and end apart: 19 -> 19, of which waited for: 11 -> 11; matrix products, arithmetic and copies ran while one was open for 5% -> 4% of each run, Pallas kernels for 35% -> 34%
where the time goes in v5:
time: 127 us; the launch traced here: 126 us
  Pallas kernels  48.7 us (38%)
  waiting for transfers between devices  35.9 us (28%)
  starting transfers between devices  32.1 us (25%)
  local copies, waits for them, and re-layouts  5.98 us (5%)
  between operations  1.69 us (1%)
  other arithmetic  1.59 us (1%)
    ppermute x17, waiting for transfers between devices, send(): return lax.ppermute(x, 'head', pairs)  33.1 us
    ppermute x17, starting transfers between devices, send(): return lax.ppermute(x, 'head', pairs)  19.5 us
    pallas_call x2, Pallas kernels, project(): pl.pallas_call(functools.partial(project_kernel, plan, len(after), start...  18.6 us
    all_to_all x2, starting transfers between devices, exchange(): return lax.all_to_all(x, 'seq', 0, 0, tiled=True)  12.6 us
    pallas_call x2, Pallas kernels, terms(): pl.pallas_call(functools.partial(terms_kernel, count, len(added), len(aft...  10.5 us
    pallas_call x1, Pallas kernels, attend(): pl.pallas_call(attend_kernel, in_specs=[pl.BlockSpec(memory_space=pltpu.S...  6.13 us
    pallas_call x1, Pallas kernels, pack(): pl.pallas_call(functools.partial(pack_kernel, lo, hi), grid_spec=pltpu.Pr...  4.59 us
    pallas_call x1, Pallas kernels, pick(): pl.pallas_call(functools.partial(pick_kernel, lo, hi, len(tables) > 1), g...  4.2 us
  transfers between devices with their start and end apart: 19, of which 11 were waited for; matrix products, arithmetic and copies ran while one was open for 4% of the time, Pallas kernels for 34%

profile of v5, /device:TPU:1, one launch (start us, length us, event | category | flops | bytes accessed | tf_op | source)
XLA Modules:
  0.0 125.9 jit_solution(10764646884641874656)
XLA Ops:
  0.0 1.4 %collective-permute-start.10 = (bf16[512,8192]{1,0:T(8,128)(2,1)}, bf16[512,8192]{1,0:T(8,128)(2,1)}, u32[]{:S(2)}, u32[]{:S(2)}) collective-permute-start(bf16[512,8192]{1,0:T(8,128)(2,1)} %wa_ref.1), channel_id=1, source_target_pairs={{0,1},{1,0},{2,3},{3,2},{4,5},{5,4},{6,7},{7,6},{8,9},{9,8},{10,11... | collective-permute-start | bytes 25165832 | tf_op jit(solution)/shard_map/ppermute | solution.py:34
  1.4 2.8 %collective-permute-start.2 = (bf16[512,1024]{1,0:T(8,128)(2,1)}, bf16[512,1024]{1,0:T(8,128)(2,1)S(1)}, u32[]{:S(2)}, u32[]{:S(2)}) collective-permute-start(bf16[512,1024]{1,0:T(8,128)(2,1)} %refs_0_.3), channel_id=1, source_target_pairs={{0,6},{1,7},{2,0},{3,1},{4,2},{5,3},{6,4},{7,5},{8,14},{9,15},{10,... | collective-permute-start | bytes 3145736 | tf_op jit(solution)/shard_map/ppermute | solution.py:34
  4.2 0.8 copy.14
  5.0 0.1 reshape_reshape.3.chain_ref
  5.1 0.7 copy-done.4
  5.8 1.0 shard_map.100
  6.8 4.6 %shard_map.104 = bf16[16,9,32,128]{3,2,1,0:T(8,128)(2,1)} custom-call(s32[24,128]{1,0:T(8,128)S(1)} %get-tuple-element.129.first_ref, bf16[8,2,16,16,128]{4,3,2,1,0:T(8,128)(2,1)} %bitcast.14, bf16[8,2,16,16,128]{4,3,2,1,0:T(8,128)(2,1)} %bitcast.15, bf16[8,2,16,16,128]{4,3,2,1,0:T(8,128)(2,1)} %bitcast.20, bf16[8,2,16,16,128]{4,3,2,1,0:T(8,128)(2,1)} %bitcast.21), custom_call_target="tpu_custom_call" | custom-call | bytes 4194304 | tf_op jit(solution)/shard_map/pallas_call | solution.py:193
  11.4 7.8 %all-to-all-start.3 = ((bf16[16,9,32,128]{3,2,1,0:T(8,128)(2,1)}), bf16[16,9,32,128]{3,2,1,0:T(8,128)(2,1)}, u32[]{:S(2)}, u32[]{:S(2)}) async-start(bf16[16,9,32,128]{3,2,1,0:T(8,128)(2,1)} %shard_map.104), calls=%async_computation.3 | async-start | bytes 2359296 | tf_op jit(solution)/shard_map/all_to_all | solution.py:267
  19.2 0.6 collective-permute-start.4
  19.9 7.3 %collective-permute-done.2.refs_4_ = bf16[512,1024]{1,0:T(8,128)(2,1)S(1)} collective-permute-done((bf16[512,1024]{1,0:T(8,128)(2,1)}, bf16[512,1024]{1,0:T(8,128)(2,1)S(1)}, u32[]{:S(2)}, u32[]{:S(2)}) %collective-permute-start.2) | collective-permute-done | bytes 1048608 | tf_op jit(solution)/shard_map/ppermute | solution.py:34
  27.1 0.8 collective-permute-start.6
  27.9 2.3 %collective-permute-done.refs_2_ = bf16[512,1024]{1,0:T(8,128)(2,1)S(1)} collective-permute-done((bf16[512,1024]{1,0:T(8,128)(2,1)}, bf16[512,1024]{1,0:T(8,128)(2,1)S(1)}, u32[]{:S(2)}, u32[]{:S(2)}) %collective-permute-start) | collective-permute-done | bytes 1048608 | tf_op jit(solution)/shard_map/ppermute | solution.py:34
  30.2 1.0 collective-permute-start.5
  31.2 0.6 fusion
  32.5 0.7 dynamic-slice_bitcast_fusion.idx_ref
  33.2 0.8 slice.17
  34.0 0.8 slice.16
  34.9 2.8 %all-to-all-done.3 = bf16[16,9,32,128]{3,2,1,0:T(8,128)(2,1)} async-done(((bf16[16,9,32,128]{3,2,1,0:T(8,128)(2,1)}), bf16[16,9,32,128]{3,2,1,0:T(8,128)(2,1)}, u32[]{:S(2)}, u32[]{:S(2)}) %all-to-all-start.3) | async-done | bytes 1179680 | tf_op jit(solution)/shard_map/all_to_all | solution.py:267
  37.6 4.2 %conditional.2 = (bf16[16,13,32,128]{3,2,1,0:T(8,128)(2,1)}) conditional(s32[]{:T(128)} %bitcast.7, (s32[8,256]{1,0:T(8,128)S(1)}, bf16[16,9,32,128]{3,2,1,0:T(8,128)(2,1)}, bf16[256,1024]{1,0:T(8,128)(2,1)}, bf16[256,1024]{1,0:T(8,128)(2,1)}, s32[12]{0:T(128)S(1)}) %tuple.17, (bf16[4096,128]{1,0:T(8,128)(2,1)}, bf16[4096,128]{1,0:T(8,128)(2,1)}, ...), branch_computations={%region_0.1_spmd, %region_1.2_spmd} | conditional | bytes 10485796 | solution.py:577
  37.6 4.2 %branch_0_fun.2 = bf16[16,13,32,128]{3,2,1,0:T(8,128)(2,1)} custom-call(s32[8,256]{1,0:T(8,128)S(1)} %get-tuple-element.72.slot_ref, bf16[16,9,32,128]{3,2,1,0:T(8,128)(2,1)} %get-tuple-element.74.refs_0_, bf16[256,1024]{1,0:T(8,128)(2,1)} %get-tuple-element.75.refs_1_, bf16[256,1024]{1,0:T(8,128)(2,1)} %get-tuple-element.76.refs_2_, ...), custom_call_target="tpu_custom_call" | custom-call | bytes 2359296 | tf_op jit(solution)/shard_map/cond/branch_0_fun/pallas_call | solution.py:251
  41.8 4.9 %all-to-all-start.4 = ((bf16[16,13,32,128]{3,2,1,0:T(8,128)(2,1)}), bf16[16,13,32,128]{3,2,1,0:T(8,128)(2,1)}, u32[]{:S(2)}, u32[]{:S(2)}) async-start(bf16[16,13,32,128]{3,2,1,0:T(8,128)(2,1)} %get-tuple-element.140), calls=%async_computation.4 | async-start | bytes 3407872 | tf_op jit(solution)/shard_map/all_to_all | solution.py:267
  46.7 2.1 %collective-permute-start.3 = (bf16[256,1024]{1,0:T(8,128)(2,1)}, bf16[256,1024]{1,0:T(8,128)(2,1)}, u32[]{:S(2)}, u32[]{:S(2)}) collective-permute-start(bf16[256,1024]{1,0:T(8,128)(2,1)} %slice.17), channel_id=1, source_target_pairs={{0,6},{1,7},{2,0},{3,1},{4,2},{5,3},{6,4},{7,5},{8,14},{9,15},{10,... | collective-permute-start | bytes 1572872 | tf_op jit(solution)/shard_map/ppermute | solution.py:34
  48.8 12.0 %shard_map.101.refs_2_.refs_7_ = f32[512,768]{1,0:T(8,128)} custom-call(s32[12]{0:T(128)S(1)} %dynamic-slice_bitcast_fusion.idx_ref, bf16[512,1024]{1,0:T(8,128)(2,1)S(1)} %copy-done.2, bf16[512,1024]{1,0:T(8,128)(2,1)} %collective-permute-done.4.refs_1_, bf16[512,1024]{1,0:T(8,128)(2,1)S(1)} %collective-permute-done.refs_2_, ...), custom_call_target="tpu_custom_call" | custom-call | flops 4831838208 | bytes 15728640 | tf_op jit(solution)/shard_map/pallas_call | solution.py:320
  60.8 0.6 collective-permute-done.1.refs_0_
  61.4 3.2 %collective-permute-start.7 = (bf16[256,1024]{1,0:T(8,128)(2,1)}, bf16[256,1024]{1,0:T(8,128)(2,1)S(1)}, u32[]{:S(2)}, u32[]{:S(2)}) collective-permute-start(bf16[256,1024]{1,0:T(8,128)(2,1)} %get-tuple-element.123.refs_0_), channel_id=1, source_target_pairs={{0,1},{1,0},{2,3},{3,2},{4,5},{5,4},{6,7},{7,6},{8,9},{9,8},{10,11... | collective-permute-start | bytes 1572872 | tf_op jit(solution)/shard_map/ppermute | solution.py:34
  65.3 1.8 %collective-permute-done.7.refs_2_ = bf16[256,1024]{1,0:T(8,128)(2,1)S(1)} collective-permute-done((bf16[256,1024]{1,0:T(8,128)(2,1)}, bf16[256,1024]{1,0:T(8,128)(2,1)S(1)}, u32[]{:S(2)}, u32[]{:S(2)}) %collective-permute-start.7) | collective-permute-done | bytes 524320 | tf_op jit(solution)/shard_map/ppermute | solution.py:34
  67.1 0.2 collective-permute-done.8.refs_3_
  67.3 0.6 copy-done.13
  67.9 6.6 %shard_map.103 = (bf16[512,512]{1,0:T(8,128)(2,1)}, bf16[512,128]{1,0:T(8,128)(2,1)S(1)}, bf16[512,128]{1,0:T(8,128)(2,1)S(1)}) custom-call(s32[12]{0:T(128)S(1)} %dynamic-slice_bitcast_fusion.idx_ref, bf16[256,1024]{1,0:T(8,128)(2,1)} %get-tuple-element.123.refs_0_, bf16[256,1024]{1,0:T(8,128)(2,1)} %get-tuple-element.124.refs_1_, ...), custom_call_target="tpu_custom_call" | custom-call | flops 1610612736 | bytes 5242880 | tf_op jit(solution)/shard_map/pallas_call | solution.py:320
  74.5 6.2 %conditional.3 = (bf16[512,512]{1,0:T(8,128)(2,1)S(1)}) conditional(s32[]{:T(128)} %bitcast.5, (s32[24,128]{1,0:T(8,128)S(1)}, bf16[512,512]{1,0:T(8,128)(2,1)}, bf16[512,128]{1,0:T(8,128)(2,1)S(1)}, bf16[512,128]{1,0:T(8,128)(2,1)S(1)}, bf16[16,13,32,128]{3,2,1,0:T(8,128)(2,1)}) %tuple.19, (bf16[4096,128]{1,0:T(8,128)(2,1)S(1)}, ...), branch_computations={%region_2.3_spmd, %region_3.4_spmd} | conditional | flops 1207959552 | bytes 15728676 | solution.py:598
  74.5 6.1 %branch_0_fun.3 = bf16[512,512]{1,0:T(8,128)(2,1)S(1)} custom-call(s32[24,128]{1,0:T(8,128)S(1)} %get-tuple-element.86.slot_ref, bf16[512,512]{1,0:T(8,128)(2,1)} %get-tuple-element.87.q_ref, bf16[512,128]{1,0:T(8,128)(2,1)S(1)} %get-tuple-element.88.k_ref, bf16[512,128]{1,0:T(8,128)(2,1)S(1)} %get-tuple-element.89.v_ref, ...), custom_call_target="tpu_custom_call" | custom-call | flops 1207959552 | bytes 4456448 | tf_op jit(solution)/shard_map/cond/branch_0_fun/pallas_call | solution.py:396
  80.7 0.5 collective-permute-start.9
  81.1 1.5 %collective-permute-done.9.b_ref.sib_ref = bf16[512,512]{1,0:T(8,128)(2,1)S(1)} collective-permute-done((bf16[512,512]{1,0:T(8,128)(2,1)S(1)}, bf16[512,512]{1,0:T(8,128)(2,1)S(1)}, u32[]{:S(2)}, u32[]{:S(2)}) %collective-permute-start.9) | collective-permute-done | bytes 524320 | tf_op jit(solution)/shard_map/ppermute | solution.py:34
  82.7 0.8 copy-done
  83.5 4.4 %shard_map.105 = (bf16[256,1024]{1,0:T(8,128)(2,1)S(1)}, bf16[256,1024]{1,0:T(8,128)(2,1)}) custom-call(s32[12]{0:T(128)S(1)} %dynamic-slice_bitcast_fusion.idx_ref, bf16[512,512]{1,0:T(8,128)(2,1)S(1)} %get-tuple-element.141.a_ref.own_ref, bf16[512,512]{1,0:T(8,128)(2,1)} %copy-done, bf16[512,8192]{1,0:T(8,128)(2,1)} %wa_ref.1, ...), custom_call_target="tpu_custom_call" | custom-call | flops 1073741824 | bytes 4194304 | tf_op jit(solution)/shard_map/pallas_call | solution.py:433
  87.9 2.7 %collective-permute-start.15 = (bf16[256,1024]{1,0:T(8,128)(2,1)}, bf16[256,1024]{1,0:T(8,128)(2,1)S(1)}, u32[]{:S(2)}, u32[]{:S(2)}) collective-permute-start(bf16[256,1024]{1,0:T(8,128)(2,1)} %get-tuple-element.137), channel_id=1, source_target_pairs={{0,6},{1,7},{2,0},{3,1},{4,2},{5,3},{6,4},{7,5},{8,14},{9,15},{10,... | collective-permute-start | bytes 1572872 | tf_op jit(solution)/shard_map/ppermute | solution.py:34
  90.6 6.1 %shard_map.106 = (f32[256,1024]{1,0:T(8,128)}, bf16[256,1024]{1,0:T(8,128)(2,1)S(1)}, bf16[256,1024]{1,0:T(8,128)(2,1)}, f32[256,1024]{1,0:T(8,128)}) custom-call(s32[12]{0:T(128)S(1)} %dynamic-slice_bitcast_fusion.idx_ref, bf16[512,512]{1,0:T(8,128)(2,1)} %copy-done.10, bf16[512,512]{1,0:T(8,128)(2,1)} %copy-done, bf16[512,8192]{1,0:T(8,128)(2,1)} %wa_ref.1, ...), custom_call_target="tpu_custom_call" | custom-call | flops 2147483648 | bytes 8388608 | tf_op jit(solution)/shard_map/pallas_call | solution.py:433
  96.7 0.3 collective-permute-start.11
  97.0 1.2 collective-permute-start.12
  98.2 4.0 %collective-permute-done.13 = bf16[256,1024]{1,0:T(8,128)(2,1)S(1)} collective-permute-done((bf16[256,1024]{1,0:T(8,128)(2,1)S(1)}, bf16[256,1024]{1,0:T(8,128)(2,1)S(1)}, u32[]{:S(2)}, u32[]{:S(2)}) %collective-permute-start.13) | collective-permute-done | bytes 524320 | tf_op jit(solution)/shard_map/ppermute | solution.py:34
  102.3 1.5 %add_convert_fusion.1 = bf16[256,1024]{1,0:T(8,128)(2,1)S(1)} fusion(f32[256,1024]{1,0:T(8,128)} %get-tuple-element.134, bf16[256,1024]{1,0:T(8,128)(2,1)S(1)} %collective-permute-done.13), kind=kLoop, calls=%fused_computation.1 | loop fusion | flops 786432 | bytes 2097152 | tf_op jit(solution)/shard_map/convert_element_type | solution.py:494
  103.8 0.1 add_convert_fusion
  104.0 2.7 %collective-permute-start.16 = (bf16[256,1024]{1,0:T(8,128)(2,1)S(1)}, bf16[256,1024]{1,0:T(8,128)(2,1)S(1)}, u32[]{:S(2)}, u32[]{:S(2)}) collective-permute-start(bf16[256,1024]{1,0:T(8,128)(2,1)S(1)} %add_convert_fusion), channel_id=1, source_target_pairs={{0,6},{1,7},{2,0},{3,1},{4,2},{5,3},{6,4},{7,5},{8,14},{9,15},{10,... | collective-permute-start | bytes 1572872 | tf_op jit(solution)/shard_map/ppermute | solution.py:34
  106.7 6.1 %collective-permute-done.11.up_ref = bf16[256,1024]{1,0:T(8,128)(2,1)S(1)} collective-permute-done((bf16[256,1024]{1,0:T(8,128)(2,1)}, bf16[256,1024]{1,0:T(8,128)(2,1)S(1)}, u32[]{:S(2)}, u32[]{:S(2)}) %collective-permute-start.11) | collective-permute-done | bytes 524320 | tf_op jit(solution)/shard_map/ppermute | solution.py:34
  112.8 0.7 collective-permute-done.12.low_ref
  113.5 2.6 %shard_map.107 = (f32[256,1024]{1,0:T(8,128)S(1)}, f32[256,1024]{1,0:T(8,128)S(1)}) custom-call(bf16[512,512]{1,0:T(8,128)(2,1)S(1)} %copy-done.11, bf16[512,512]{1,0:T(8,128)(2,1)S(1)} %copy-done.1, bf16[512,8192]{1,0:T(8,128)(2,1)S(1)} %bitcast.12, bf16[512,8192]{1,0:T(8,128)(2,1)} %collective-permute-done.10.refs_1_.refs_2_.refs_3_.wb_ref, ...), custom_call_target="tpu_custom_call" | custom-call | flops 1073741824 | bytes 4194304 | tf_op jit(solution)/shard_map/pallas_call | solution.py:477
  116.1 8.6 %collective-permute-done.14.low_top = bf16[256,1024]{1,0:T(8,128)(2,1)S(1)} collective-permute-done((bf16[256,1024]{1,0:T(8,128)(2,1)S(1)}, bf16[256,1024]{1,0:T(8,128)(2,1)S(1)}, u32[]{:S(2)}, u32[]{:S(2)}) %collective-permute-start.14) | collective-permute-done | bytes 524320 | tf_op jit(solution)/shard_map/ppermute | solution.py:34
  124.7 1.0 shard_map.108
  (42 shorter events, 0.2 us)
Async XLA Ops:
  0.0 82.7 %collective-permute-start.10 = (bf16[512,8192]{1,0:T(8,128)(2,1)}, bf16[512,8192]{1,0:T(8,128)(2,1)}, u32[]{:S(2)}, u32[]{:S(2)}) collective-permute-start(bf16[512,8192]{1,0:T(8,128)(2,1)} %wa_ref.1), channel_id=1, source_target_pairs={{0,1},{1,0},{2,3},{3,2},{4,5},{5,4},{6,7},{7,6},{8,9},{9,8},{10,11... | collective-permute-start | bytes 25165832 | tf_op jit(solution)/shard_map/ppermute | solution.py:34
  1.4 25.7 %collective-permute-start.2 = (bf16[512,1024]{1,0:T(8,128)(2,1)}, bf16[512,1024]{1,0:T(8,128)(2,1)S(1)}, u32[]{:S(2)}, u32[]{:S(2)}) collective-permute-start(bf16[512,1024]{1,0:T(8,128)(2,1)} %refs_0_.3), channel_id=1, source_target_pairs={{0,6},{1,7},{2,0},{3,1},{4,2},{5,3},{6,4},{7,5},{8,14},{9,15},{10,... | collective-permute-start | bytes 3145736 | tf_op jit(solution)/shard_map/ppermute | solution.py:34
  4.2 26.0 %collective-permute-start = (bf16[512,1024]{1,0:T(8,128)(2,1)}, bf16[512,1024]{1,0:T(8,128)(2,1)S(1)}, u32[]{:S(2)}, u32[]{:S(2)}) collective-permute-start(bf16[512,1024]{1,0:T(8,128)(2,1)} %refs_0_.3), channel_id=1, source_target_pairs={{0,2},{1,3},{2,4},{3,5},{4,6},{5,7},{6,0},{7,1},{8,10},{9,11},{10,... | collective-permute-start | bytes 3145736 | tf_op jit(solution)/shard_map/ppermute | solution.py:34
  5.1 0.7 copy-start.4
  11.4 7.8 %copy-start.2 = (bf16[512,1024]{1,0:T(8,128)(2,1)S(1)}, bf16[512,1024]{1,0:T(8,128)(2,1)}, u32[]{:S(2)}) copy-start(bf16[512,1024]{1,0:T(8,128)(2,1)} %refs_0_.3) | copy-start | bytes 3145732
  11.4 26.2 %all-to-all-start.3 = ((bf16[16,9,32,128]{3,2,1,0:T(8,128)(2,1)}), bf16[16,9,32,128]{3,2,1,0:T(8,128)(2,1)}, u32[]{:S(2)}, u32[]{:S(2)}) async-start(bf16[16,9,32,128]{3,2,1,0:T(8,128)(2,1)} %shard_map.104), calls=%async_computation.3 | async-start | bytes 2359296 | tf_op jit(solution)/shard_map/all_to_all | solution.py:267
  19.2 29.6 %collective-permute-start.4 = (bf16[512,1024]{1,0:T(8,128)(2,1)S(1)}, bf16[512,1024]{1,0:T(8,128)(2,1)}, u32[]{:S(2)}, u32[]{:S(2)}) collective-permute-start(bf16[512,1024]{1,0:T(8,128)(2,1)S(1)} %copy-done.2), channel_id=1, source_target_pairs={{0,1},{1,0},{2,3},{3,2},{4,5},{5,4},{6,7},{7,6},{8,9},{9,8},{10,11... | collective-permute-start | bytes 3145736 | tf_op jit(solution)/shard_map/ppermute | solution.py:34
  27.1 21.6 %collective-permute-start.6 = (bf16[512,1024]{1,0:T(8,128)(2,1)S(1)}, bf16[512,1024]{1,0:T(8,128)(2,1)}, u32[]{:S(2)}, u32[]{:S(2)}) collective-permute-start(bf16[512,1024]{1,0:T(8,128)(2,1)S(1)} %collective-permute-done.2.refs_4_), channel_id=1, source_target_pairs={{0,1},{1,0},{2,3},{3,2},{4,5},{5,4},{6,7},{7,6},{8,9},{9,8},{10,11... | collective-permute-start | bytes 3145736 | tf_op jit(solution)/shard_map/ppermute | solution.py:34
  30.2 18.5 %collective-permute-start.5 = (bf16[512,1024]{1,0:T(8,128)(2,1)S(1)}, bf16[512,1024]{1,0:T(8,128)(2,1)}, u32[]{:S(2)}, u32[]{:S(2)}) collective-permute-start(bf16[512,1024]{1,0:T(8,128)(2,1)S(1)} %collective-permute-done.refs_2_), channel_id=1, source_target_pairs={{0,1},{1,0},{2,3},{3,2},{4,5},{5,4},{6,7},{7,6},{8,9},{9,8},{10,11... | collective-permute-start | bytes 3145736 | tf_op jit(solution)/shard_map/ppermute | solution.py:34
  41.8 32.6 %all-to-all-start.4 = ((bf16[16,13,32,128]{3,2,1,0:T(8,128)(2,1)}), bf16[16,13,32,128]{3,2,1,0:T(8,128)(2,1)}, u32[]{:S(2)}, u32[]{:S(2)}) async-start(bf16[16,13,32,128]{3,2,1,0:T(8,128)(2,1)} %get-tuple-element.140), calls=%async_computation.4 | async-start | bytes 3407872 | tf_op jit(solution)/shard_map/all_to_all | solution.py:267
  46.7 14.1 %collective-permute-start.3 = (bf16[256,1024]{1,0:T(8,128)(2,1)}, bf16[256,1024]{1,0:T(8,128)(2,1)}, u32[]{:S(2)}, u32[]{:S(2)}) collective-permute-start(bf16[256,1024]{1,0:T(8,128)(2,1)} %slice.17), channel_id=1, source_target_pairs={{0,6},{1,7},{2,0},{3,1},{4,2},{5,3},{6,4},{7,5},{8,14},{9,15},{10,... | collective-permute-start | bytes 1572872 | tf_op jit(solution)/shard_map/ppermute | solution.py:34
  48.8 12.6 %collective-permute-start.1 = (bf16[256,1024]{1,0:T(8,128)(2,1)}, bf16[256,1024]{1,0:T(8,128)(2,1)}, u32[]{:S(2)}, u32[]{:S(2)}) collective-permute-start(bf16[256,1024]{1,0:T(8,128)(2,1)} %slice.16), channel_id=1, source_target_pairs={{0,2},{1,3},{2,4},{3,5},{4,6},{5,7},{6,0},{7,1},{8,10},{9,11},{10,... | collective-permute-start | bytes 1572872 | tf_op jit(solution)/shard_map/ppermute | solution.py:34
  61.4 5.7 %collective-permute-start.7 = (bf16[256,1024]{1,0:T(8,128)(2,1)}, bf16[256,1024]{1,0:T(8,128)(2,1)S(1)}, u32[]{:S(2)}, u32[]{:S(2)}) collective-permute-start(bf16[256,1024]{1,0:T(8,128)(2,1)} %get-tuple-element.123.refs_0_), channel_id=1, source_target_pairs={{0,1},{1,0},{2,3},{3,2},{4,5},{5,4},{6,7},{7,6},{8,9},{9,8},{10,11... | collective-permute-start | bytes 1572872 | tf_op jit(solution)/shard_map/ppermute | solution.py:34
  64.6 2.6 %collective-permute-start.8 = (bf16[256,1024]{1,0:T(8,128)(2,1)}, bf16[256,1024]{1,0:T(8,128)(2,1)}, u32[]{:S(2)}, u32[]{:S(2)}) collective-permute-start(bf16[256,1024]{1,0:T(8,128)(2,1)} %get-tuple-element.124.refs_1_), channel_id=1, source_target_pairs={{0,1},{1,0},{2,3},{3,2},{4,5},{5,4},{6,7},{7,6},{8,9},{9,8},{10,11... | collective-permute-start | bytes 1572872 | tf_op jit(solution)/shard_map/ppermute | solution.py:34
  65.3 9.2 %copy-start.5 = (bf16[4096,128]{1,0:T(8,128)(2,1)S(1)}, bf16[4096,128]{1,0:T(8,128)(2,1)}, u32[]{:S(2)}) copy-start(bf16[4096,128]{1,0:T(8,128)(2,1)} %param.19) | copy-start | bytes 3145732
  65.3 9.2 %copy-start.6 = (bf16[4096,128]{1,0:T(8,128)(2,1)S(1)}, bf16[4096,128]{1,0:T(8,128)(2,1)}, u32[]{:S(2)}) copy-start(bf16[4096,128]{1,0:T(8,128)(2,1)} %param.20) | copy-start | bytes 3145732
  65.3 9.2 %copy-start.7 = (bf16[256,1024]{1,0:T(8,128)(2,1)S(1)}, bf16[256,1024]{1,0:T(8,128)(2,1)}, u32[]{:S(2)}) copy-start(bf16[256,1024]{1,0:T(8,128)(2,1)} %slice.17) | copy-start | bytes 1572868
  65.3 9.2 %copy-start.9 = (bf16[256,1024]{1,0:T(8,128)(2,1)S(1)}, bf16[256,1024]{1,0:T(8,128)(2,1)}, u32[]{:S(2)}) copy-start(bf16[256,1024]{1,0:T(8,128)(2,1)} %slice.16) | copy-start | bytes 1572868
  67.1 0.8 copy-start.13
  80.7 7.2 %copy-start.10 = (bf16[512,512]{1,0:T(8,128)(2,1)}, bf16[512,512]{1,0:T(8,128)(2,1)S(1)}, u32[]{:S(2)}) copy-start(bf16[512,512]{1,0:T(8,128)(2,1)S(1)} %get-tuple-element.141.a_ref.own_ref) | copy-start | bytes 1572868
  80.7 2.0 %collective-permute-start.9 = (bf16[512,512]{1,0:T(8,128)(2,1)S(1)}, bf16[512,512]{1,0:T(8,128)(2,1)S(1)}, u32[]{:S(2)}, u32[]{:S(2)}) collective-permute-start(bf16[512,512]{1,0:T(8,128)(2,1)S(1)} %get-tuple-element.141.a_ref.own_ref), channel_id=1, source_target_pairs={{0,1},{1,0},{2,3},{3,2},{4,5},{5,4},{6,7},{7,6},{8,9},{9,8},{10,11... | collective-permute-start | bytes 1572872 | tf_op jit(solution)/shard_map/ppermute | solution.py:34
  82.7 0.8 copy-start
  83.5 30.0 %slice-start = ((s8[8388608]{0:T(1024)(128)(4,1)}), s8[4194304]{0:T(1024)(128)(4,1)S(1)}, s32[]{:S(2)}) async-start(s8[8388608]{0:T(1024)(128)(4,1)} %bitcast.11), calls=%async_computation.5 | async-start | bytes 8388608
  87.9 2.7 %copy-start.3 = (bf16[256,1024]{1,0:T(8,128)(2,1)}, bf16[256,1024]{1,0:T(8,128)(2,1)S(1)}, u32[]{:S(2)}) copy-start(bf16[256,1024]{1,0:T(8,128)(2,1)S(1)} %get-tuple-element.130.refs_4_) | copy-start | bytes 1572868
  87.9 14.4 %collective-permute-start.13 = (bf16[256,1024]{1,0:T(8,128)(2,1)S(1)}, bf16[256,1024]{1,0:T(8,128)(2,1)S(1)}, u32[]{:S(2)}, u32[]{:S(2)}) collective-permute-start(bf16[256,1024]{1,0:T(8,128)(2,1)S(1)} %get-tuple-element.130.refs_4_), channel_id=1, source_target_pairs={{0,2},{1,3},{2,4},{3,5},{4,6},{5,7},{6,0},{7,1},{8,10},{9,11},{10,... | collective-permute-start | bytes 1572872 | tf_op jit(solution)/shard_map/ppermute | solution.py:34
  87.9 25.6 %slice-start.1 = ((s8[8388608]{0:T(1024)(128)(4,1)}), s8[4194304]{0:T(1024)(128)(4,1)S(1)}, s32[]{:S(2)}) async-start(s8[8388608]{0:T(1024)(128)(4,1)} %bitcast.11), calls=%async_computation.6 | async-start | bytes 8388608
  87.9 15.9 %collective-permute-start.15 = (bf16[256,1024]{1,0:T(8,128)(2,1)}, bf16[256,1024]{1,0:T(8,128)(2,1)S(1)}, u32[]{:S(2)}, u32[]{:S(2)}) collective-permute-start(bf16[256,1024]{1,0:T(8,128)(2,1)} %get-tuple-element.137), channel_id=1, source_target_pairs={{0,6},{1,7},{2,0},{3,1},{4,2},{5,3},{6,4},{7,5},{8,14},{9,15},{10,... | collective-permute-start | bytes 1572872 | tf_op jit(solution)/shard_map/ppermute | solution.py:34
  96.7 7.1 %copy-start.12 = (f32[256,1024]{1,0:T(8,128)S(1)}, f32[256,1024]{1,0:T(8,128)}, u32[]{:S(2)}) copy-start(f32[256,1024]{1,0:T(8,128)} %get-tuple-element.136) | copy-start | bytes 3145732
  96.7 16.1 %collective-permute-start.11 = (bf16[256,1024]{1,0:T(8,128)(2,1)}, bf16[256,1024]{1,0:T(8,128)(2,1)S(1)}, u32[]{:S(2)}, u32[]{:S(2)}) collective-permute-start(bf16[256,1024]{1,0:T(8,128)(2,1)} %get-tuple-element.131), channel_id=1, source_target_pairs={{0,6},{1,7},{2,0},{3,1},{4,2},{5,3},{6,4},{7,5},{8,14},{9,15},{10,... | collective-permute-start | bytes 1572872 | tf_op jit(solution)/shard_map/ppermute | solution.py:34
  97.0 16.5 %collective-permute-start.12 = (bf16[256,1024]{1,0:T(8,128)(2,1)S(1)}, bf16[256,1024]{1,0:T(8,128)(2,1)S(1)}, u32[]{:S(2)}, u32[]{:S(2)}) collective-permute-start(bf16[256,1024]{1,0:T(8,128)(2,1)S(1)} %get-tuple-element.132), channel_id=1, source_target_pairs={{0,2},{1,3},{2,4},{3,5},{4,6},{5,7},{6,0},{7,1},{8,10},{9,11},{10,... | collective-permute-start | bytes 1572872 | tf_op jit(solution)/shard_map/ppermute | solution.py:34
  102.3 11.2 %copy-start.1 = (bf16[512,512]{1,0:T(8,128)(2,1)S(1)}, bf16[512,512]{1,0:T(8,128)(2,1)}, u32[]{:S(2)}) copy-start(bf16[512,512]{1,0:T(8,128)(2,1)} %copy-done) | copy-start | bytes 1572868
  102.3 11.2 %copy-start.11 = (bf16[512,512]{1,0:T(8,128)(2,1)S(1)}, bf16[512,512]{1,0:T(8,128)(2,1)}, u32[]{:S(2)}) copy-start(bf16[512,512]{1,0:T(8,128)(2,1)} %copy-done.10) | copy-start | bytes 1572868
  103.7 21.0 %collective-permute-start.14 = (bf16[256,1024]{1,0:T(8,128)(2,1)S(1)}, bf16[256,1024]{1,0:T(8,128)(2,1)S(1)}, u32[]{:S(2)}, u32[]{:S(2)}) collective-permute-start(bf16[256,1024]{1,0:T(8,128)(2,1)S(1)} %add_convert_fusion.1), channel_id=1, source_target_pairs={{0,2},{1,3},{2,4},{3,5},{4,6},{5,7},{6,0},{7,1},{8,10},{9,11},{10,... | collective-permute-start | bytes 1572872 | tf_op jit(solution)/shard_map/ppermute | solution.py:34
  104.0 20.8 %collective-permute-start.16 = (bf16[256,1024]{1,0:T(8,128)(2,1)S(1)}, bf16[256,1024]{1,0:T(8,128)(2,1)S(1)}, u32[]{:S(2)}, u32[]{:S(2)}) collective-permute-start(bf16[256,1024]{1,0:T(8,128)(2,1)S(1)} %add_convert_fusion), channel_id=1, source_target_pairs={{0,6},{1,7},{2,0},{3,1},{4,2},{5,3},{6,4},{7,5},{8,14},{9,15},{10,... | collective-permute-start | bytes 1572872 | tf_op jit(solution)/shard_map/ppermute | solution.py:34

commit v6 on v5

--- a/solution.py
+++ b/solution.py
@@ -285,9 +285,10 @@
 
         @pl.when(step == s)
         def _():
+            w_kv = jnp.concatenate([wk[...], wv[...]], axis=1)
             for (lo, hi), x in zip(pieces, mine):
-                for w, c, n in ((wq, 0, nq), (wk, nq, nk), (wv, nq + nk, nk)):
-                    d = jnp.dot(x[...], w[...], preferred_element_type=jnp.float32)
+                for w, c, n in ((wq[...], 0, nq), (w_kv, nq, 2 * nk)):
+                    d = jnp.dot(x[...], w, preferred_element_type=jnp.float32)
                     if s == 0 and has_acc:
                         acc[lo:hi, c : c + n] = start[lo:hi, c : c + n] + d
                     elif s == 0:

time: 127 us -> 126 us (level)
  Pallas kernels: 48.7 us -> 47.1 us
    pallas_call x2, Pallas kernels: 18.6 us -> 17 us  [project(): pl.pallas_call(functools.partial(project_kernel, plan, len(after), start...]
  transfers between devices with their start and end apart: 19 -> 19, of which waited for: 11 -> 11; matrix products, arithmetic and copies ran while one was open for 4% -> 4% of each run, Pallas kernels for 34% -> 33%
where the time goes in v6:
time: 126 us; the launch traced here: 125 us
  Pallas kernels  47.1 us (37%)
  waiting for transfers between devices  36.9 us (29%)
  starting transfers between devices  32.1 us (25%)
  local copies, waits for them, and re-layouts  5.98 us (5%)
  between operations  1.69 us (1%)
  other arithmetic  1.59 us (1%)
    ppermute x17, waiting for transfers between devices, send(): return lax.ppermute(x, 'head', pairs)  34.1 us
    ppermute x17, starting transfers between devices, send(): return lax.ppermute(x, 'head', pairs)  19.5 us
    pallas_call x2, Pallas kernels, project(): pl.pallas_call(functools.partial(project_kernel, plan, len(after), start...  17 us
    all_to_all x2, starting transfers between devices, exchange(): return lax.all_to_all(x, 'seq', 0, 0, tiled=True)  12.6 us
    pallas_call x2, Pallas kernels, terms(): pl.pallas_call(functools.partial(terms_kernel, count, len(added), len(aft...  10.5 us
    pallas_call x1, Pallas kernels, attend(): pl.pallas_call(attend_kernel, in_specs=[pl.BlockSpec(memory_space=pltpu.S...  6.12 us
    pallas_call x1, Pallas kernels, pack(): pl.pallas_call(functools.partial(pack_kernel, lo, hi), grid_spec=pltpu.Pr...  4.59 us
    pallas_call x1, Pallas kernels, pick(): pl.pallas_call(functools.partial(pick_kernel, lo, hi, len(tables) > 1), g...  4.2 us
  transfers between devices with their start and end apart: 19, of which 11 were waited for; matrix products, arithmetic and copies ran while one was open for 4% of the time, Pallas kernels for 33%

profile of v6, /device:TPU:1, one launch (start us, length us, event | category | flops | bytes accessed | tf_op | source)
XLA Modules:
  0.0 125.4 jit_solution(7397337529075407174)
XLA Ops:
  0.0 1.4 %collective-permute-start.10 = (bf16[512,8192]{1,0:T(8,128)(2,1)}, bf16[512,8192]{1,0:T(8,128)(2,1)}, u32[]{:S(2)}, u32[]{:S(2)}) collective-permute-start(bf16[512,8192]{1,0:T(8,128)(2,1)} %wa_ref.1), channel_id=1, source_target_pairs={{0,1},{1,0},{2,3},{3,2},{4,5},{5,4},{6,7},{7,6},{8,9},{9,8},{10,11... | collective-permute-start | bytes 25165832 | tf_op jit(solution)/shard_map/ppermute | solution.py:34
  1.4 2.8 %collective-permute-start.2 = (bf16[512,1024]{1,0:T(8,128)(2,1)}, bf16[512,1024]{1,0:T(8,128)(2,1)S(1)}, u32[]{:S(2)}, u32[]{:S(2)}) collective-permute-start(bf16[512,1024]{1,0:T(8,128)(2,1)} %refs_0_.3), channel_id=1, source_target_pairs={{0,6},{1,7},{2,0},{3,1},{4,2},{5,3},{6,4},{7,5},{8,14},{9,15},{10,... | collective-permute-start | bytes 3145736 | tf_op jit(solution)/shard_map/ppermute | solution.py:34
  4.2 0.8 copy.14
  5.0 0.1 reshape_reshape.3.chain_ref
  5.1 0.7 copy-done.4
  5.8 1.0 shard_map.100
  6.8 4.6 %shard_map.104 = bf16[16,9,32,128]{3,2,1,0:T(8,128)(2,1)} custom-call(s32[24,128]{1,0:T(8,128)S(1)} %get-tuple-element.129.first_ref, bf16[8,2,16,16,128]{4,3,2,1,0:T(8,128)(2,1)} %bitcast.14, bf16[8,2,16,16,128]{4,3,2,1,0:T(8,128)(2,1)} %bitcast.15, bf16[8,2,16,16,128]{4,3,2,1,0:T(8,128)(2,1)} %bitcast.20, bf16[8,2,16,16,128]{4,3,2,1,0:T(8,128)(2,1)} %bitcast.21), custom_call_target="tpu_custom_call" | custom-call | bytes 4194304 | tf_op jit(solution)/shard_map/pallas_call | solution.py:193
  11.4 7.8 %all-to-all-start.3 = ((bf16[16,9,32,128]{3,2,1,0:T(8,128)(2,1)}), bf16[16,9,32,128]{3,2,1,0:T(8,128)(2,1)}, u32[]{:S(2)}, u32[]{:S(2)}) async-start(bf16[16,9,32,128]{3,2,1,0:T(8,128)(2,1)} %shard_map.104), calls=%async_computation.3 | async-start | bytes 2359296 | tf_op jit(solution)/shard_map/all_to_all | solution.py:267
  19.2 0.6 collective-permute-start.4
  19.9 7.3 %collective-permute-done.2.refs_4_ = bf16[512,1024]{1,0:T(8,128)(2,1)S(1)} collective-permute-done((bf16[512,1024]{1,0:T(8,128)(2,1)}, bf16[512,1024]{1,0:T(8,128)(2,1)S(1)}, u32[]{:S(2)}, u32[]{:S(2)}) %collective-permute-start.2) | collective-permute-done | bytes 1048608 | tf_op jit(solution)/shard_map/ppermute | solution.py:34
  27.1 0.8 collective-permute-start.6
  27.9 2.3 %collective-permute-done.refs_2_ = bf16[512,1024]{1,0:T(8,128)(2,1)S(1)} collective-permute-done((bf16[512,1024]{1,0:T(8,128)(2,1)}, bf16[512,1024]{1,0:T(8,128)(2,1)S(1)}, u32[]{:S(2)}, u32[]{:S(2)}) %collective-permute-start) | collective-permute-done | bytes 1048608 | tf_op jit(solution)/shard_map/ppermute | solution.py:34
  30.2 1.0 collective-permute-start.5
  31.2 0.6 fusion
  32.5 0.7 dynamic-slice_bitcast_fusion.idx_ref
  33.2 0.8 slice.17
  34.0 0.8 slice.16
  34.9 2.8 %all-to-all-done.3 = bf16[16,9,32,128]{3,2,1,0:T(8,128)(2,1)} async-done(((bf16[16,9,32,128]{3,2,1,0:T(8,128)(2,1)}), bf16[16,9,32,128]{3,2,1,0:T(8,128)(2,1)}, u32[]{:S(2)}, u32[]{:S(2)}) %all-to-all-start.3) | async-done | bytes 1179680 | tf_op jit(solution)/shard_map/all_to_all | solution.py:267
  37.6 4.2 %conditional.2 = (bf16[16,13,32,128]{3,2,1,0:T(8,128)(2,1)}) conditional(s32[]{:T(128)} %bitcast.7, (s32[8,256]{1,0:T(8,128)S(1)}, bf16[16,9,32,128]{3,2,1,0:T(8,128)(2,1)}, bf16[256,1024]{1,0:T(8,128)(2,1)}, bf16[256,1024]{1,0:T(8,128)(2,1)}, s32[12]{0:T(128)S(1)}) %tuple.17, (bf16[4096,128]{1,0:T(8,128)(2,1)}, bf16[4096,128]{1,0:T(8,128)(2,1)}, ...), branch_computations={%region_0.1_spmd, %region_1.2_spmd} | conditional | bytes 10485796 | solution.py:578
  37.6 4.2 %branch_0_fun.2 = bf16[16,13,32,128]{3,2,1,0:T(8,128)(2,1)} custom-call(s32[8,256]{1,0:T(8,128)S(1)} %get-tuple-element.72.slot_ref, bf16[16,9,32,128]{3,2,1,0:T(8,128)(2,1)} %get-tuple-element.74.refs_0_, bf16[256,1024]{1,0:T(8,128)(2,1)} %get-tuple-element.75.refs_1_, bf16[256,1024]{1,0:T(8,128)(2,1)} %get-tuple-element.76.refs_2_, ...), custom_call_target="tpu_custom_call" | custom-call | bytes 2359296 | tf_op jit(solution)/shard_map/cond/branch_0_fun/pallas_call | solution.py:251
  41.8 4.9 %all-to-all-start.4 = ((bf16[16,13,32,128]{3,2,1,0:T(8,128)(2,1)}), bf16[16,13,32,128]{3,2,1,0:T(8,128)(2,1)}, u32[]{:S(2)}, u32[]{:S(2)}) async-start(bf16[16,13,32,128]{3,2,1,0:T(8,128)(2,1)} %get-tuple-element.140), calls=%async_computation.4 | async-start | bytes 3407872 | tf_op jit(solution)/shard_map/all_to_all | solution.py:267
  46.7 2.1 %collective-permute-start.3 = (bf16[256,1024]{1,0:T(8,128)(2,1)}, bf16[256,1024]{1,0:T(8,128)(2,1)}, u32[]{:S(2)}, u32[]{:S(2)}) collective-permute-start(bf16[256,1024]{1,0:T(8,128)(2,1)} %slice.17), channel_id=1, source_target_pairs={{0,6},{1,7},{2,0},{3,1},{4,2},{5,3},{6,4},{7,5},{8,14},{9,15},{10,... | collective-permute-start | bytes 1572872 | tf_op jit(solution)/shard_map/ppermute | solution.py:34
  48.8 11.0 %shard_map.101.refs_2_.refs_7_ = f32[512,768]{1,0:T(8,128)} custom-call(s32[12]{0:T(128)S(1)} %dynamic-slice_bitcast_fusion.idx_ref, bf16[512,1024]{1,0:T(8,128)(2,1)S(1)} %copy-done.2, bf16[512,1024]{1,0:T(8,128)(2,1)} %collective-permute-done.4.refs_1_, bf16[512,1024]{1,0:T(8,128)(2,1)S(1)} %collective-permute-done.refs_2_, ...), custom_call_target="tpu_custom_call" | custom-call | flops 4831838208 | bytes 15728640 | tf_op jit(solution)/shard_map/pallas_call | solution.py:321
  59.8 1.6 %collective-permute-done.1.refs_0_ = bf16[256,1024]{1,0:T(8,128)(2,1)} collective-permute-done((bf16[256,1024]{1,0:T(8,128)(2,1)}, bf16[256,1024]{1,0:T(8,128)(2,1)}, u32[]{:S(2)}, u32[]{:S(2)}) %collective-permute-start.1) | collective-permute-done | bytes 524320 | tf_op jit(solution)/shard_map/ppermute | solution.py:34
  61.4 3.2 %collective-permute-start.7 = (bf16[256,1024]{1,0:T(8,128)(2,1)}, bf16[256,1024]{1,0:T(8,128)(2,1)S(1)}, u32[]{:S(2)}, u32[]{:S(2)}) collective-permute-start(bf16[256,1024]{1,0:T(8,128)(2,1)} %get-tuple-element.123.refs_0_), channel_id=1, source_target_pairs={{0,1},{1,0},{2,3},{3,2},{4,5},{5,4},{6,7},{7,6},{8,9},{9,8},{10,11... | collective-permute-start | bytes 1572872 | tf_op jit(solution)/shard_map/ppermute | solution.py:34
  65.3 1.8 %collective-permute-done.7.refs_2_ = bf16[256,1024]{1,0:T(8,128)(2,1)S(1)} collective-permute-done((bf16[256,1024]{1,0:T(8,128)(2,1)}, bf16[256,1024]{1,0:T(8,128)(2,1)S(1)}, u32[]{:S(2)}, u32[]{:S(2)}) %collective-permute-start.7) | collective-permute-done | bytes 524320 | tf_op jit(solution)/shard_map/ppermute | solution.py:34
  67.1 0.2 collective-permute-done.8.refs_3_
  67.3 0.6 copy-done.13
  67.9 6.0 %shard_map.103 = (bf16[512,512]{1,0:T(8,128)(2,1)}, bf16[512,128]{1,0:T(8,128)(2,1)S(1)}, bf16[512,128]{1,0:T(8,128)(2,1)S(1)}) custom-call(s32[12]{0:T(128)S(1)} %dynamic-slice_bitcast_fusion.idx_ref, bf16[256,1024]{1,0:T(8,128)(2,1)} %get-tuple-element.123.refs_0_, bf16[256,1024]{1,0:T(8,128)(2,1)} %get-tuple-element.124.refs_1_, ...), custom_call_target="tpu_custom_call" | custom-call | flops 1610612736 | bytes 5242880 | tf_op jit(solution)/shard_map/pallas_call | solution.py:321
  73.9 6.1 %conditional.3 = (bf16[512,512]{1,0:T(8,128)(2,1)S(1)}) conditional(s32[]{:T(128)} %bitcast.5, (s32[24,128]{1,0:T(8,128)S(1)}, bf16[512,512]{1,0:T(8,128)(2,1)}, bf16[512,128]{1,0:T(8,128)(2,1)S(1)}, bf16[512,128]{1,0:T(8,128)(2,1)S(1)}, bf16[16,13,32,128]{3,2,1,0:T(8,128)(2,1)}) %tuple.19, (bf16[4096,128]{1,0:T(8,128)(2,1)S(1)}, ...), branch_computations={%region_2.3_spmd, %region_3.4_spmd} | conditional | flops 1207959552 | bytes 15728676 | solution.py:599
  74.0 6.1 %branch_0_fun.3 = bf16[512,512]{1,0:T(8,128)(2,1)S(1)} custom-call(s32[24,128]{1,0:T(8,128)S(1)} %get-tuple-element.86.slot_ref, bf16[512,512]{1,0:T(8,128)(2,1)} %get-tuple-element.87.q_ref, bf16[512,128]{1,0:T(8,128)(2,1)S(1)} %get-tuple-element.88.k_ref, bf16[512,128]{1,0:T(8,128)(2,1)S(1)} %get-tuple-element.89.v_ref, ...), custom_call_target="tpu_custom_call" | custom-call | flops 1207959552 | bytes 4456448 | tf_op jit(solution)/shard_map/cond/branch_0_fun/pallas_call | solution.py:397
  80.1 0.5 collective-permute-start.9
  80.6 1.5 %collective-permute-done.9.b_ref.sib_ref = bf16[512,512]{1,0:T(8,128)(2,1)S(1)} collective-permute-done((bf16[512,512]{1,0:T(8,128)(2,1)S(1)}, bf16[512,512]{1,0:T(8,128)(2,1)S(1)}, u32[]{:S(2)}, u32[]{:S(2)}) %collective-permute-start.9) | collective-permute-done | bytes 524320 | tf_op jit(solution)/shard_map/ppermute | solution.py:34
  82.1 0.8 copy-done
  82.9 4.4 %shard_map.105 = (bf16[256,1024]{1,0:T(8,128)(2,1)S(1)}, bf16[256,1024]{1,0:T(8,128)(2,1)}) custom-call(s32[12]{0:T(128)S(1)} %dynamic-slice_bitcast_fusion.idx_ref, bf16[512,512]{1,0:T(8,128)(2,1)S(1)} %get-tuple-element.141.a_ref.own_ref, bf16[512,512]{1,0:T(8,128)(2,1)} %copy-done, bf16[512,8192]{1,0:T(8,128)(2,1)} %wa_ref.1, ...), custom_call_target="tpu_custom_call" | custom-call | flops 1073741824 | bytes 4194304 | tf_op jit(solution)/shard_map/pallas_call | solution.py:434
  87.4 2.7 %collective-permute-start.15 = (bf16[256,1024]{1,0:T(8,128)(2,1)}, bf16[256,1024]{1,0:T(8,128)(2,1)S(1)}, u32[]{:S(2)}, u32[]{:S(2)}) collective-permute-start(bf16[256,1024]{1,0:T(8,128)(2,1)} %get-tuple-element.137), channel_id=1, source_target_pairs={{0,6},{1,7},{2,0},{3,1},{4,2},{5,3},{6,4},{7,5},{8,14},{9,15},{10,... | collective-permute-start | bytes 1572872 | tf_op jit(solution)/shard_map/ppermute | solution.py:34
  90.0 6.1 %shard_map.106 = (f32[256,1024]{1,0:T(8,128)}, bf16[256,1024]{1,0:T(8,128)(2,1)S(1)}, bf16[256,1024]{1,0:T(8,128)(2,1)}, f32[256,1024]{1,0:T(8,128)}) custom-call(s32[12]{0:T(128)S(1)} %dynamic-slice_bitcast_fusion.idx_ref, bf16[512,512]{1,0:T(8,128)(2,1)} %copy-done.10, bf16[512,512]{1,0:T(8,128)(2,1)} %copy-done, bf16[512,8192]{1,0:T(8,128)(2,1)} %wa_ref.1, ...), custom_call_target="tpu_custom_call" | custom-call | flops 2147483648 | bytes 8388608 | tf_op jit(solution)/shard_map/pallas_call | solution.py:434
  96.1 0.3 collective-permute-start.11
  96.5 1.2 collective-permute-start.12
  97.7 4.0 %collective-permute-done.13 = bf16[256,1024]{1,0:T(8,128)(2,1)S(1)} collective-permute-done((bf16[256,1024]{1,0:T(8,128)(2,1)S(1)}, bf16[256,1024]{1,0:T(8,128)(2,1)S(1)}, u32[]{:S(2)}, u32[]{:S(2)}) %collective-permute-start.13) | collective-permute-done | bytes 524320 | tf_op jit(solution)/shard_map/ppermute | solution.py:34
  101.7 1.5 %add_convert_fusion.1 = bf16[256,1024]{1,0:T(8,128)(2,1)S(1)} fusion(f32[256,1024]{1,0:T(8,128)} %get-tuple-element.134, bf16[256,1024]{1,0:T(8,128)(2,1)S(1)} %collective-permute-done.13), kind=kLoop, calls=%fused_computation.1 | loop fusion | flops 786432 | bytes 2097152 | tf_op jit(solution)/shard_map/convert_element_type | solution.py:495
  103.3 0.1 add_convert_fusion
  103.4 2.7 %collective-permute-start.16 = (bf16[256,1024]{1,0:T(8,128)(2,1)S(1)}, bf16[256,1024]{1,0:T(8,128)(2,1)S(1)}, u32[]{:S(2)}, u32[]{:S(2)}) collective-permute-start(bf16[256,1024]{1,0:T(8,128)(2,1)S(1)} %add_convert_fusion), channel_id=1, source_target_pairs={{0,6},{1,7},{2,0},{3,1},{4,2},{5,3},{6,4},{7,5},{8,14},{9,15},{10,... | collective-permute-start | bytes 1572872 | tf_op jit(solution)/shard_map/ppermute | solution.py:34
  106.1 6.1 %collective-permute-done.11.up_ref = bf16[256,1024]{1,0:T(8,128)(2,1)S(1)} collective-permute-done((bf16[256,1024]{1,0:T(8,128)(2,1)}, bf16[256,1024]{1,0:T(8,128)(2,1)S(1)}, u32[]{:S(2)}, u32[]{:S(2)}) %collective-permute-start.11) | collective-permute-done | bytes 524320 | tf_op jit(solution)/shard_map/ppermute | solution.py:34
  112.2 0.7 collective-permute-done.12.low_ref
  113.0 2.6 %shard_map.107 = (f32[256,1024]{1,0:T(8,128)S(1)}, f32[256,1024]{1,0:T(8,128)S(1)}) custom-call(bf16[512,512]{1,0:T(8,128)(2,1)S(1)} %copy-done.11, bf16[512,512]{1,0:T(8,128)(2,1)S(1)} %copy-done.1, bf16[512,8192]{1,0:T(8,128)(2,1)S(1)} %bitcast.12, bf16[512,8192]{1,0:T(8,128)(2,1)} %collective-permute-done.10.refs_1_.refs_2_.refs_3_.wb_ref, ...), custom_call_target="tpu_custom_call" | custom-call | flops 1073741824 | bytes 4194304 | tf_op jit(solution)/shard_map/pallas_call | solution.py:478
  115.6 8.6 %collective-permute-done.14.low_top = bf16[256,1024]{1,0:T(8,128)(2,1)S(1)} collective-permute-done((bf16[256,1024]{1,0:T(8,128)(2,1)S(1)}, bf16[256,1024]{1,0:T(8,128)(2,1)S(1)}, u32[]{:S(2)}, u32[]{:S(2)}) %collective-permute-start.14) | collective-permute-done | bytes 524320 | tf_op jit(solution)/shard_map/ppermute | solution.py:34
  124.2 1.0 shard_map.108
  (42 shorter events, 0.2 us)
Async XLA Ops:
  0.0 82.1 %collective-permute-start.10 = (bf16[512,8192]{1,0:T(8,128)(2,1)}, bf16[512,8192]{1,0:T(8,128)(2,1)}, u32[]{:S(2)}, u32[]{:S(2)}) collective-permute-start(bf16[512,8192]{1,0:T(8,128)(2,1)} %wa_ref.1), channel_id=1, source_target_pairs={{0,1},{1,0},{2,3},{3,2},{4,5},{5,4},{6,7},{7,6},{8,9},{9,8},{10,11... | collective-permute-start | bytes 25165832 | tf_op jit(solution)/shard_map/ppermute | solution.py:34
  1.4 25.7 %collective-permute-start.2 = (bf16[512,1024]{1,0:T(8,128)(2,1)}, bf16[512,1024]{1,0:T(8,128)(2,1)S(1)}, u32[]{:S(2)}, u32[]{:S(2)}) collective-permute-start(bf16[512,1024]{1,0:T(8,128)(2,1)} %refs_0_.3), channel_id=1, source_target_pairs={{0,6},{1,7},{2,0},{3,1},{4,2},{5,3},{6,4},{7,5},{8,14},{9,15},{10,... | collective-permute-start | bytes 3145736 | tf_op jit(solution)/shard_map/ppermute | solution.py:34
  4.2 26.0 %collective-permute-start = (bf16[512,1024]{1,0:T(8,128)(2,1)}, bf16[512,1024]{1,0:T(8,128)(2,1)S(1)}, u32[]{:S(2)}, u32[]{:S(2)}) collective-permute-start(bf16[512,1024]{1,0:T(8,128)(2,1)} %refs_0_.3), channel_id=1, source_target_pairs={{0,2},{1,3},{2,4},{3,5},{4,6},{5,7},{6,0},{7,1},{8,10},{9,11},{10,... | collective-permute-start | bytes 3145736 | tf_op jit(solution)/shard_map/ppermute | solution.py:34
  5.1 0.7 copy-start.4
  11.4 7.8 %copy-start.2 = (bf16[512,1024]{1,0:T(8,128)(2,1)S(1)}, bf16[512,1024]{1,0:T(8,128)(2,1)}, u32[]{:S(2)}) copy-start(bf16[512,1024]{1,0:T(8,128)(2,1)} %refs_0_.3) | copy-start | bytes 3145732
  11.4 26.2 %all-to-all-start.3 = ((bf16[16,9,32,128]{3,2,1,0:T(8,128)(2,1)}), bf16[16,9,32,128]{3,2,1,0:T(8,128)(2,1)}, u32[]{:S(2)}, u32[]{:S(2)}) async-start(bf16[16,9,32,128]{3,2,1,0:T(8,128)(2,1)} %shard_map.104), calls=%async_computation.3 | async-start | bytes 2359296 | tf_op jit(solution)/shard_map/all_to_all | solution.py:267
  19.2 29.6 %collective-permute-start.4 = (bf16[512,1024]{1,0:T(8,128)(2,1)S(1)}, bf16[512,1024]{1,0:T(8,128)(2,1)}, u32[]{:S(2)}, u32[]{:S(2)}) collective-permute-start(bf16[512,1024]{1,0:T(8,128)(2,1)S(1)} %copy-done.2), channel_id=1, source_target_pairs={{0,1},{1,0},{2,3},{3,2},{4,5},{5,4},{6,7},{7,6},{8,9},{9,8},{10,11... | collective-permute-start | bytes 3145736 | tf_op jit(solution)/shard_map/ppermute | solution.py:34
  27.1 21.6 %collective-permute-start.6 = (bf16[512,1024]{1,0:T(8,128)(2,1)S(1)}, bf16[512,1024]{1,0:T(8,128)(2,1)}, u32[]{:S(2)}, u32[]{:S(2)}) collective-permute-start(bf16[512,1024]{1,0:T(8,128)(2,1)S(1)} %collective-permute-done.2.refs_4_), channel_id=1, source_target_pairs={{0,1},{1,0},{2,3},{3,2},{4,5},{5,4},{6,7},{7,6},{8,9},{9,8},{10,11... | collective-permute-start | bytes 3145736 | tf_op jit(solution)/shard_map/ppermute | solution.py:34
  30.2 18.5 %collective-permute-start.5 = (bf16[512,1024]{1,0:T(8,128)(2,1)S(1)}, bf16[512,1024]{1,0:T(8,128)(2,1)}, u32[]{:S(2)}, u32[]{:S(2)}) collective-permute-start(bf16[512,1024]{1,0:T(8,128)(2,1)S(1)} %collective-permute-done.refs_2_), channel_id=1, source_target_pairs={{0,1},{1,0},{2,3},{3,2},{4,5},{5,4},{6,7},{7,6},{8,9},{9,8},{10,11... | collective-permute-start | bytes 3145736 | tf_op jit(solution)/shard_map/ppermute | solution.py:34
  41.8 32.1 %all-to-all-start.4 = ((bf16[16,13,32,128]{3,2,1,0:T(8,128)(2,1)}), bf16[16,13,32,128]{3,2,1,0:T(8,128)(2,1)}, u32[]{:S(2)}, u32[]{:S(2)}) async-start(bf16[16,13,32,128]{3,2,1,0:T(8,128)(2,1)} %get-tuple-element.140), calls=%async_computation.4 | async-start | bytes 3407872 | tf_op jit(solution)/shard_map/all_to_all | solution.py:267
  46.7 13.1 %collective-permute-start.3 = (bf16[256,1024]{1,0:T(8,128)(2,1)}, bf16[256,1024]{1,0:T(8,128)(2,1)}, u32[]{:S(2)}, u32[]{:S(2)}) collective-permute-start(bf16[256,1024]{1,0:T(8,128)(2,1)} %slice.17), channel_id=1, source_target_pairs={{0,6},{1,7},{2,0},{3,1},{4,2},{5,3},{6,4},{7,5},{8,14},{9,15},{10,... | collective-permute-start | bytes 1572872 | tf_op jit(solution)/shard_map/ppermute | solution.py:34
  48.8 12.6 %collective-permute-start.1 = (bf16[256,1024]{1,0:T(8,128)(2,1)}, bf16[256,1024]{1,0:T(8,128)(2,1)}, u32[]{:S(2)}, u32[]{:S(2)}) collective-permute-start(bf16[256,1024]{1,0:T(8,128)(2,1)} %slice.16), channel_id=1, source_target_pairs={{0,2},{1,3},{2,4},{3,5},{4,6},{5,7},{6,0},{7,1},{8,10},{9,11},{10,... | collective-permute-start | bytes 1572872 | tf_op jit(solution)/shard_map/ppermute | solution.py:34
  61.4 5.7 %collective-permute-start.7 = (bf16[256,1024]{1,0:T(8,128)(2,1)}, bf16[256,1024]{1,0:T(8,128)(2,1)S(1)}, u32[]{:S(2)}, u32[]{:S(2)}) collective-permute-start(bf16[256,1024]{1,0:T(8,128)(2,1)} %get-tuple-element.123.refs_0_), channel_id=1, source_target_pairs={{0,1},{1,0},{2,3},{3,2},{4,5},{5,4},{6,7},{7,6},{8,9},{9,8},{10,11... | collective-permute-start | bytes 1572872 | tf_op jit(solution)/shard_map/ppermute | solution.py:34
  64.6 2.6 %collective-permute-start.8 = (bf16[256,1024]{1,0:T(8,128)(2,1)}, bf16[256,1024]{1,0:T(8,128)(2,1)}, u32[]{:S(2)}, u32[]{:S(2)}) collective-permute-start(bf16[256,1024]{1,0:T(8,128)(2,1)} %get-tuple-element.124.refs_1_), channel_id=1, source_target_pairs={{0,1},{1,0},{2,3},{3,2},{4,5},{5,4},{6,7},{7,6},{8,9},{9,8},{10,11... | collective-permute-start | bytes 1572872 | tf_op jit(solution)/shard_map/ppermute | solution.py:34
  65.3 8.6 %copy-start.5 = (bf16[4096,128]{1,0:T(8,128)(2,1)S(1)}, bf16[4096,128]{1,0:T(8,128)(2,1)}, u32[]{:S(2)}) copy-start(bf16[4096,128]{1,0:T(8,128)(2,1)} %param.19) | copy-start | bytes 3145732
  65.3 8.6 %copy-start.6 = (bf16[4096,128]{1,0:T(8,128)(2,1)S(1)}, bf16[4096,128]{1,0:T(8,128)(2,1)}, u32[]{:S(2)}) copy-start(bf16[4096,128]{1,0:T(8,128)(2,1)} %param.20) | copy-start | bytes 3145732
  65.3 8.6 %copy-start.7 = (bf16[256,1024]{1,0:T(8,128)(2,1)S(1)}, bf16[256,1024]{1,0:T(8,128)(2,1)}, u32[]{:S(2)}) copy-start(bf16[256,1024]{1,0:T(8,128)(2,1)} %slice.17) | copy-start | bytes 1572868
  65.3 8.6 %copy-start.9 = (bf16[256,1024]{1,0:T(8,128)(2,1)S(1)}, bf16[256,1024]{1,0:T(8,128)(2,1)}, u32[]{:S(2)}) copy-start(bf16[256,1024]{1,0:T(8,128)(2,1)} %slice.16) | copy-start | bytes 1572868
  67.1 0.8 copy-start.13
  80.1 7.2 %copy-start.10 = (bf16[512,512]{1,0:T(8,128)(2,1)}, bf16[512,512]{1,0:T(8,128)(2,1)S(1)}, u32[]{:S(2)}) copy-start(bf16[512,512]{1,0:T(8,128)(2,1)S(1)} %get-tuple-element.141.a_ref.own_ref) | copy-start | bytes 1572868
  80.1 2.0 %collective-permute-start.9 = (bf16[512,512]{1,0:T(8,128)(2,1)S(1)}, bf16[512,512]{1,0:T(8,128)(2,1)S(1)}, u32[]{:S(2)}, u32[]{:S(2)}) collective-permute-start(bf16[512,512]{1,0:T(8,128)(2,1)S(1)} %get-tuple-element.141.a_ref.own_ref), channel_id=1, source_target_pairs={{0,1},{1,0},{2,3},{3,2},{4,5},{5,4},{6,7},{7,6},{8,9},{9,8},{10,11... | collective-permute-start | bytes 1572872 | tf_op jit(solution)/shard_map/ppermute | solution.py:34
  82.1 0.8 copy-start
  82.9 30.1 %slice-start = ((s8[8388608]{0:T(1024)(128)(4,1)}), s8[4194304]{0:T(1024)(128)(4,1)S(1)}, s32[]{:S(2)}) async-start(s8[8388608]{0:T(1024)(128)(4,1)} %bitcast.11), calls=%async_computation.5 | async-start | bytes 8388608
  87.3 2.7 %copy-start.3 = (bf16[256,1024]{1,0:T(8,128)(2,1)}, bf16[256,1024]{1,0:T(8,128)(2,1)S(1)}, u32[]{:S(2)}) copy-start(bf16[256,1024]{1,0:T(8,128)(2,1)S(1)} %get-tuple-element.130.refs_4_) | copy-start | bytes 1572868
  87.3 14.4 %collective-permute-start.13 = (bf16[256,1024]{1,0:T(8,128)(2,1)S(1)}, bf16[256,1024]{1,0:T(8,128)(2,1)S(1)}, u32[]{:S(2)}, u32[]{:S(2)}) collective-permute-start(bf16[256,1024]{1,0:T(8,128)(2,1)S(1)} %get-tuple-element.130.refs_4_), channel_id=1, source_target_pairs={{0,2},{1,3},{2,4},{3,5},{4,6},{5,7},{6,0},{7,1},{8,10},{9,11},{10,... | collective-permute-start | bytes 1572872 | tf_op jit(solution)/shard_map/ppermute | solution.py:34
  87.4 25.6 %slice-start.1 = ((s8[8388608]{0:T(1024)(128)(4,1)}), s8[4194304]{0:T(1024)(128)(4,1)S(1)}, s32[]{:S(2)}) async-start(s8[8388608]{0:T(1024)(128)(4,1)} %bitcast.11), calls=%async_computation.6 | async-start | bytes 8388608
  87.4 15.9 %collective-permute-start.15 = (bf16[256,1024]{1,0:T(8,128)(2,1)}, bf16[256,1024]{1,0:T(8,128)(2,1)S(1)}, u32[]{:S(2)}, u32[]{:S(2)}) collective-permute-start(bf16[256,1024]{1,0:T(8,128)(2,1)} %get-tuple-element.137), channel_id=1, source_target_pairs={{0,6},{1,7},{2,0},{3,1},{4,2},{5,3},{6,4},{7,5},{8,14},{9,15},{10,... | collective-permute-start | bytes 1572872 | tf_op jit(solution)/shard_map/ppermute | solution.py:34
  96.1 7.1 %copy-start.12 = (f32[256,1024]{1,0:T(8,128)S(1)}, f32[256,1024]{1,0:T(8,128)}, u32[]{:S(2)}) copy-start(f32[256,1024]{1,0:T(8,128)} %get-tuple-element.136) | copy-start | bytes 3145732
  96.1 16.1 %collective-permute-start.11 = (bf16[256,1024]{1,0:T(8,128)(2,1)}, bf16[256,1024]{1,0:T(8,128)(2,1)S(1)}, u32[]{:S(2)}, u32[]{:S(2)}) collective-permute-start(bf16[256,1024]{1,0:T(8,128)(2,1)} %get-tuple-element.131), channel_id=1, source_target_pairs={{0,6},{1,7},{2,0},{3,1},{4,2},{5,3},{6,4},{7,5},{8,14},{9,15},{10,... | collective-permute-start | bytes 1572872 | tf_op jit(solution)/shard_map/ppermute | solution.py:34
  96.5 16.5 %collective-permute-start.12 = (bf16[256,1024]{1,0:T(8,128)(2,1)S(1)}, bf16[256,1024]{1,0:T(8,128)(2,1)S(1)}, u32[]{:S(2)}, u32[]{:S(2)}) collective-permute-start(bf16[256,1024]{1,0:T(8,128)(2,1)S(1)} %get-tuple-element.132), channel_id=1, source_target_pairs={{0,2},{1,3},{2,4},{3,5},{4,6},{5,7},{6,0},{7,1},{8,10},{9,11},{10,... | collective-permute-start | bytes 1572872 | tf_op jit(solution)/shard_map/ppermute | solution.py:34
  101.7 11.2 %copy-start.1 = (bf16[512,512]{1,0:T(8,128)(2,1)S(1)}, bf16[512,512]{1,0:T(8,128)(2,1)}, u32[]{:S(2)}) copy-start(bf16[512,512]{1,0:T(8,128)(2,1)} %copy-done) | copy-start | bytes 1572868
  101.7 11.2 %copy-start.11 = (bf16[512,512]{1,0:T(8,128)(2,1)S(1)}, bf16[512,512]{1,0:T(8,128)(2,1)}, u32[]{:S(2)}) copy-start(bf16[512,512]{1,0:T(8,128)(2,1)} %copy-done.10) | copy-start | bytes 1572868
  103.2 21.0 %collective-permute-start.14 = (bf16[256,1024]{1,0:T(8,128)(2,1)S(1)}, bf16[256,1024]{1,0:T(8,128)(2,1)S(1)}, u32[]{:S(2)}, u32[]{:S(2)}) collective-permute-start(bf16[256,1024]{1,0:T(8,128)(2,1)S(1)} %add_convert_fusion.1), channel_id=1, source_target_pairs={{0,2},{1,3},{2,4},{3,5},{4,6},{5,7},{6,0},{7,1},{8,10},{9,11},{10,... | collective-permute-start | bytes 1572872 | tf_op jit(solution)/shard_map/ppermute | solution.py:34
  103.4 20.8 %collective-permute-start.16 = (bf16[256,1024]{1,0:T(8,128)(2,1)S(1)}, bf16[256,1024]{1,0:T(8,128)(2,1)S(1)}, u32[]{:S(2)}, u32[]{:S(2)}) collective-permute-start(bf16[256,1024]{1,0:T(8,128)(2,1)S(1)} %add_convert_fusion), channel_id=1, source_target_pairs={{0,6},{1,7},{2,0},{3,1},{4,2},{5,3},{6,4},{7,5},{8,14},{9,15},{10,... | collective-permute-start | bytes 1572872 | tf_op jit(solution)/shard_map/ppermute | solution.py:34
